TPU v7x, 32 devices: a whole 2x2x4 slice. The times are simulated.
32 devices in a mesh: parts: 2 (over x), gx: 4 (over y, core), gy: 4 (over z).
Axes of the slice: x: 2, y: 2, z: 4, core: 2. Of those that a mesh axis runs over, the one named last changes fastest.
Arguments:
- forcing_right_side: float32 [32, 32, 1024], P(('parts', 'gx'), 'gy'), parts along dimension 0, may hold values from -18 to 18
- earlier_warmth: float32 [32, 32, 1024], P(('parts', 'gx'), 'gy'), parts along dimension 0, may hold values from 0 to 2
- matter_condition: int32 [32, 32, 1024], P(('parts', 'gx'), 'gy'), parts along dimension 0, may hold values from 0 to 2
- compressed_slot_number: int32 [32, 32, 1024], P(('parts', 'gx'), 'gy'), parts along dimension 0, may hold values from 0 to 127
- normal_draw_factor: float32 [32, 32, 1024], P(('parts', 'gx'), 'gy'), parts along dimension 0, may hold values from -6 to 6
Outputs:
- solution: float32 [32, 32, 1024], P(('parts', 'gx'), 'gy'), parts along dimension 0
- residual: float32 [32, 32, 1024], P(('parts', 'gx'), 'gy'), parts along dimension 0
There are 2 independent parts, one for each index of `parts`. A program takes and returns all parts, laid end to end along the dimension named above; each array names one. Nothing has to cross between parts.
Inputs may be any that keep to these rules, and one draw needn't show every extreme that they name: `matter_condition`: phase labels the cell as powder, solid or liquid. `compressed_slot_number`: each cell's row of the sketch.
All inputs are finite; a program needn't handle non-finite values.
Results may differ from a plain program's by a relative error of at most 0.0003.
Values sent between devices are 32-bit elements; how exact they have to be, the bound alone decides.
No kernel may reach another device: no remote copies, remote signals or barrier semaphores. Data moves between devices by JAX's collectives and lax.ppermute only.
A program may use at most 64 MiB of HBM per device.

v0:
```python
import jax
import jax.numpy as jnp
from jax import lax
from jax.experimental import pallas as pl
from jax.experimental.pallas import tpu as pltpu
from jax.sharding import PartitionSpec as P

SKETCH = 128
LOW = 32
HIGH = SKETCH // LOW
FIELDS = 3
PAIR = 2
LANES = 128
epsilon = 1e-06


def traits(warmth, phase):
    powder, solid = phase == 0, phase == 1
    offset = jnp.where(powder, 0.2, jnp.where(solid, 1.0, 0.6))
    return offset * (0.5 + warmth), jnp.where(powder, 1.0, jnp.where(solid, 2.0, 1.5))


def link(first, second):
    total = first + second
    return 2.0 * first * second / jnp.where(total > 0.0, total, 1.0)


def ahead(plane, axis):
    return pltpu.roll(plane, plane.shape[axis] - 1, axis)


def inner_links(cond):
    links = []
    for axis in (0, 1):
        index = lax.broadcasted_iota(jnp.int32, cond.shape, axis)
        links.append(
            jnp.where(index < cond.shape[axis] - 1, link(cond, ahead(cond, axis)), 0.0)
        )
    return links


def inner_flow(field, links):
    total = None
    for axis in (0, 1):
        flow = links[axis] * (field - ahead(field, axis))
        part = flow - pltpu.roll(flow, 1, axis)
        total = part if total is None else total + part
    return total


def apply_inside(images, x_links, links, caps):
    results = []
    flow_low = x_links[0] * (images[0] - images[1])
    for i in range(1, len(images) - 1):
        image = images[i]
        flow = x_links[i] * (image - images[i + 1])
        inside = inner_flow(image, links[i - 1])
        results.append(caps[i - 1] * image + inside + (flow - flow_low))
        flow_low = flow
    return results


def parts_of(slot):
    high = jnp.floor(slot * (1.0 / LOW))
    return slot - LOW * high, high


def one_hot(values, j, count, each):
    shape = (count * each, values.shape[1])
    index = lax.broadcasted_iota(jnp.int32, shape, 0) // each
    index = index.astype(jnp.float32).astype(jnp.bfloat16)
    row = jnp.broadcast_to(values[j : j + 1], shape).astype(jnp.bfloat16)
    one = jnp.ones_like(row)
    return jnp.where(row == index, one, jnp.zeros_like(one))


def put_cells(fields, draw, start, cells_ref):
    coarse, fine = [], []
    for field in fields:
        weighted = draw * field
        head = weighted.astype(jnp.bfloat16).astype(jnp.float32)
        coarse.append(head)
        fine.append(weighted - head)
    for f, part in enumerate((coarse + fine) * 2):
        for t in range(cells_ref.shape[0]):
            cells_ref[t, pl.ds(start + f, draw.shape[0], stride=8), :] = part[
                :, t * LANES : (t + 1) * LANES
            ]


def masked_cells(mask, start, j, cells_ref):
    at = pl.ds(start + j * 8, 8)
    cells = jnp.concatenate([cells_ref[t, at, :] for t in range(cells_ref.shape[0])], axis=1)
    return jnp.concatenate([cells, cells], axis=0).astype(jnp.bfloat16) * mask


def product(left, right):
    return lax.dot_general(
        jnp.concatenate(left, axis=1),
        jnp.concatenate(right, axis=1),
        (((1,), (1,)), ((), ())),
        preferred_element_type=jnp.float32,
    )


def as_sketch(total):
    each = 2 * PAIR
    total = jnp.concatenate([total[h * each : (h + 1) * each] for h in range(HIGH)], axis=1)
    return total[:PAIR] + total[PAIR:]


def sketch_rows(planes, low_ref, high_ref, cells_ref):
    total = 0.0
    each = HIGH * 2 * PAIR
    for i, (fields, draw, chosen) in enumerate(planes):
        rows = draw.shape[0]
        start = i * rows * 8
        put_cells(fields, draw, start, cells_ref)
        left, right = [], []
        for j in chosen:
            at = i * rows + j
            mask = high_ref[at * each : (at + 1) * each]
            left.append(masked_cells(mask, start, j, cells_ref))
            right.append(low_ref[at * LOW : (at + 1) * LOW])
        total = total + product(left, right)
    return total


def slot_kernel(b_ref, draw_ref, slot_ref, low_ref, high_ref, sketch_ref, cells_ref):
    planes, rows = b_ref.shape[:2]
    each = HIGH * 2 * PAIR
    total = 0.0
    for i in range(planes):
        start = i * rows * 8
        put_cells((b_ref[i],) * PAIR, draw_ref[i], start, cells_ref)
        low, high = parts_of(slot_ref[i])
        left, right = [], []
        for j in range(rows):
            at = i * rows + j
            mask, hot = one_hot(high, j, HIGH, 2 * PAIR), one_hot(low, j, LOW, 1)
            high_ref[at * each : (at + 1) * each] = mask
            low_ref[at * LOW : (at + 1) * LOW] = hot
            left.append(masked_cells(mask, start, j, cells_ref))
            right.append(hot)
        total = total + product(left, right)
    sketch_ref[...] = as_sketch(total)


def first_kernel(
    b_hbm, warmth_hbm, phase_hbm, draw_hbm, slot_hbm, b_ref, cond_ref, cap_ref, y_link_ref,
    z_link_ref, inner_ref, draw_ref, slot_ref, x_first_ref, x_second_ref, y_first_ref,
    y_second_ref, warmth_ref, phase_ref, number_ref, arrived,
):
    copies = [
        pltpu.make_async_copy(source, target, arrived.at[k])
        for k, (source, target) in enumerate(
            (
                (b_hbm, b_ref),
                (warmth_hbm, warmth_ref),
                (phase_hbm, phase_ref),
                (draw_hbm, draw_ref),
                (slot_hbm, number_ref),
            )
        )
    ]
    for copy in copies:
        copy.start()
    for copy in copies[:3]:
        copy.wait()
    planes, rows = b_ref.shape[:2]
    images, conds = [], []
    for i in range(planes):
        cond, cap = traits(warmth_ref[i], phase_ref[i])
        cap_ref[i] = cap
        cond_ref[i] = cond
        y_link_ref[i], z_link_ref[i] = links = inner_links(cond)
        field = b_ref[i]
        image = cap * field + inner_flow(field, links)
        if i:
            flow = link(conds[-1], cond) * (b_ref[i - 1] - field)
            images[-1] = images[-1] + flow
            image = image - flow
        conds.append(cond)
        images.append(image)
    for i in range(planes):
        inner_ref[i] = images[i]
    for k, field in enumerate((images, [b_ref[i] for i in range(planes)], conds)):
        at = slice(k * rows, (k + 1) * rows)
        x_first_ref[at], x_second_ref[at] = by_turn(field[0], field[-1], "gx")
        for i, plane in enumerate(field):
            at = slice(k * planes + i, k * planes + i + 1)
            y_first_ref[at], y_second_ref[at] = by_turn(plane[:1], plane[rows - 1 :], "gy")
    for copy in copies[3:]:
        copy.wait()
    for i in range(planes):
        slot_ref[i] = number_ref[i].astype(jnp.float32)
    for k, ref in enumerate((draw_ref, slot_ref)):
        ends = [ref[0], ref[planes - 1]]
        for e, j in enumerate((0, rows - 1)):
            at = slice(3 * rows + 2 * k + e, 3 * rows + 2 * k + e + 1)
            lines = [plane[j : j + 1] for plane in ends]
            x_first_ref[at], x_second_ref[at] = by_turn(*lines, "gx")
        for e, plane in enumerate(ends):
            at = slice(3 * planes + 2 * k + e, 3 * planes + 2 * k + e + 1)
            lines = [plane[:1], plane[rows - 1 :]]
            y_first_ref[at], y_second_ref[at] = by_turn(*lines, "gy")


def by_turn(one, other, axis):
    odd = lax.axis_index(axis) % 2 == 1
    return jnp.where(odd, one, other), jnp.where(odd, other, one)


def has_beside(axis):
    at = lax.axis_index(axis)
    return at > 0, at < lax.axis_size(axis) - 1


def reached(rows):
    others = [j for j in range(rows) if 2 <= j < rows - 2]
    return [j for j in range(rows) if j not in others], others


def inside_kernel(
    b_ref, cond_ref, cap_ref, y_link_ref, z_link_ref, inner_ref, draw_ref, low_ref, high_ref,
    got_second_ref, got_first_ref, wide_ref, x_link_ref, beside_ref, sketch_ref, cells_ref,
):
    planes, rows = b_ref.shape[:2]
    (image_low, image_high), (b_low, b_high), (c_low, c_high) = (
        by_turn(*(ref[k * rows : (k + 1) * rows] for ref in (got_first_ref, got_second_ref)), "gx")
        for k in range(3)
    )
    below, above = has_beside("gx")
    c_low, c_high = jnp.where(below, c_low, 0.0), jnp.where(above, c_high, 0.0)
    for k, plane in enumerate((b_low, b_high, c_low, c_high)):
        beside_ref[k] = plane
    conds = [c_low] + [cond_ref[i] for i in range(planes)] + [c_high]
    x_links = [link(conds[i], conds[i + 1]) for i in range(planes + 1)]
    for i, conductance in enumerate(x_links):
        x_link_ref[i] = conductance
    low_flow = x_links[0] * (b_low - b_ref[0])
    high_flow = x_links[-1] * (b_ref[planes - 1] - b_high)
    images = [image_low + low_flow] + [inner_ref[i] for i in range(planes)]
    images.append(image_high - high_flow)
    images[1] = images[1] - low_flow
    images[-2] = images[-2] + high_flow
    for i, image in enumerate(images):
        wide_ref[i] = image
    links = [(y_link_ref[i], z_link_ref[i]) for i in range(planes)]
    twice = apply_inside(images, x_links, links, [cap_ref[i] for i in range(planes)])
    chosen = reached(rows)[1]
    cells = [((images[i + 1], twice[i]), draw_ref[i], chosen) for i in range(planes)]
    sketch_ref[...] = sketch_rows(cells, low_ref, high_ref, cells_ref)


def third_kernel(
    b_ref, cap_ref, y_link_ref, z_link_ref, draw_ref, low_ref, high_ref, own_second_ref,
    own_first_ref, wide_ref, x_link_ref, beside_ref, x_second_ref, x_first_ref, y_second_ref,
    y_first_ref, b_sketch_ref, inside_ref, image_ref, twice_ref, sketch_ref, corner_first_ref,
    corner_second_ref, ends_ref, cells_ref, extra_ref,
):
    planes, rows, depth = b_ref.shape
    index = lax.broadcasted_iota(jnp.int32, (rows, depth), 0)
    images = [wide_ref[i] for i in range(planes + 2)]
    x_links = [x_link_ref[i] for i in range(planes + 1)]
    b_beside, c_beside = (beside_ref[0], beside_ref[1]), (beside_ref[2], beside_ref[3])
    x_ends = []
    for end, i in enumerate((0, planes - 1)):
        conductance = x_links[-end]
        x_ends.append((i, conductance, conductance * (b_ref[i] - b_beside[end])))
    x_tails = by_turn(x_first_ref[3 * rows :], x_second_ref[3 * rows :], "gx")
    own_lines = by_turn(own_first_ref[...], own_second_ref[...], "gy")
    y_lines = by_turn(y_first_ref[...], y_second_ref[...], "gy")
    beside = []
    for side, (j, here, own, line) in enumerate(
        zip((0, rows - 1), has_beside("gy"), own_lines, y_lines)
    ):
        row = slice(j, j + 1)
        beyond, b_line, c_line = (line[k * planes : (k + 1) * planes] for k in range(3))
        c_line = jnp.where(here, c_line, 0.0)
        y_link = link(own[2 * planes : 3 * planes], c_line)
        y_flow = y_link * (own[planes : 2 * planes] - b_line)
        beyond = beyond - y_flow
        for i in range(planes):
            at = slice(i, i + 1)
            images[i + 1] = images[i + 1] + jnp.where(index == j, y_flow[at], 0.0)
            beside.append((i, jnp.where(index == j, y_link[at], 0.0), beyond[at]))
        for end, (i, x_link, x_flow) in enumerate(x_ends):
            line_at, at = slice(i, i + 1), 4 * side + 2 * end
            tail = x_tails[end]
            values = -x_link[row] * y_flow[line_at], tail[side:][:1], tail[2 + side :][:1]
            for k, value in enumerate(values):
                extra_ref[k, at : at + 1] = value
            tail = line[3 * planes :]
            values = -y_link[line_at] * x_flow[row], tail[end:][:1], tail[2 + end :][:1]
            for k, value in enumerate(values):
                extra_ref[k, at + 1 : at + 2] = value
            at = 6 * (2 * side + end)
            values = x_link[row], b_beside[end][row], c_beside[end][row]
            values += y_link[line_at], b_line[line_at], c_line[line_at]
            for k, value in enumerate(values):
                ends_ref[at + k : at + k + 1] = value
    links = [(y_link_ref[i], z_link_ref[i]) for i in range(planes)]
    twice = apply_inside(images, x_links, links, [cap_ref[i] for i in range(planes)])
    for i, conductance, value in beside:
        twice[i] = twice[i] + conductance * (images[i + 1] - value)
    for i in range(planes):
        image_ref[i] = images[i + 1]
        twice_ref[i] = twice[i]
    chosen = reached(rows)[0]
    cells = [((images[i + 1], twice[i]), draw_ref[i], chosen) for i in range(planes)]
    total = inside_ref[...] + sketch_rows(cells, low_ref, high_ref, cells_ref)
    start = planes * rows * 8
    put_cells((jnp.zeros((8, depth), jnp.float32), extra_ref[0]), extra_ref[1], start, cells_ref)
    low, high = parts_of(extra_ref[2])
    left, right = [], []
    for j in range(8):
        mask = one_hot(high, j, HIGH, 2 * PAIR)
        left.append(masked_cells(mask, start, j, cells_ref))
        right.append(one_hot(low, j, LOW, 1))
    sketch_ref[1 : 1 + PAIR] = as_sketch(total + product(left, right))
    sketch_ref[:1] = b_sketch_ref[:1]
    sketch_ref[1 + PAIR :] = b_sketch_ref[:1]
    for k, plane in enumerate(b_beside + c_beside):
        at = slice(k, k + 1)
        corner_first_ref[at], corner_second_ref[at] = by_turn(
            plane[:1], plane[rows - 1 :], "gy"
        )


def last_kernel(
    sketch_ref, b_ref, image_ref, twice_ref, ends_ref, corner_first_ref, corner_second_ref,
    solution_ref, residual_ref,
):
    sketches = jnp.sum(sketch_ref[...], axis=0)

    def inner(first, second):
        return jnp.sum(first * second, axis=1, keepdims=True)

    s0, s1, s2 = (sketches[i : i + 1] for i in range(FIELDS))
    beta_inverse = 1.0 / jnp.sqrt(inner(s0, s0) + epsilon)
    h00 = inner(s0, s1) * beta_inverse * beta_inverse
    q0, p0 = s0 * beta_inverse, s1 * beta_inverse
    t0 = p0 - h00 * q0
    p1 = s2 * beta_inverse - h00 * p0
    n0 = jnp.sqrt(inner(t0, t0) + epsilon)
    n0_inverse = 1.0 / n0
    h01 = inner(q0, p1) * n0_inverse
    h11 = inner(t0, p1) * n0_inverse * n0_inverse
    t1 = p1 * n0_inverse - h01 * q0 - h11 * (t0 * n0_inverse)
    n1_square = inner(t1, t1) + epsilon
    first = h00 * h00 + n0 * n0
    cross = h00 * h01 + n0 * h11
    ratio = cross / first
    second = h01 * h01 + h11 * h11 + n1_square - cross * ratio
    y1 = (h01 - ratio * h00) / second
    y0 = h00 / first - ratio * y1
    c1 = y1 * n0_inverse
    c0 = y0 - h00 * c1
    planes, rows, depth = b_ref.shape
    for i in range(planes):
        b, image = b_ref[i], image_ref[i]
        solution_ref[i] = c0 * b + c1 * image
        residual_ref[i] = b - c0 * image - c1 * twice_ref[i]
    corners = by_turn(corner_first_ref[...], corner_second_ref[...], "gy")
    for side, (j, here, corner) in enumerate(zip((0, rows - 1), has_beside("gy"), corners)):
        for end, i in enumerate((0, planes - 1)):
            b, cond = corner[end : end + 1], corner[2 + end : 3 + end]
            cond = jnp.where(here, cond, 0.0)
            at = 6 * (2 * side + end)
            x_link, x_b, x_cond, y_link, y_b, y_cond = (
                ends_ref[at + k : at + k + 1] for k in range(6)
            )
            lacked = x_link * link(x_cond, cond) * (x_b - b)
            lacked = lacked + y_link * link(y_cond, cond) * (y_b - b)
            residual_ref[i, j : j + 1] = residual_ref[i, j : j + 1] + c1 * lacked


def call(kernel, shapes, *operands, scratch=(), inputs=pltpu.VMEM, flops=0):
    return pl.pallas_call(
        kernel,
        out_shape=[
            shape if hasattr(shape, "dtype") else jax.ShapeDtypeStruct(shape, jnp.float32)
            for shape in shapes
        ],
        in_specs=[pl.BlockSpec(memory_space=inputs)] * len(operands),
        out_specs=[pl.BlockSpec(memory_space=pltpu.VMEM)] * len(shapes),
        scratch_shapes=scratch,
        compiler_params=pltpu.CompilerParams(vmem_limit_bytes=48 * 1024 * 1024),
        cost_estimate=pl.CostEstimate(flops=flops, bytes_accessed=0, transcendentals=0),
    )(*operands)


def swap(array, axis, turn):
    nx, ny = lax.axis_size("gx"), lax.axis_size("gy")
    pairs = []
    for x in range(nx):
        for y in range(ny):
            here, count = (x, nx) if axis == "gx" else (y, ny)
            there = here + 1 if here % 2 == turn else here - 1
            if 0 <= there < count:
                partner = (there, y) if axis == "gx" else (x, there)
            else:
                partner = (x, y ^ 1) if axis == "gx" else (x ^ 1, y)
            pairs.append((x * ny + y, partner[0] * ny + partner[1]))
    return lax.ppermute(array, ("gx", "gy"), pairs)


def everyones(sketch):
    count = lax.axis_size("gx") * lax.axis_size("gy")
    copies = jnp.broadcast_to(sketch[None], (count,) + sketch.shape)
    return lax.all_to_all(copies, ("gx", "gy"), 0, 0)


def body(b, warmth, phase, slots, draw):
    planes, rows, depth = b.shape
    block, wide = b.shape, (planes + 2, rows, depth)
    face, line, corner = (3 * rows + 4, depth), (3 * planes + 4, depth), (4, depth)
    cells = pltpu.VMEM((depth // LANES, (planes * rows + 8) * 8, LANES), jnp.float32)
    total = HIGH * 2 * PAIR, LOW
    hots = [
        jax.ShapeDtypeStruct((planes * rows * count, depth), jnp.bfloat16)
        for count in (LOW, HIGH * 2 * PAIR)
    ]
    work = b.size * SKETCH * 6
    b, cond, cap, y_link, z_link, inner, draw, slots, x_first, x_second, y_first, y_second = call(
        first_kernel,
        [block] * 8 + [face, face, line, line],
        *(
            pltpu.with_memory_space_constraint(x, pltpu.HBM)
            for x in (b, warmth, phase, draw, slots)
        ),
        scratch=[
            pltpu.VMEM(block, warmth.dtype),
            pltpu.VMEM(block, phase.dtype),
            pltpu.VMEM(block, slots.dtype),
            pltpu.SemaphoreType.DMA((5,)),
        ],
        inputs=pltpu.HBM,
    )
    got_x = swap(x_second, "gx", 1), swap(x_first, "gx", 0)
    got_y = swap(y_second, "gy", 1), swap(y_first, "gy", 0)
    *hots, b_sketch = call(
        slot_kernel, [*hots, (PAIR, SKETCH)], b, draw, slots, scratch=[cells], flops=work
    )
    image_wide, x_link, beside, inside = call(
        inside_kernel,
        [wide, (planes + 1, rows, depth), (4, rows, depth), total],
        b, cond, cap, y_link, z_link, inner, draw, *hots, *got_x,
        scratch=[cells],
        flops=work,
    )
    image, twice, sketch, first, second, ends = call(
        third_kernel,
        [block, block, (FIELDS + 1, SKETCH), corner, corner, (24, depth)],
        b, cap, y_link, z_link, draw, *hots, y_second, y_first, image_wide, x_link, beside,
        *got_x, *got_y, b_sketch, inside,
        scratch=[cells, pltpu.VMEM((3, 8, depth), jnp.float32)],
        flops=work,
    )
    got_corners = [swap(array, "gy", turn) for turn, array in enumerate((first, second))]
    sketches = everyones(sketch)
    return tuple(
        call(last_kernel, [block, block], sketches, b, image, twice, ends, *got_corners)
    )


def solution(mesh):
    spec = P(("parts", "gx"), "gy", None)
    return jax.shard_map(
        body, mesh=mesh, in_specs=(spec,) * 5, out_specs=(spec,) * 2, check_vma=False
    )
```

profile of v0, /device:TPU:0, one launch (start us, length us, event | category | flops | bytes accessed | tf_op | source)
XLA Modules:
  0.0 24.3 jit_solution(6045787768215734624)
XLA Ops:
  0.6 1.5 %shard_map.68 = (f32[4,8,1024]{2,1,0:T(8,128)S(1)}, f32[4,8,1024]{2,1,0:T(8,128)S(1)}, f32[4,8,1024]{2,1,0:T(8,128)S(1)}, f32[4,8,1024]{2,1,0:T(8,128)S(1)}, f32...) custom-call(f32[4,8,1024]{2,1,0:T(8,128)} %b_hbm.1, ...), custom_call_target="tpu_custom_call" | custom-call | tf_op jit(solution)/shard_map/pallas_call | solution.py:380
  2.1 3.1 %collective-permute-start = (f32[28,1024]{1,0:T(8,128)S(1)}, f32[28,1024]{1,0:T(8,128)S(1)}, u32[]{:S(2)}, u32[]{:S(2)}) collective-permute-start(f32[28,1024]{1,0:T(8,128)S(1)} %get-tuple-element.39), channel_id=1, source_target_pairs={{0,1},{1,0},{2,3},{3,2},{4,8},{5,9},{6,10},{7,11},{8,4},{9,5},{10,... | collective-permute-start | bytes 344072 | tf_op jit(solution)/shard_map/ppermute | solution.py:406
  5.2 0.1 collective-permute-start.1
  5.3 0.5 %collective-permute-start.2 = (f32[16,1024]{1,0:T(8,128)S(1)}, f32[16,1024]{1,0:T(8,128)S(1)}, u32[]{:S(2)}, u32[]{:S(2)}) collective-permute-start(f32[16,1024]{1,0:T(8,128)S(1)} %get-tuple-element.35.own_second_ref), channel_id=1, source_target_pairs={{0,4},{1,2},{2,1},{3,7},{4,0},{5,6},{6,5},{7,3},{8,12},{9,10},{10,... | collective-permute-start | bytes 196616 | tf_op jit(solution)/shard_map/ppermute | solution.py:406
  5.7 2.7 %collective-permute-start.3 = (f32[16,1024]{1,0:T(8,128)S(1)}, f32[16,1024]{1,0:T(8,128)S(1)}, u32[]{:S(2)}, u32[]{:S(2)}) collective-permute-start(f32[16,1024]{1,0:T(8,128)S(1)} %get-tuple-element.36.own_first_ref), channel_id=1, source_target_pairs={{0,1},{1,0},{2,3},{3,2},{4,5},{5,4},{6,7},{7,6},{8,9},{9,8},{10,11... | collective-permute-start | bytes 196616 | tf_op jit(solution)/shard_map/ppermute | solution.py:406
  8.4 0.9 %shard_map.69 = (bf16[1024,1024]{1,0:T(8,128)(2,1)S(1)}, bf16[512,1024]{1,0:T(8,128)(2,1)S(1)}, f32[2,128]{1,0:T(2,128)S(1)}) custom-call(f32[4,8,1024]{2,1,0:T(8,128)S(1)} %get-tuple-element.27.b_ref, f32[4,8,1024]{2,1,0:T(8,128)S(1)} %get-tuple-element.31.draw_ref, f32[4,8,1024]{2,1,0:T(8,128)S(1)} %get-tuple-element.32.slot_ref), custom_call_target="tpu_custom_call" | custom-call | flops 25165824 | tf_op jit(solution)/shard_map/pallas_call | solution.py:380
  9.3 0.0 collective-permute-done.got_second_ref.x_second_ref
  9.3 0.0 collective-permute-done.1.got_first_ref.x_first_ref
  9.3 0.6 %shard_map.70 = (f32[6,8,1024]{2,1,0:T(8,128)S(1)}, f32[5,8,1024]{2,1,0:T(8,128)S(1)}, f32[4,8,1024]{2,1,0:T(8,128)S(1)}, f32[16,32]{1,0:T(8,128)S(1)}) custom-call(f32[4,8,1024]{2,1,0:T(8,128)S(1)} %get-tuple-element.27.b_ref, f32[4,8,1024]{2,1,0:T(8,128)S(1)} %get-tuple-element.37.cond_ref, f32[4,8,1024]{2,1,0:T(8,128)S(1)} %get-tuple-element.28.cap_ref, ...), custom_call_target="tpu_custom_call" | custom-call | flops 25165824 | tf_op jit(solution)/shard_map/pallas_call | solution.py:380
  9.9 0.0 collective-permute-done.2.y_second_ref
  10.0 0.9 %collective-permute-done.3.y_first_ref = f32[16,1024]{1,0:T(8,128)S(1)} collective-permute-done((f32[16,1024]{1,0:T(8,128)S(1)}, f32[16,1024]{1,0:T(8,128)S(1)}, u32[]{:S(2)}, u32[]{:S(2)}) %collective-permute-start.3) | collective-permute-done | bytes 65568 | tf_op jit(solution)/shard_map/ppermute | solution.py:406
  10.8 1.0 %shard_map.71 = (f32[4,8,1024]{2,1,0:T(8,128)S(1)}, f32[4,8,1024]{2,1,0:T(8,128)S(1)}, f32[4,128]{1,0:T(4,128)S(1)}, f32[4,1024]{1,0:T(4,128)S(1)}, f32[4,1024]{1,0:T(4,128)S(1)}, /*index=5*/f32[24,1024]{1,0:T(8,128)S(1)}) custom-call(f32[4,8,1024]{2,1,0:T(8,128)S(1)} %get-tuple-element.27.b_ref, f32[4,8,1024]{2,1,0:T(8,128)S(1)} %get-tuple-element.28.cap_ref, ...), custom_call_target="tpu_custom_call" | custom-call | flops 25165824 | tf_op jit(solution)/shard_map/pallas_call | solution.py:380
  11.8 0.6 %broadcast_in_dim.2 = f32[16,4,128]{2,1,0:T(4,128)} broadcast(f32[4,128]{1,0:T(4,128)S(1)} %get-tuple-element.46), dimensions={1,2} | broadcast | bytes 34816 | tf_op jit(solution)/shard_map/broadcast_in_dim | solution.py:411
  12.5 4.1 %all-to-all-start = ((f32[16,4,128]{2,1,0:T(4,128)}), f32[16,4,128]{2,1,0:T(4,128)S(1)}, u32[]{:S(2)}, u32[]{:S(2)}) async-start(f32[16,4,128]{2,1,0:T(4,128)} %broadcast_in_dim.2), calls=%async_computation | async-start | bytes 65536 | tf_op jit(solution)/shard_map/all_to_all | solution.py:412
  16.6 1.9 %collective-permute-start.4 = (f32[4,1024]{1,0:T(4,128)S(1)}, f32[4,1024]{1,0:T(4,128)S(1)}, u32[]{:S(2)}, u32[]{:S(2)}) collective-permute-start(f32[4,1024]{1,0:T(4,128)S(1)} %get-tuple-element.50), channel_id=1, source_target_pairs={{0,1},{1,0},{2,3},{3,2},{4,5},{5,4},{6,7},{7,6},{8,9},{9,8},{10,11... | collective-permute-start | bytes 49160 | tf_op jit(solution)/shard_map/ppermute | solution.py:406
  18.6 0.0 collective-permute-start.5
  18.6 2.0 %collective-permute-done.4.corner_first_ref = f32[4,1024]{1,0:T(4,128)S(1)} collective-permute-done((f32[4,1024]{1,0:T(4,128)S(1)}, f32[4,1024]{1,0:T(4,128)S(1)}, u32[]{:S(2)}, u32[]{:S(2)}) %collective-permute-start.4) | collective-permute-done | bytes 16416 | tf_op jit(solution)/shard_map/ppermute | solution.py:406
  20.6 0.0 collective-permute-done.5.corner_second_ref
  20.6 2.6 %all-to-all-done.sketch_ref = f32[16,4,128]{2,1,0:T(4,128)S(1)} async-done(((f32[16,4,128]{2,1,0:T(4,128)}), f32[16,4,128]{2,1,0:T(4,128)S(1)}, u32[]{:S(2)}, u32[]{:S(2)}) %all-to-all-start) | async-done | bytes 32800 | tf_op jit(solution)/shard_map/all_to_all | solution.py:412
  23.1 1.1 %shard_map.72 = (f32[4,8,1024]{2,1,0:T(8,128)}, f32[4,8,1024]{2,1,0:T(8,128)}) custom-call(f32[16,4,128]{2,1,0:T(4,128)S(1)} %all-to-all-done.sketch_ref, f32[4,8,1024]{2,1,0:T(8,128)S(1)} %get-tuple-element.27.b_ref, f32[4,8,1024]{2,1,0:T(8,128)S(1)} %get-tuple-element.47.image_ref, f32[4,8,1024]{2,1,0:T(8,128)S(1)} %get-tuple-element.48.twice_ref, ...), custom_call_target="tpu_custom_call" | custom-call | tf_op jit(solution)/shard_map/pallas_call | solution.py:380
Async XLA Ops:
  2.1 7.2 %collective-permute-start = (f32[28,1024]{1,0:T(8,128)S(1)}, f32[28,1024]{1,0:T(8,128)S(1)}, u32[]{:S(2)}, u32[]{:S(2)}) collective-permute-start(f32[28,1024]{1,0:T(8,128)S(1)} %get-tuple-element.39), channel_id=1, source_target_pairs={{0,1},{1,0},{2,3},{3,2},{4,8},{5,9},{6,10},{7,11},{8,4},{9,5},{10,... | collective-permute-start | bytes 344072 | tf_op jit(solution)/shard_map/ppermute | solution.py:406
  5.2 4.1 %collective-permute-start.1 = (f32[28,1024]{1,0:T(8,128)S(1)}, f32[28,1024]{1,0:T(8,128)S(1)}, u32[]{:S(2)}, u32[]{:S(2)}) collective-permute-start(f32[28,1024]{1,0:T(8,128)S(1)} %get-tuple-element.40), channel_id=1, source_target_pairs={{0,4},{1,5},{2,6},{3,7},{4,0},{5,1},{6,2},{7,3},{8,12},{9,13},{10,... | collective-permute-start | bytes 344072 | tf_op jit(solution)/shard_map/ppermute | solution.py:406
  5.3 4.7 %collective-permute-start.2 = (f32[16,1024]{1,0:T(8,128)S(1)}, f32[16,1024]{1,0:T(8,128)S(1)}, u32[]{:S(2)}, u32[]{:S(2)}) collective-permute-start(f32[16,1024]{1,0:T(8,128)S(1)} %get-tuple-element.35.own_second_ref), channel_id=1, source_target_pairs={{0,4},{1,2},{2,1},{3,7},{4,0},{5,6},{6,5},{7,3},{8,12},{9,10},{10,... | collective-permute-start | bytes 196616 | tf_op jit(solution)/shard_map/ppermute | solution.py:406
  5.7 5.1 %collective-permute-start.3 = (f32[16,1024]{1,0:T(8,128)S(1)}, f32[16,1024]{1,0:T(8,128)S(1)}, u32[]{:S(2)}, u32[]{:S(2)}) collective-permute-start(f32[16,1024]{1,0:T(8,128)S(1)} %get-tuple-element.36.own_first_ref), channel_id=1, source_target_pairs={{0,1},{1,0},{2,3},{3,2},{4,5},{5,4},{6,7},{7,6},{8,9},{9,8},{10,11... | collective-permute-start | bytes 196616 | tf_op jit(solution)/shard_map/ppermute | solution.py:406
  12.5 10.6 %all-to-all-start = ((f32[16,4,128]{2,1,0:T(4,128)}), f32[16,4,128]{2,1,0:T(4,128)S(1)}, u32[]{:S(2)}, u32[]{:S(2)}) async-start(f32[16,4,128]{2,1,0:T(4,128)} %broadcast_in_dim.2), calls=%async_computation | async-start | bytes 65536 | tf_op jit(solution)/shard_map/all_to_all | solution.py:412
  16.6 3.9 %collective-permute-start.4 = (f32[4,1024]{1,0:T(4,128)S(1)}, f32[4,1024]{1,0:T(4,128)S(1)}, u32[]{:S(2)}, u32[]{:S(2)}) collective-permute-start(f32[4,1024]{1,0:T(4,128)S(1)} %get-tuple-element.50), channel_id=1, source_target_pairs={{0,1},{1,0},{2,3},{3,2},{4,5},{5,4},{6,7},{7,6},{8,9},{9,8},{10,11... | collective-permute-start | bytes 49160 | tf_op jit(solution)/shard_map/ppermute | solution.py:406
  18.6 2.0 %collective-permute-start.5 = (f32[4,1024]{1,0:T(4,128)S(1)}, f32[4,1024]{1,0:T(4,128)S(1)}, u32[]{:S(2)}, u32[]{:S(2)}) collective-permute-start(f32[4,1024]{1,0:T(4,128)S(1)} %get-tuple-element.51), channel_id=1, source_target_pairs={{0,4},{1,2},{2,1},{3,7},{4,0},{5,6},{6,5},{7,3},{8,12},{9,10},{10,... | collective-permute-start | bytes 49160 | tf_op jit(solution)/shard_map/ppermute | solution.py:406
where the time goes:
time: 24.5 us; the launch traced here: 24.3 us
  starting transfers between devices  12.4 us (51%)
  waiting for transfers between devices  5.47 us (22%)
  Pallas kernels  5.13 us (21%)
  between operations  0.66 us (3%)
  local copies, waits for them, and re-layouts  0.64 us (3%)
    ppermute x6, starting transfers between devices, swap(): return lax.ppermute(array, ('gx', 'gy'), pairs)  8.23 us
    pallas_call x5, Pallas kernels, call(): pl.pallas_call(kernel, out_shape=[shape if hasattr(shape, 'dtype') else j...  5.13 us
    all_to_all x1, starting transfers between devices, everyones(): return lax.all_to_all(copies, ('gx', 'gy'), 0, 0)  4.14 us
    ppermute x6, waiting for transfers between devices, swap(): return lax.ppermute(array, ('gx', 'gy'), pairs)  2.9 us
    all_to_all x1, waiting for transfers between devices, everyones(): return lax.all_to_all(copies, ('gx', 'gy'), 0, 0)  2.56 us
    broadcast_in_dim x1, local copies, waits for them, and re-layouts, everyones(): copies = jnp.broadcast_to(sketch[None], (count,) + sketch.shape)  0.64 us
  transfers between devices with their start and end apart: 7, of which 3 were waited for; matrix products, arithmetic and copies ran while one was open for 0% of the time, Pallas kernels for 6%

commit v1 on v0

--- a/solution.py
+++ b/solution.py
@@ -392,18 +392,24 @@
 
 
 def swap(array, axis, turn):
-    nx, ny = lax.axis_size("gx"), lax.axis_size("gy")
+    parts, nx, ny = (lax.axis_size(name) for name in ("parts", "gx", "gy"))
     pairs = []
-    for x in range(nx):
-        for y in range(ny):
-            here, count = (x, nx) if axis == "gx" else (y, ny)
-            there = here + 1 if here % 2 == turn else here - 1
-            if 0 <= there < count:
-                partner = (there, y) if axis == "gx" else (x, there)
-            else:
-                partner = (x, y ^ 1) if axis == "gx" else (x ^ 1, y)
-            pairs.append((x * ny + y, partner[0] * ny + partner[1]))
-    return lax.ppermute(array, ("gx", "gy"), pairs)
+    for part in range(parts):
+        for x in range(nx):
+            for y in range(ny):
+                here, count = (x, nx) if axis == "gx" else (y, ny)
+                there = here + 1 if here % 2 == turn else here - 1
+                if 0 <= there < count:
+                    partner = (part, there, y) if axis == "gx" else (part, x, there)
+                elif axis == "gy":
+                    partner = (part, x ^ 1, y)
+                else:
+                    partner = (part, x, y ^ 1) if parts % 2 else (part ^ 1, x, y)
+                source, target = (
+                    (p * nx + i) * ny + j for p, i, j in ((part, x, y), partner)
+                )
+                pairs.append((source, target))
+    return lax.ppermute(array, ("parts", "gx", "gy"), pairs)
 
 
 def everyones(sketch):

time: 24.5 us -> 24.6 us (level)
  no operation moved by 1% of the time
where the time goes in v1:
time: 24.6 us; the launch traced here: 24.4 us
  starting transfers between devices  12.6 us (51%)
  waiting for transfers between devices  5.37 us (22%)
  Pallas kernels  5.13 us (21%)
  between operations  0.66 us (3%)
  local copies, waits for them, and re-layouts  0.64 us (3%)
    ppermute x6, starting transfers between devices, swap(): return lax.ppermute(array, ('parts', 'gx', 'gy'), pairs)  8.24 us
    pallas_call x5, Pallas kernels, call(): pl.pallas_call(kernel, out_shape=[shape if hasattr(shape, 'dtype') else j...  5.13 us
    all_to_all x1, starting transfers between devices, everyones(): return lax.all_to_all(copies, ('gx', 'gy'), 0, 0)  4.36 us
    ppermute x6, waiting for transfers between devices, swap(): return lax.ppermute(array, ('parts', 'gx', 'gy'), pairs)  2.8 us
    all_to_all x1, waiting for transfers between devices, everyones(): return lax.all_to_all(copies, ('gx', 'gy'), 0, 0)  2.56 us
    broadcast_in_dim x1, local copies, waits for them, and re-layouts, everyones(): copies = jnp.broadcast_to(sketch[None], (count,) + sketch.shape)  0.64 us
  transfers between devices with their start and end apart: 7, of which 3 were waited for; matrix products, arithmetic and copies ran while one was open for 0% of the time, Pallas kernels for 6%

profile of v1, /device:TPU:0, one launch (start us, length us, event | category | flops | bytes accessed | tf_op | source)
XLA Modules:
  0.0 24.4 jit_solution(10037573877257592189)
XLA Ops:
  0.6 1.5 %shard_map.68 = (f32[4,8,1024]{2,1,0:T(8,128)S(1)}, f32[4,8,1024]{2,1,0:T(8,128)S(1)}, f32[4,8,1024]{2,1,0:T(8,128)S(1)}, f32[4,8,1024]{2,1,0:T(8,128)S(1)}, f32...) custom-call(f32[4,8,1024]{2,1,0:T(8,128)} %b_hbm.1, ...), custom_call_target="tpu_custom_call" | custom-call | tf_op jit(solution)/shard_map/pallas_call | solution.py:380
  2.1 3.0 %collective-permute-start = (f32[28,1024]{1,0:T(8,128)S(1)}, f32[28,1024]{1,0:T(8,128)S(1)}, u32[]{:S(2)}, u32[]{:S(2)}) collective-permute-start(f32[28,1024]{1,0:T(8,128)S(1)} %get-tuple-element.39), channel_id=1, source_target_pairs={{0,16},{1,17},{2,18},{3,19},{4,8},{5,9},{6,10},{7,11},{8,4},{9,5},... | collective-permute-start | bytes 344072 | tf_op jit(solution)/shard_map/ppermute | solution.py:412
  5.1 0.1 collective-permute-start.1
  5.3 0.4 %collective-permute-start.2 = (f32[16,1024]{1,0:T(8,128)S(1)}, f32[16,1024]{1,0:T(8,128)S(1)}, u32[]{:S(2)}, u32[]{:S(2)}) collective-permute-start(f32[16,1024]{1,0:T(8,128)S(1)} %get-tuple-element.35.own_second_ref), channel_id=1, source_target_pairs={{0,4},{1,2},{2,1},{3,7},{4,0},{5,6},{6,5},{7,3},{8,12},{9,10},{10,... | collective-permute-start | bytes 196616 | tf_op jit(solution)/shard_map/ppermute | solution.py:412
  5.6 2.8 %collective-permute-start.3 = (f32[16,1024]{1,0:T(8,128)S(1)}, f32[16,1024]{1,0:T(8,128)S(1)}, u32[]{:S(2)}, u32[]{:S(2)}) collective-permute-start(f32[16,1024]{1,0:T(8,128)S(1)} %get-tuple-element.36.own_first_ref), channel_id=1, source_target_pairs={{0,1},{1,0},{2,3},{3,2},{4,5},{5,4},{6,7},{7,6},{8,9},{9,8},{10,11... | collective-permute-start | bytes 196616 | tf_op jit(solution)/shard_map/ppermute | solution.py:412
  8.4 0.9 %shard_map.69 = (bf16[1024,1024]{1,0:T(8,128)(2,1)S(1)}, bf16[512,1024]{1,0:T(8,128)(2,1)S(1)}, f32[2,128]{1,0:T(2,128)S(1)}) custom-call(f32[4,8,1024]{2,1,0:T(8,128)S(1)} %get-tuple-element.27.b_ref, f32[4,8,1024]{2,1,0:T(8,128)S(1)} %get-tuple-element.31.draw_ref, f32[4,8,1024]{2,1,0:T(8,128)S(1)} %get-tuple-element.32.slot_ref), custom_call_target="tpu_custom_call" | custom-call | flops 25165824 | tf_op jit(solution)/shard_map/pallas_call | solution.py:380
  9.3 0.0 collective-permute-done.got_second_ref.x_second_ref
  9.3 0.0 collective-permute-done.1.got_first_ref.x_first_ref
  9.3 0.6 %shard_map.70 = (f32[6,8,1024]{2,1,0:T(8,128)S(1)}, f32[5,8,1024]{2,1,0:T(8,128)S(1)}, f32[4,8,1024]{2,1,0:T(8,128)S(1)}, f32[16,32]{1,0:T(8,128)S(1)}) custom-call(f32[4,8,1024]{2,1,0:T(8,128)S(1)} %get-tuple-element.27.b_ref, f32[4,8,1024]{2,1,0:T(8,128)S(1)} %get-tuple-element.37.cond_ref, f32[4,8,1024]{2,1,0:T(8,128)S(1)} %get-tuple-element.28.cap_ref, ...), custom_call_target="tpu_custom_call" | custom-call | flops 25165824 | tf_op jit(solution)/shard_map/pallas_call | solution.py:380
  10.0 0.0 collective-permute-done.2.y_second_ref
  10.0 0.8 %collective-permute-done.3.y_first_ref = f32[16,1024]{1,0:T(8,128)S(1)} collective-permute-done((f32[16,1024]{1,0:T(8,128)S(1)}, f32[16,1024]{1,0:T(8,128)S(1)}, u32[]{:S(2)}, u32[]{:S(2)}) %collective-permute-start.3) | collective-permute-done | bytes 65568 | tf_op jit(solution)/shard_map/ppermute | solution.py:412
  10.7 1.0 %shard_map.71 = (f32[4,8,1024]{2,1,0:T(8,128)S(1)}, f32[4,8,1024]{2,1,0:T(8,128)S(1)}, f32[4,128]{1,0:T(4,128)S(1)}, f32[4,1024]{1,0:T(4,128)S(1)}, f32[4,1024]{1,0:T(4,128)S(1)}, /*index=5*/f32[24,1024]{1,0:T(8,128)S(1)}) custom-call(f32[4,8,1024]{2,1,0:T(8,128)S(1)} %get-tuple-element.27.b_ref, f32[4,8,1024]{2,1,0:T(8,128)S(1)} %get-tuple-element.28.cap_ref, ...), custom_call_target="tpu_custom_call" | custom-call | flops 25165824 | tf_op jit(solution)/shard_map/pallas_call | solution.py:380
  11.8 0.6 %broadcast_in_dim.2 = f32[16,4,128]{2,1,0:T(4,128)} broadcast(f32[4,128]{1,0:T(4,128)S(1)} %get-tuple-element.46), dimensions={1,2} | broadcast | bytes 34816 | tf_op jit(solution)/shard_map/broadcast_in_dim | solution.py:417
  12.4 4.4 %all-to-all-start = ((f32[16,4,128]{2,1,0:T(4,128)}), f32[16,4,128]{2,1,0:T(4,128)S(1)}, u32[]{:S(2)}, u32[]{:S(2)}) async-start(f32[16,4,128]{2,1,0:T(4,128)} %broadcast_in_dim.2), calls=%async_computation | async-start | bytes 65536 | tf_op jit(solution)/shard_map/all_to_all | solution.py:418
  16.8 1.9 %collective-permute-start.4 = (f32[4,1024]{1,0:T(4,128)S(1)}, f32[4,1024]{1,0:T(4,128)S(1)}, u32[]{:S(2)}, u32[]{:S(2)}) collective-permute-start(f32[4,1024]{1,0:T(4,128)S(1)} %get-tuple-element.50), channel_id=1, source_target_pairs={{0,1},{1,0},{2,3},{3,2},{4,5},{5,4},{6,7},{7,6},{8,9},{9,8},{10,11... | collective-permute-start | bytes 49160 | tf_op jit(solution)/shard_map/ppermute | solution.py:412
  18.7 0.0 collective-permute-start.5
  18.7 2.0 %collective-permute-done.4.corner_first_ref = f32[4,1024]{1,0:T(4,128)S(1)} collective-permute-done((f32[4,1024]{1,0:T(4,128)S(1)}, f32[4,1024]{1,0:T(4,128)S(1)}, u32[]{:S(2)}, u32[]{:S(2)}) %collective-permute-start.4) | collective-permute-done | bytes 16416 | tf_op jit(solution)/shard_map/ppermute | solution.py:412
  20.7 0.0 collective-permute-done.5.corner_second_ref
  20.7 2.6 %all-to-all-done.sketch_ref = f32[16,4,128]{2,1,0:T(4,128)S(1)} async-done(((f32[16,4,128]{2,1,0:T(4,128)}), f32[16,4,128]{2,1,0:T(4,128)S(1)}, u32[]{:S(2)}, u32[]{:S(2)}) %all-to-all-start) | async-done | bytes 32800 | tf_op jit(solution)/shard_map/all_to_all | solution.py:418
  23.3 1.1 %shard_map.72 = (f32[4,8,1024]{2,1,0:T(8,128)}, f32[4,8,1024]{2,1,0:T(8,128)}) custom-call(f32[16,4,128]{2,1,0:T(4,128)S(1)} %all-to-all-done.sketch_ref, f32[4,8,1024]{2,1,0:T(8,128)S(1)} %get-tuple-element.27.b_ref, f32[4,8,1024]{2,1,0:T(8,128)S(1)} %get-tuple-element.47.image_ref, f32[4,8,1024]{2,1,0:T(8,128)S(1)} %get-tuple-element.48.twice_ref, ...), custom_call_target="tpu_custom_call" | custom-call | tf_op jit(solution)/shard_map/pallas_call | solution.py:380
Async XLA Ops:
  2.1 7.2 %collective-permute-start = (f32[28,1024]{1,0:T(8,128)S(1)}, f32[28,1024]{1,0:T(8,128)S(1)}, u32[]{:S(2)}, u32[]{:S(2)}) collective-permute-start(f32[28,1024]{1,0:T(8,128)S(1)} %get-tuple-element.39), channel_id=1, source_target_pairs={{0,16},{1,17},{2,18},{3,19},{4,8},{5,9},{6,10},{7,11},{8,4},{9,5},... | collective-permute-start | bytes 344072 | tf_op jit(solution)/shard_map/ppermute | solution.py:412
  5.1 4.2 %collective-permute-start.1 = (f32[28,1024]{1,0:T(8,128)S(1)}, f32[28,1024]{1,0:T(8,128)S(1)}, u32[]{:S(2)}, u32[]{:S(2)}) collective-permute-start(f32[28,1024]{1,0:T(8,128)S(1)} %get-tuple-element.40), channel_id=1, source_target_pairs={{0,4},{1,5},{2,6},{3,7},{4,0},{5,1},{6,2},{7,3},{8,12},{9,13},{10,... | collective-permute-start | bytes 344072 | tf_op jit(solution)/shard_map/ppermute | solution.py:412
  5.3 4.7 %collective-permute-start.2 = (f32[16,1024]{1,0:T(8,128)S(1)}, f32[16,1024]{1,0:T(8,128)S(1)}, u32[]{:S(2)}, u32[]{:S(2)}) collective-permute-start(f32[16,1024]{1,0:T(8,128)S(1)} %get-tuple-element.35.own_second_ref), channel_id=1, source_target_pairs={{0,4},{1,2},{2,1},{3,7},{4,0},{5,6},{6,5},{7,3},{8,12},{9,10},{10,... | collective-permute-start | bytes 196616 | tf_op jit(solution)/shard_map/ppermute | solution.py:412
  5.6 5.1 %collective-permute-start.3 = (f32[16,1024]{1,0:T(8,128)S(1)}, f32[16,1024]{1,0:T(8,128)S(1)}, u32[]{:S(2)}, u32[]{:S(2)}) collective-permute-start(f32[16,1024]{1,0:T(8,128)S(1)} %get-tuple-element.36.own_first_ref), channel_id=1, source_target_pairs={{0,1},{1,0},{2,3},{3,2},{4,5},{5,4},{6,7},{7,6},{8,9},{9,8},{10,11... | collective-permute-start | bytes 196616 | tf_op jit(solution)/shard_map/ppermute | solution.py:412
  12.4 10.9 %all-to-all-start = ((f32[16,4,128]{2,1,0:T(4,128)}), f32[16,4,128]{2,1,0:T(4,128)S(1)}, u32[]{:S(2)}, u32[]{:S(2)}) async-start(f32[16,4,128]{2,1,0:T(4,128)} %broadcast_in_dim.2), calls=%async_computation | async-start | bytes 65536 | tf_op jit(solution)/shard_map/all_to_all | solution.py:418
  16.8 3.9 %collective-permute-start.4 = (f32[4,1024]{1,0:T(4,128)S(1)}, f32[4,1024]{1,0:T(4,128)S(1)}, u32[]{:S(2)}, u32[]{:S(2)}) collective-permute-start(f32[4,1024]{1,0:T(4,128)S(1)} %get-tuple-element.50), channel_id=1, source_target_pairs={{0,1},{1,0},{2,3},{3,2},{4,5},{5,4},{6,7},{7,6},{8,9},{9,8},{10,11... | collective-permute-start | bytes 49160 | tf_op jit(solution)/shard_map/ppermute | solution.py:412
  18.7 2.0 %collective-permute-start.5 = (f32[4,1024]{1,0:T(4,128)S(1)}, f32[4,1024]{1,0:T(4,128)S(1)}, u32[]{:S(2)}, u32[]{:S(2)}) collective-permute-start(f32[4,1024]{1,0:T(4,128)S(1)} %get-tuple-element.51), channel_id=1, source_target_pairs={{0,4},{1,2},{2,1},{3,7},{4,0},{5,6},{6,5},{7,3},{8,12},{9,10},{10,... | collective-permute-start | bytes 49160 | tf_op jit(solution)/shard_map/ppermute | solution.py:412

commit v2 on v0

--- a/solution.py
+++ b/solution.py
@@ -407,9 +407,13 @@
 
 
 def everyones(sketch):
-    count = lax.axis_size("gx") * lax.axis_size("gy")
-    copies = jnp.broadcast_to(sketch[None], (count,) + sketch.shape)
-    return lax.all_to_all(copies, ("gx", "gy"), 0, 0)
+    nx, ny = lax.axis_size("gx"), lax.axis_size("gy")
+    middle = nx // 2 - 1, ny // 2
+    places = [(x, y) for x in range(nx) for y in range(ny)]
+    places.sort(key=lambda at: (abs(at[1] - middle[1]), abs(at[0] - middle[0]), at))
+    group = [x * ny + y for x, y in places]
+    copies = jnp.broadcast_to(sketch[None], (nx * ny,) + sketch.shape)
+    return lax.all_to_all(copies, ("gx", "gy"), 0, 0, axis_index_groups=[group])
 
 
 def body(b, warmth, phase, slots, draw):

time: 24.5 us -> 22.7 us (0.927)
  waiting for transfers between devices: 5.47 us -> 4.39 us
  starting transfers between devices: 12.4 us -> 11.7 us
    all_to_all x1, waiting for transfers between devices: 2.56 us -> 0.35 us  [everyones(): return lax.all_to_all(copies, ('gx', 'gy'), 0, 0, axis_index_groups=[group])]
    ppermute x6, starting transfers between devices: 8.23 us -> 6.89 us  [swap(): return lax.ppermute(array, ('gx', 'gy'), pairs)]
    ppermute x6, waiting for transfers between devices: 2.9 us -> 4.04 us  [swap(): return lax.ppermute(array, ('gx', 'gy'), pairs)]
    all_to_all x1, starting transfers between devices: 4.14 us -> 4.8 us  [everyones(): return lax.all_to_all(copies, ('gx', 'gy'), 0, 0, axis_index_groups=[group])]
  transfers between devices with their start and end apart: 7 -> 7, of which waited for: 3 -> 3; matrix products, arithmetic and copies ran while one was open for 0% -> 0% of each run, Pallas kernels for 6% -> 7%
where the time goes in v2:
time: 22.7 us; the launch traced here: 22.5 us
  starting transfers between devices  11.7 us (52%)
  Pallas kernels  5.13 us (23%)
  waiting for transfers between devices  4.39 us (19%)
  between operations  0.66 us (3%)
  local copies, waits for them, and re-layouts  0.64 us (3%)
    ppermute x6, starting transfers between devices, swap(): return lax.ppermute(array, ('gx', 'gy'), pairs)  6.89 us
    pallas_call x5, Pallas kernels, call(): pl.pallas_call(kernel, out_shape=[shape if hasattr(shape, 'dtype') else j...  5.13 us
    all_to_all x1, starting transfers between devices, everyones(): return lax.all_to_all(copies, ('gx', 'gy'), 0, 0, axis_index_groups=[group])  4.8 us
    ppermute x6, waiting for transfers between devices, swap(): return lax.ppermute(array, ('gx', 'gy'), pairs)  4.04 us
    broadcast_in_dim x1, local copies, waits for them, and re-layouts, everyones(): copies = jnp.broadcast_to(sketch[None], (nx * ny,) + sketch.shape)  0.64 us
  transfers between devices with their start and end apart: 7, of which 3 were waited for; matrix products, arithmetic and copies ran while one was open for 0% of the time, Pallas kernels for 7%

profile of v2, /device:TPU:0, one launch (start us, length us, event | category | flops | bytes accessed | tf_op | source)
XLA Modules:
  0.0 22.5 jit_solution(8831364746311525731)
XLA Ops:
  0.6 1.5 %shard_map.68 = (f32[4,8,1024]{2,1,0:T(8,128)S(1)}, f32[4,8,1024]{2,1,0:T(8,128)S(1)}, f32[4,8,1024]{2,1,0:T(8,128)S(1)}, f32[4,8,1024]{2,1,0:T(8,128)S(1)}, f32...) custom-call(f32[4,8,1024]{2,1,0:T(8,128)} %b_hbm.1, ...), custom_call_target="tpu_custom_call" | custom-call | tf_op jit(solution)/shard_map/pallas_call | solution.py:380
  2.1 3.1 %collective-permute-start = (f32[28,1024]{1,0:T(8,128)S(1)}, f32[28,1024]{1,0:T(8,128)S(1)}, u32[]{:S(2)}, u32[]{:S(2)}) collective-permute-start(f32[28,1024]{1,0:T(8,128)S(1)} %get-tuple-element.39), channel_id=1, source_target_pairs={{0,1},{1,0},{2,3},{3,2},{4,8},{5,9},{6,10},{7,11},{8,4},{9,5},{10,... | collective-permute-start | bytes 344072 | tf_op jit(solution)/shard_map/ppermute | solution.py:406
  5.2 0.1 collective-permute-start.1
  5.3 0.5 %collective-permute-start.2 = (f32[16,1024]{1,0:T(8,128)S(1)}, f32[16,1024]{1,0:T(8,128)S(1)}, u32[]{:S(2)}, u32[]{:S(2)}) collective-permute-start(f32[16,1024]{1,0:T(8,128)S(1)} %get-tuple-element.35.own_second_ref), channel_id=1, source_target_pairs={{0,4},{1,2},{2,1},{3,7},{4,0},{5,6},{6,5},{7,3},{8,12},{9,10},{10,... | collective-permute-start | bytes 196616 | tf_op jit(solution)/shard_map/ppermute | solution.py:406
  5.7 2.7 %collective-permute-start.3 = (f32[16,1024]{1,0:T(8,128)S(1)}, f32[16,1024]{1,0:T(8,128)S(1)}, u32[]{:S(2)}, u32[]{:S(2)}) collective-permute-start(f32[16,1024]{1,0:T(8,128)S(1)} %get-tuple-element.36.own_first_ref), channel_id=1, source_target_pairs={{0,1},{1,0},{2,3},{3,2},{4,5},{5,4},{6,7},{7,6},{8,9},{9,8},{10,11... | collective-permute-start | bytes 196616 | tf_op jit(solution)/shard_map/ppermute | solution.py:406
  8.4 0.9 %shard_map.69 = (bf16[1024,1024]{1,0:T(8,128)(2,1)S(1)}, bf16[512,1024]{1,0:T(8,128)(2,1)S(1)}, f32[2,128]{1,0:T(2,128)S(1)}) custom-call(f32[4,8,1024]{2,1,0:T(8,128)S(1)} %get-tuple-element.27.b_ref, f32[4,8,1024]{2,1,0:T(8,128)S(1)} %get-tuple-element.31.draw_ref, f32[4,8,1024]{2,1,0:T(8,128)S(1)} %get-tuple-element.32.slot_ref), custom_call_target="tpu_custom_call" | custom-call | flops 25165824 | tf_op jit(solution)/shard_map/pallas_call | solution.py:380
  9.3 0.0 collective-permute-done.got_second_ref.x_second_ref
  9.3 0.0 collective-permute-done.1.got_first_ref.x_first_ref
  9.3 0.6 %shard_map.70 = (f32[6,8,1024]{2,1,0:T(8,128)S(1)}, f32[5,8,1024]{2,1,0:T(8,128)S(1)}, f32[4,8,1024]{2,1,0:T(8,128)S(1)}, f32[16,32]{1,0:T(8,128)S(1)}) custom-call(f32[4,8,1024]{2,1,0:T(8,128)S(1)} %get-tuple-element.27.b_ref, f32[4,8,1024]{2,1,0:T(8,128)S(1)} %get-tuple-element.37.cond_ref, f32[4,8,1024]{2,1,0:T(8,128)S(1)} %get-tuple-element.28.cap_ref, ...), custom_call_target="tpu_custom_call" | custom-call | flops 25165824 | tf_op jit(solution)/shard_map/pallas_call | solution.py:380
  9.9 0.0 collective-permute-done.2.y_second_ref
  10.0 0.9 %collective-permute-done.3.y_first_ref = f32[16,1024]{1,0:T(8,128)S(1)} collective-permute-done((f32[16,1024]{1,0:T(8,128)S(1)}, f32[16,1024]{1,0:T(8,128)S(1)}, u32[]{:S(2)}, u32[]{:S(2)}) %collective-permute-start.3) | collective-permute-done | bytes 65568 | tf_op jit(solution)/shard_map/ppermute | solution.py:406
  10.8 1.0 %shard_map.71 = (f32[4,8,1024]{2,1,0:T(8,128)S(1)}, f32[4,8,1024]{2,1,0:T(8,128)S(1)}, f32[4,128]{1,0:T(4,128)S(1)}, f32[4,1024]{1,0:T(4,128)S(1)}, f32[4,1024]{1,0:T(4,128)S(1)}, /*index=5*/f32[24,1024]{1,0:T(8,128)S(1)}) custom-call(f32[4,8,1024]{2,1,0:T(8,128)S(1)} %get-tuple-element.27.b_ref, f32[4,8,1024]{2,1,0:T(8,128)S(1)} %get-tuple-element.28.cap_ref, ...), custom_call_target="tpu_custom_call" | custom-call | flops 25165824 | tf_op jit(solution)/shard_map/pallas_call | solution.py:380
  11.8 0.6 %broadcast_in_dim.2 = f32[16,4,128]{2,1,0:T(4,128)} broadcast(f32[4,128]{1,0:T(4,128)S(1)} %get-tuple-element.46), dimensions={1,2} | broadcast | bytes 34816 | tf_op jit(solution)/shard_map/broadcast_in_dim | solution.py:415
  12.5 4.8 %all-to-all-start = ((f32[16,4,128]{2,1,0:T(4,128)}), f32[16,4,128]{2,1,0:T(4,128)S(1)}, u32[]{:S(2)}, u32[]{:S(2)}) async-start(f32[16,4,128]{2,1,0:T(4,128)} %broadcast_in_dim.2), calls=%async_computation | async-start | bytes 65536 | tf_op jit(solution)/shard_map/all_to_all | solution.py:416
  17.3 0.6 %collective-permute-start.4 = (f32[4,1024]{1,0:T(4,128)S(1)}, f32[4,1024]{1,0:T(4,128)S(1)}, u32[]{:S(2)}, u32[]{:S(2)}) collective-permute-start(f32[4,1024]{1,0:T(4,128)S(1)} %get-tuple-element.50), channel_id=1, source_target_pairs={{0,1},{1,0},{2,3},{3,2},{4,5},{5,4},{6,7},{7,6},{8,9},{9,8},{10,11... | collective-permute-start | bytes 49160 | tf_op jit(solution)/shard_map/ppermute | solution.py:406
  17.9 0.0 collective-permute-start.5
  17.9 3.1 %collective-permute-done.4.corner_first_ref = f32[4,1024]{1,0:T(4,128)S(1)} collective-permute-done((f32[4,1024]{1,0:T(4,128)S(1)}, f32[4,1024]{1,0:T(4,128)S(1)}, u32[]{:S(2)}, u32[]{:S(2)}) %collective-permute-start.4) | collective-permute-done | bytes 16416 | tf_op jit(solution)/shard_map/ppermute | solution.py:406
  21.0 0.0 collective-permute-done.5.corner_second_ref
  21.0 0.3 %all-to-all-done.sketch_ref = f32[16,4,128]{2,1,0:T(4,128)S(1)} async-done(((f32[16,4,128]{2,1,0:T(4,128)}), f32[16,4,128]{2,1,0:T(4,128)S(1)}, u32[]{:S(2)}, u32[]{:S(2)}) %all-to-all-start) | async-done | bytes 32800 | tf_op jit(solution)/shard_map/all_to_all | solution.py:416
  21.4 1.1 %shard_map.72 = (f32[4,8,1024]{2,1,0:T(8,128)}, f32[4,8,1024]{2,1,0:T(8,128)}) custom-call(f32[16,4,128]{2,1,0:T(4,128)S(1)} %all-to-all-done.sketch_ref, f32[4,8,1024]{2,1,0:T(8,128)S(1)} %get-tuple-element.27.b_ref, f32[4,8,1024]{2,1,0:T(8,128)S(1)} %get-tuple-element.47.image_ref, f32[4,8,1024]{2,1,0:T(8,128)S(1)} %get-tuple-element.48.twice_ref, ...), custom_call_target="tpu_custom_call" | custom-call | tf_op jit(solution)/shard_map/pallas_call | solution.py:380
Async XLA Ops:
  2.1 7.2 %collective-permute-start = (f32[28,1024]{1,0:T(8,128)S(1)}, f32[28,1024]{1,0:T(8,128)S(1)}, u32[]{:S(2)}, u32[]{:S(2)}) collective-permute-start(f32[28,1024]{1,0:T(8,128)S(1)} %get-tuple-element.39), channel_id=1, source_target_pairs={{0,1},{1,0},{2,3},{3,2},{4,8},{5,9},{6,10},{7,11},{8,4},{9,5},{10,... | collective-permute-start | bytes 344072 | tf_op jit(solution)/shard_map/ppermute | solution.py:406
  5.2 4.1 %collective-permute-start.1 = (f32[28,1024]{1,0:T(8,128)S(1)}, f32[28,1024]{1,0:T(8,128)S(1)}, u32[]{:S(2)}, u32[]{:S(2)}) collective-permute-start(f32[28,1024]{1,0:T(8,128)S(1)} %get-tuple-element.40), channel_id=1, source_target_pairs={{0,4},{1,5},{2,6},{3,7},{4,0},{5,1},{6,2},{7,3},{8,12},{9,13},{10,... | collective-permute-start | bytes 344072 | tf_op jit(solution)/shard_map/ppermute | solution.py:406
  5.3 4.7 %collective-permute-start.2 = (f32[16,1024]{1,0:T(8,128)S(1)}, f32[16,1024]{1,0:T(8,128)S(1)}, u32[]{:S(2)}, u32[]{:S(2)}) collective-permute-start(f32[16,1024]{1,0:T(8,128)S(1)} %get-tuple-element.35.own_second_ref), channel_id=1, source_target_pairs={{0,4},{1,2},{2,1},{3,7},{4,0},{5,6},{6,5},{7,3},{8,12},{9,10},{10,... | collective-permute-start | bytes 196616 | tf_op jit(solution)/shard_map/ppermute | solution.py:406
  5.7 5.1 %collective-permute-start.3 = (f32[16,1024]{1,0:T(8,128)S(1)}, f32[16,1024]{1,0:T(8,128)S(1)}, u32[]{:S(2)}, u32[]{:S(2)}) collective-permute-start(f32[16,1024]{1,0:T(8,128)S(1)} %get-tuple-element.36.own_first_ref), channel_id=1, source_target_pairs={{0,1},{1,0},{2,3},{3,2},{4,5},{5,4},{6,7},{7,6},{8,9},{9,8},{10,11... | collective-permute-start | bytes 196616 | tf_op jit(solution)/shard_map/ppermute | solution.py:406
  12.5 8.9 %all-to-all-start = ((f32[16,4,128]{2,1,0:T(4,128)}), f32[16,4,128]{2,1,0:T(4,128)S(1)}, u32[]{:S(2)}, u32[]{:S(2)}) async-start(f32[16,4,128]{2,1,0:T(4,128)} %broadcast_in_dim.2), calls=%async_computation | async-start | bytes 65536 | tf_op jit(solution)/shard_map/all_to_all | solution.py:416
  17.3 3.7 %collective-permute-start.4 = (f32[4,1024]{1,0:T(4,128)S(1)}, f32[4,1024]{1,0:T(4,128)S(1)}, u32[]{:S(2)}, u32[]{:S(2)}) collective-permute-start(f32[4,1024]{1,0:T(4,128)S(1)} %get-tuple-element.50), channel_id=1, source_target_pairs={{0,1},{1,0},{2,3},{3,2},{4,5},{5,4},{6,7},{7,6},{8,9},{9,8},{10,11... | collective-permute-start | bytes 49160 | tf_op jit(solution)/shard_map/ppermute | solution.py:406
  17.9 3.2 %collective-permute-start.5 = (f32[4,1024]{1,0:T(4,128)S(1)}, f32[4,1024]{1,0:T(4,128)S(1)}, u32[]{:S(2)}, u32[]{:S(2)}) collective-permute-start(f32[4,1024]{1,0:T(4,128)S(1)} %get-tuple-element.51), channel_id=1, source_target_pairs={{0,4},{1,2},{2,1},{3,7},{4,0},{5,6},{6,5},{7,3},{8,12},{9,10},{10,... | collective-permute-start | bytes 49160 | tf_op jit(solution)/shard_map/ppermute | solution.py:406

commit v3 on v2

--- a/solution.py
+++ b/solution.py
@@ -410,7 +410,7 @@
     nx, ny = lax.axis_size("gx"), lax.axis_size("gy")
     middle = nx // 2 - 1, ny // 2
     places = [(x, y) for x in range(nx) for y in range(ny)]
-    places.sort(key=lambda at: (abs(at[1] - middle[1]), abs(at[0] - middle[0]), at))
+    places.sort(key=lambda at: (at != middle, -abs(at[1] - middle[1]), at[0] % 2, at))
     group = [x * ny + y for x, y in places]
     copies = jnp.broadcast_to(sketch[None], (nx * ny,) + sketch.shape)
     return lax.all_to_all(copies, ("gx", "gy"), 0, 0, axis_index_groups=[group])

time: 22.7 us -> 22.9 us (level)
  no operation moved by 1% of the time
where the time goes in v3:
time: 22.9 us; the launch traced here: 22.7 us
  starting transfers between devices  11.7 us (51%)
  Pallas kernels  5.13 us (22%)
  waiting for transfers between devices  4.59 us (20%)
  between operations  0.66 us (3%)
  local copies, waits for them, and re-layouts  0.64 us (3%)
    ppermute x6, starting transfers between devices, swap(): return lax.ppermute(array, ('gx', 'gy'), pairs)  6.91 us
    pallas_call x5, Pallas kernels, call(): pl.pallas_call(kernel, out_shape=[shape if hasattr(shape, 'dtype') else j...  5.13 us
    all_to_all x1, starting transfers between devices, everyones(): return lax.all_to_all(copies, ('gx', 'gy'), 0, 0, axis_index_groups=[group])  4.76 us
    ppermute x6, waiting for transfers between devices, swap(): return lax.ppermute(array, ('gx', 'gy'), pairs)  4.03 us
    broadcast_in_dim x1, local copies, waits for them, and re-layouts, everyones(): copies = jnp.broadcast_to(sketch[None], (nx * ny,) + sketch.shape)  0.64 us
    all_to_all x1, waiting for transfers between devices, everyones(): return lax.all_to_all(copies, ('gx', 'gy'), 0, 0, axis_index_groups=[group])  0.56 us
  transfers between devices with their start and end apart: 7, of which 3 were waited for; matrix products, arithmetic and copies ran while one was open for 0% of the time, Pallas kernels for 7%

profile of v3, /device:TPU:0, one launch (start us, length us, event | category | flops | bytes accessed | tf_op | source)
XLA Modules:
  0.0 22.7 jit_solution(13638409327893565409)
XLA Ops:
  0.6 1.5 %shard_map.68 = (f32[4,8,1024]{2,1,0:T(8,128)S(1)}, f32[4,8,1024]{2,1,0:T(8,128)S(1)}, f32[4,8,1024]{2,1,0:T(8,128)S(1)}, f32[4,8,1024]{2,1,0:T(8,128)S(1)}, f32...) custom-call(f32[4,8,1024]{2,1,0:T(8,128)} %b_hbm.1, ...), custom_call_target="tpu_custom_call" | custom-call | tf_op jit(solution)/shard_map/pallas_call | solution.py:380
  2.1 3.1 %collective-permute-start = (f32[28,1024]{1,0:T(8,128)S(1)}, f32[28,1024]{1,0:T(8,128)S(1)}, u32[]{:S(2)}, u32[]{:S(2)}) collective-permute-start(f32[28,1024]{1,0:T(8,128)S(1)} %get-tuple-element.39), channel_id=1, source_target_pairs={{0,1},{1,0},{2,3},{3,2},{4,8},{5,9},{6,10},{7,11},{8,4},{9,5},{10,... | collective-permute-start | bytes 344072 | tf_op jit(solution)/shard_map/ppermute | solution.py:406
  5.2 0.1 collective-permute-start.1
  5.3 0.5 %collective-permute-start.2 = (f32[16,1024]{1,0:T(8,128)S(1)}, f32[16,1024]{1,0:T(8,128)S(1)}, u32[]{:S(2)}, u32[]{:S(2)}) collective-permute-start(f32[16,1024]{1,0:T(8,128)S(1)} %get-tuple-element.35.own_second_ref), channel_id=1, source_target_pairs={{0,4},{1,2},{2,1},{3,7},{4,0},{5,6},{6,5},{7,3},{8,12},{9,10},{10,... | collective-permute-start | bytes 196616 | tf_op jit(solution)/shard_map/ppermute | solution.py:406
  5.7 2.7 %collective-permute-start.3 = (f32[16,1024]{1,0:T(8,128)S(1)}, f32[16,1024]{1,0:T(8,128)S(1)}, u32[]{:S(2)}, u32[]{:S(2)}) collective-permute-start(f32[16,1024]{1,0:T(8,128)S(1)} %get-tuple-element.36.own_first_ref), channel_id=1, source_target_pairs={{0,1},{1,0},{2,3},{3,2},{4,5},{5,4},{6,7},{7,6},{8,9},{9,8},{10,11... | collective-permute-start | bytes 196616 | tf_op jit(solution)/shard_map/ppermute | solution.py:406
  8.4 0.9 %shard_map.69 = (bf16[1024,1024]{1,0:T(8,128)(2,1)S(1)}, bf16[512,1024]{1,0:T(8,128)(2,1)S(1)}, f32[2,128]{1,0:T(2,128)S(1)}) custom-call(f32[4,8,1024]{2,1,0:T(8,128)S(1)} %get-tuple-element.27.b_ref, f32[4,8,1024]{2,1,0:T(8,128)S(1)} %get-tuple-element.31.draw_ref, f32[4,8,1024]{2,1,0:T(8,128)S(1)} %get-tuple-element.32.slot_ref), custom_call_target="tpu_custom_call" | custom-call | flops 25165824 | tf_op jit(solution)/shard_map/pallas_call | solution.py:380
  9.3 0.0 collective-permute-done.got_second_ref.x_second_ref
  9.3 0.0 collective-permute-done.1.got_first_ref.x_first_ref
  9.3 0.6 %shard_map.70 = (f32[6,8,1024]{2,1,0:T(8,128)S(1)}, f32[5,8,1024]{2,1,0:T(8,128)S(1)}, f32[4,8,1024]{2,1,0:T(8,128)S(1)}, f32[16,32]{1,0:T(8,128)S(1)}) custom-call(f32[4,8,1024]{2,1,0:T(8,128)S(1)} %get-tuple-element.27.b_ref, f32[4,8,1024]{2,1,0:T(8,128)S(1)} %get-tuple-element.37.cond_ref, f32[4,8,1024]{2,1,0:T(8,128)S(1)} %get-tuple-element.28.cap_ref, ...), custom_call_target="tpu_custom_call" | custom-call | flops 25165824 | tf_op jit(solution)/shard_map/pallas_call | solution.py:380
  9.9 0.0 collective-permute-done.2.y_second_ref
  10.0 0.9 %collective-permute-done.3.y_first_ref = f32[16,1024]{1,0:T(8,128)S(1)} collective-permute-done((f32[16,1024]{1,0:T(8,128)S(1)}, f32[16,1024]{1,0:T(8,128)S(1)}, u32[]{:S(2)}, u32[]{:S(2)}) %collective-permute-start.3) | collective-permute-done | bytes 65568 | tf_op jit(solution)/shard_map/ppermute | solution.py:406
  10.8 1.0 %shard_map.71 = (f32[4,8,1024]{2,1,0:T(8,128)S(1)}, f32[4,8,1024]{2,1,0:T(8,128)S(1)}, f32[4,128]{1,0:T(4,128)S(1)}, f32[4,1024]{1,0:T(4,128)S(1)}, f32[4,1024]{1,0:T(4,128)S(1)}, /*index=5*/f32[24,1024]{1,0:T(8,128)S(1)}) custom-call(f32[4,8,1024]{2,1,0:T(8,128)S(1)} %get-tuple-element.27.b_ref, f32[4,8,1024]{2,1,0:T(8,128)S(1)} %get-tuple-element.28.cap_ref, ...), custom_call_target="tpu_custom_call" | custom-call | flops 25165824 | tf_op jit(solution)/shard_map/pallas_call | solution.py:380
  11.8 0.6 %broadcast_in_dim.2 = f32[16,4,128]{2,1,0:T(4,128)} broadcast(f32[4,128]{1,0:T(4,128)S(1)} %get-tuple-element.46), dimensions={1,2} | broadcast | bytes 34816 | tf_op jit(solution)/shard_map/broadcast_in_dim | solution.py:415
  12.5 4.8 %all-to-all-start = ((f32[16,4,128]{2,1,0:T(4,128)}), f32[16,4,128]{2,1,0:T(4,128)S(1)}, u32[]{:S(2)}, u32[]{:S(2)}) async-start(f32[16,4,128]{2,1,0:T(4,128)} %broadcast_in_dim.2), calls=%async_computation | async-start | bytes 65536 | tf_op jit(solution)/shard_map/all_to_all | solution.py:416
  17.2 0.6 %collective-permute-start.4 = (f32[4,1024]{1,0:T(4,128)S(1)}, f32[4,1024]{1,0:T(4,128)S(1)}, u32[]{:S(2)}, u32[]{:S(2)}) collective-permute-start(f32[4,1024]{1,0:T(4,128)S(1)} %get-tuple-element.50), channel_id=1, source_target_pairs={{0,1},{1,0},{2,3},{3,2},{4,5},{5,4},{6,7},{7,6},{8,9},{9,8},{10,11... | collective-permute-start | bytes 49160 | tf_op jit(solution)/shard_map/ppermute | solution.py:406
  17.9 0.0 collective-permute-start.5
  17.9 3.1 %collective-permute-done.4.corner_first_ref = f32[4,1024]{1,0:T(4,128)S(1)} collective-permute-done((f32[4,1024]{1,0:T(4,128)S(1)}, f32[4,1024]{1,0:T(4,128)S(1)}, u32[]{:S(2)}, u32[]{:S(2)}) %collective-permute-start.4) | collective-permute-done | bytes 16416 | tf_op jit(solution)/shard_map/ppermute | solution.py:406
  21.0 0.0 collective-permute-done.5.corner_second_ref
  21.0 0.6 %all-to-all-done.sketch_ref = f32[16,4,128]{2,1,0:T(4,128)S(1)} async-done(((f32[16,4,128]{2,1,0:T(4,128)}), f32[16,4,128]{2,1,0:T(4,128)S(1)}, u32[]{:S(2)}, u32[]{:S(2)}) %all-to-all-start) | async-done | bytes 32800 | tf_op jit(solution)/shard_map/all_to_all | solution.py:416
  21.6 1.1 %shard_map.72 = (f32[4,8,1024]{2,1,0:T(8,128)}, f32[4,8,1024]{2,1,0:T(8,128)}) custom-call(f32[16,4,128]{2,1,0:T(4,128)S(1)} %all-to-all-done.sketch_ref, f32[4,8,1024]{2,1,0:T(8,128)S(1)} %get-tuple-element.27.b_ref, f32[4,8,1024]{2,1,0:T(8,128)S(1)} %get-tuple-element.47.image_ref, f32[4,8,1024]{2,1,0:T(8,128)S(1)} %get-tuple-element.48.twice_ref, ...), custom_call_target="tpu_custom_call" | custom-call | tf_op jit(solution)/shard_map/pallas_call | solution.py:380
Async XLA Ops:
  2.1 7.2 %collective-permute-start = (f32[28,1024]{1,0:T(8,128)S(1)}, f32[28,1024]{1,0:T(8,128)S(1)}, u32[]{:S(2)}, u32[]{:S(2)}) collective-permute-start(f32[28,1024]{1,0:T(8,128)S(1)} %get-tuple-element.39), channel_id=1, source_target_pairs={{0,1},{1,0},{2,3},{3,2},{4,8},{5,9},{6,10},{7,11},{8,4},{9,5},{10,... | collective-permute-start | bytes 344072 | tf_op jit(solution)/shard_map/ppermute | solution.py:406
  5.2 4.1 %collective-permute-start.1 = (f32[28,1024]{1,0:T(8,128)S(1)}, f32[28,1024]{1,0:T(8,128)S(1)}, u32[]{:S(2)}, u32[]{:S(2)}) collective-permute-start(f32[28,1024]{1,0:T(8,128)S(1)} %get-tuple-element.40), channel_id=1, source_target_pairs={{0,4},{1,5},{2,6},{3,7},{4,0},{5,1},{6,2},{7,3},{8,12},{9,13},{10,... | collective-permute-start | bytes 344072 | tf_op jit(solution)/shard_map/ppermute | solution.py:406
  5.3 4.7 %collective-permute-start.2 = (f32[16,1024]{1,0:T(8,128)S(1)}, f32[16,1024]{1,0:T(8,128)S(1)}, u32[]{:S(2)}, u32[]{:S(2)}) collective-permute-start(f32[16,1024]{1,0:T(8,128)S(1)} %get-tuple-element.35.own_second_ref), channel_id=1, source_target_pairs={{0,4},{1,2},{2,1},{3,7},{4,0},{5,6},{6,5},{7,3},{8,12},{9,10},{10,... | collective-permute-start | bytes 196616 | tf_op jit(solution)/shard_map/ppermute | solution.py:406
  5.7 5.1 %collective-permute-start.3 = (f32[16,1024]{1,0:T(8,128)S(1)}, f32[16,1024]{1,0:T(8,128)S(1)}, u32[]{:S(2)}, u32[]{:S(2)}) collective-permute-start(f32[16,1024]{1,0:T(8,128)S(1)} %get-tuple-element.36.own_first_ref), channel_id=1, source_target_pairs={{0,1},{1,0},{2,3},{3,2},{4,5},{5,4},{6,7},{7,6},{8,9},{9,8},{10,11... | collective-permute-start | bytes 196616 | tf_op jit(solution)/shard_map/ppermute | solution.py:406
  12.5 9.1 %all-to-all-start = ((f32[16,4,128]{2,1,0:T(4,128)}), f32[16,4,128]{2,1,0:T(4,128)S(1)}, u32[]{:S(2)}, u32[]{:S(2)}) async-start(f32[16,4,128]{2,1,0:T(4,128)} %broadcast_in_dim.2), calls=%async_computation | async-start | bytes 65536 | tf_op jit(solution)/shard_map/all_to_all | solution.py:416
  17.2 3.7 %collective-permute-start.4 = (f32[4,1024]{1,0:T(4,128)S(1)}, f32[4,1024]{1,0:T(4,128)S(1)}, u32[]{:S(2)}, u32[]{:S(2)}) collective-permute-start(f32[4,1024]{1,0:T(4,128)S(1)} %get-tuple-element.50), channel_id=1, source_target_pairs={{0,1},{1,0},{2,3},{3,2},{4,5},{5,4},{6,7},{7,6},{8,9},{9,8},{10,11... | collective-permute-start | bytes 49160 | tf_op jit(solution)/shard_map/ppermute | solution.py:406
  17.9 3.1 %collective-permute-start.5 = (f32[4,1024]{1,0:T(4,128)S(1)}, f32[4,1024]{1,0:T(4,128)S(1)}, u32[]{:S(2)}, u32[]{:S(2)}) collective-permute-start(f32[4,1024]{1,0:T(4,128)S(1)} %get-tuple-element.51), channel_id=1, source_target_pairs={{0,4},{1,2},{2,1},{3,7},{4,0},{5,6},{6,5},{7,3},{8,12},{9,10},{10,... | collective-permute-start | bytes 49160 | tf_op jit(solution)/shard_map/ppermute | solution.py:406

commit v4 on v2

--- a/solution.py
+++ b/solution.py
@@ -408,7 +408,7 @@
 
 def everyones(sketch):
     nx, ny = lax.axis_size("gx"), lax.axis_size("gy")
-    middle = nx // 2 - 1, ny // 2
+    middle = nx // 2 - 1, (ny - 1) // 2
     places = [(x, y) for x in range(nx) for y in range(ny)]
     places.sort(key=lambda at: (abs(at[1] - middle[1]), abs(at[0] - middle[0]), at))
     group = [x * ny + y for x, y in places]

time: 22.7 us -> 23.2 us (1.022)
  waiting for transfers between devices: 4.39 us -> 4.99 us
    all_to_all x1, waiting for transfers between devices: 0.35 us -> 1.23 us  [everyones(): return lax.all_to_all(copies, ('gx', 'gy'), 0, 0, axis_index_groups=[group])]
    all_to_all x1, starting transfers between devices: 4.8 us -> 4.37 us  [everyones(): return lax.all_to_all(copies, ('gx', 'gy'), 0, 0, axis_index_groups=[group])]
    ppermute x6, starting transfers between devices: 6.89 us -> 7.24 us  [swap(): return lax.ppermute(array, ('gx', 'gy'), pairs)]
    ppermute x6, waiting for transfers between devices: 4.04 us -> 3.76 us  [swap(): return lax.ppermute(array, ('gx', 'gy'), pairs)]
where the time goes in v4:
time: 23.2 us; the launch traced here: 23 us
  starting transfers between devices  11.6 us (50%)
  Pallas kernels  5.13 us (22%)
  waiting for transfers between devices  4.99 us (22%)
  between operations  0.66 us (3%)
  local copies, waits for them, and re-layouts  0.64 us (3%)
    ppermute x6, starting transfers between devices, swap(): return lax.ppermute(array, ('gx', 'gy'), pairs)  7.24 us
    pallas_call x5, Pallas kernels, call(): pl.pallas_call(kernel, out_shape=[shape if hasattr(shape, 'dtype') else j...  5.13 us
    all_to_all x1, starting transfers between devices, everyones(): return lax.all_to_all(copies, ('gx', 'gy'), 0, 0, axis_index_groups=[group])  4.37 us
    ppermute x6, waiting for transfers between devices, swap(): return lax.ppermute(array, ('gx', 'gy'), pairs)  3.76 us
    all_to_all x1, waiting for transfers between devices, everyones(): return lax.all_to_all(copies, ('gx', 'gy'), 0, 0, axis_index_groups=[group])  1.23 us
    broadcast_in_dim x1, local copies, waits for them, and re-layouts, everyones(): copies = jnp.broadcast_to(sketch[None], (nx * ny,) + sketch.shape)  0.64 us
  transfers between devices with their start and end apart: 7, of which 3 were waited for; matrix products, arithmetic and copies ran while one was open for 0% of the time, Pallas kernels for 7%

profile of v4, /device:TPU:0, one launch (start us, length us, event | category | flops | bytes accessed | tf_op | source)
XLA Modules:
  0.0 23.0 jit_solution(15101075861949786998)
XLA Ops:
  0.6 1.5 %shard_map.68 = (f32[4,8,1024]{2,1,0:T(8,128)S(1)}, f32[4,8,1024]{2,1,0:T(8,128)S(1)}, f32[4,8,1024]{2,1,0:T(8,128)S(1)}, f32[4,8,1024]{2,1,0:T(8,128)S(1)}, f32...) custom-call(f32[4,8,1024]{2,1,0:T(8,128)} %b_hbm.1, ...), custom_call_target="tpu_custom_call" | custom-call | tf_op jit(solution)/shard_map/pallas_call | solution.py:380
  2.1 3.1 %collective-permute-start = (f32[28,1024]{1,0:T(8,128)S(1)}, f32[28,1024]{1,0:T(8,128)S(1)}, u32[]{:S(2)}, u32[]{:S(2)}) collective-permute-start(f32[28,1024]{1,0:T(8,128)S(1)} %get-tuple-element.39), channel_id=1, source_target_pairs={{0,1},{1,0},{2,3},{3,2},{4,8},{5,9},{6,10},{7,11},{8,4},{9,5},{10,... | collective-permute-start | bytes 344072 | tf_op jit(solution)/shard_map/ppermute | solution.py:406
  5.2 0.1 collective-permute-start.1
  5.3 0.5 %collective-permute-start.2 = (f32[16,1024]{1,0:T(8,128)S(1)}, f32[16,1024]{1,0:T(8,128)S(1)}, u32[]{:S(2)}, u32[]{:S(2)}) collective-permute-start(f32[16,1024]{1,0:T(8,128)S(1)} %get-tuple-element.35.own_second_ref), channel_id=1, source_target_pairs={{0,4},{1,2},{2,1},{3,7},{4,0},{5,6},{6,5},{7,3},{8,12},{9,10},{10,... | collective-permute-start | bytes 196616 | tf_op jit(solution)/shard_map/ppermute | solution.py:406
  5.7 2.7 %collective-permute-start.3 = (f32[16,1024]{1,0:T(8,128)S(1)}, f32[16,1024]{1,0:T(8,128)S(1)}, u32[]{:S(2)}, u32[]{:S(2)}) collective-permute-start(f32[16,1024]{1,0:T(8,128)S(1)} %get-tuple-element.36.own_first_ref), channel_id=1, source_target_pairs={{0,1},{1,0},{2,3},{3,2},{4,5},{5,4},{6,7},{7,6},{8,9},{9,8},{10,11... | collective-permute-start | bytes 196616 | tf_op jit(solution)/shard_map/ppermute | solution.py:406
  8.4 0.9 %shard_map.69 = (bf16[1024,1024]{1,0:T(8,128)(2,1)S(1)}, bf16[512,1024]{1,0:T(8,128)(2,1)S(1)}, f32[2,128]{1,0:T(2,128)S(1)}) custom-call(f32[4,8,1024]{2,1,0:T(8,128)S(1)} %get-tuple-element.27.b_ref, f32[4,8,1024]{2,1,0:T(8,128)S(1)} %get-tuple-element.31.draw_ref, f32[4,8,1024]{2,1,0:T(8,128)S(1)} %get-tuple-element.32.slot_ref), custom_call_target="tpu_custom_call" | custom-call | flops 25165824 | tf_op jit(solution)/shard_map/pallas_call | solution.py:380
  9.3 0.0 collective-permute-done.got_second_ref.x_second_ref
  9.3 0.0 collective-permute-done.1.got_first_ref.x_first_ref
  9.3 0.6 %shard_map.70 = (f32[6,8,1024]{2,1,0:T(8,128)S(1)}, f32[5,8,1024]{2,1,0:T(8,128)S(1)}, f32[4,8,1024]{2,1,0:T(8,128)S(1)}, f32[16,32]{1,0:T(8,128)S(1)}) custom-call(f32[4,8,1024]{2,1,0:T(8,128)S(1)} %get-tuple-element.27.b_ref, f32[4,8,1024]{2,1,0:T(8,128)S(1)} %get-tuple-element.37.cond_ref, f32[4,8,1024]{2,1,0:T(8,128)S(1)} %get-tuple-element.28.cap_ref, ...), custom_call_target="tpu_custom_call" | custom-call | flops 25165824 | tf_op jit(solution)/shard_map/pallas_call | solution.py:380
  9.9 0.0 collective-permute-done.2.y_second_ref
  10.0 0.9 %collective-permute-done.3.y_first_ref = f32[16,1024]{1,0:T(8,128)S(1)} collective-permute-done((f32[16,1024]{1,0:T(8,128)S(1)}, f32[16,1024]{1,0:T(8,128)S(1)}, u32[]{:S(2)}, u32[]{:S(2)}) %collective-permute-start.3) | collective-permute-done | bytes 65568 | tf_op jit(solution)/shard_map/ppermute | solution.py:406
  10.8 1.0 %shard_map.71 = (f32[4,8,1024]{2,1,0:T(8,128)S(1)}, f32[4,8,1024]{2,1,0:T(8,128)S(1)}, f32[4,128]{1,0:T(4,128)S(1)}, f32[4,1024]{1,0:T(4,128)S(1)}, f32[4,1024]{1,0:T(4,128)S(1)}, /*index=5*/f32[24,1024]{1,0:T(8,128)S(1)}) custom-call(f32[4,8,1024]{2,1,0:T(8,128)S(1)} %get-tuple-element.27.b_ref, f32[4,8,1024]{2,1,0:T(8,128)S(1)} %get-tuple-element.28.cap_ref, ...), custom_call_target="tpu_custom_call" | custom-call | flops 25165824 | tf_op jit(solution)/shard_map/pallas_call | solution.py:380
  11.8 0.6 %broadcast_in_dim.2 = f32[16,4,128]{2,1,0:T(4,128)} broadcast(f32[4,128]{1,0:T(4,128)S(1)} %get-tuple-element.46), dimensions={1,2} | broadcast | bytes 34816 | tf_op jit(solution)/shard_map/broadcast_in_dim | solution.py:415
  12.5 4.4 %all-to-all-start = ((f32[16,4,128]{2,1,0:T(4,128)}), f32[16,4,128]{2,1,0:T(4,128)S(1)}, u32[]{:S(2)}, u32[]{:S(2)}) async-start(f32[16,4,128]{2,1,0:T(4,128)} %broadcast_in_dim.2), calls=%async_computation | async-start | bytes 65536 | tf_op jit(solution)/shard_map/all_to_all | solution.py:416
  16.9 0.9 %collective-permute-start.4 = (f32[4,1024]{1,0:T(4,128)S(1)}, f32[4,1024]{1,0:T(4,128)S(1)}, u32[]{:S(2)}, u32[]{:S(2)}) collective-permute-start(f32[4,1024]{1,0:T(4,128)S(1)} %get-tuple-element.50), channel_id=1, source_target_pairs={{0,1},{1,0},{2,3},{3,2},{4,5},{5,4},{6,7},{7,6},{8,9},{9,8},{10,11... | collective-permute-start | bytes 49160 | tf_op jit(solution)/shard_map/ppermute | solution.py:406
  17.8 0.0 collective-permute-start.5
  17.8 2.9 %collective-permute-done.4.corner_first_ref = f32[4,1024]{1,0:T(4,128)S(1)} collective-permute-done((f32[4,1024]{1,0:T(4,128)S(1)}, f32[4,1024]{1,0:T(4,128)S(1)}, u32[]{:S(2)}, u32[]{:S(2)}) %collective-permute-start.4) | collective-permute-done | bytes 16416 | tf_op jit(solution)/shard_map/ppermute | solution.py:406
  20.7 0.0 collective-permute-done.5.corner_second_ref
  20.7 1.2 %all-to-all-done.sketch_ref = f32[16,4,128]{2,1,0:T(4,128)S(1)} async-done(((f32[16,4,128]{2,1,0:T(4,128)}), f32[16,4,128]{2,1,0:T(4,128)S(1)}, u32[]{:S(2)}, u32[]{:S(2)}) %all-to-all-start) | async-done | bytes 32800 | tf_op jit(solution)/shard_map/all_to_all | solution.py:416
  21.9 1.1 %shard_map.72 = (f32[4,8,1024]{2,1,0:T(8,128)}, f32[4,8,1024]{2,1,0:T(8,128)}) custom-call(f32[16,4,128]{2,1,0:T(4,128)S(1)} %all-to-all-done.sketch_ref, f32[4,8,1024]{2,1,0:T(8,128)S(1)} %get-tuple-element.27.b_ref, f32[4,8,1024]{2,1,0:T(8,128)S(1)} %get-tuple-element.47.image_ref, f32[4,8,1024]{2,1,0:T(8,128)S(1)} %get-tuple-element.48.twice_ref, ...), custom_call_target="tpu_custom_call" | custom-call | tf_op jit(solution)/shard_map/pallas_call | solution.py:380
Async XLA Ops:
  2.1 7.2 %collective-permute-start = (f32[28,1024]{1,0:T(8,128)S(1)}, f32[28,1024]{1,0:T(8,128)S(1)}, u32[]{:S(2)}, u32[]{:S(2)}) collective-permute-start(f32[28,1024]{1,0:T(8,128)S(1)} %get-tuple-element.39), channel_id=1, source_target_pairs={{0,1},{1,0},{2,3},{3,2},{4,8},{5,9},{6,10},{7,11},{8,4},{9,5},{10,... | collective-permute-start | bytes 344072 | tf_op jit(solution)/shard_map/ppermute | solution.py:406
  5.2 4.1 %collective-permute-start.1 = (f32[28,1024]{1,0:T(8,128)S(1)}, f32[28,1024]{1,0:T(8,128)S(1)}, u32[]{:S(2)}, u32[]{:S(2)}) collective-permute-start(f32[28,1024]{1,0:T(8,128)S(1)} %get-tuple-element.40), channel_id=1, source_target_pairs={{0,4},{1,5},{2,6},{3,7},{4,0},{5,1},{6,2},{7,3},{8,12},{9,13},{10,... | collective-permute-start | bytes 344072 | tf_op jit(solution)/shard_map/ppermute | solution.py:406
  5.3 4.7 %collective-permute-start.2 = (f32[16,1024]{1,0:T(8,128)S(1)}, f32[16,1024]{1,0:T(8,128)S(1)}, u32[]{:S(2)}, u32[]{:S(2)}) collective-permute-start(f32[16,1024]{1,0:T(8,128)S(1)} %get-tuple-element.35.own_second_ref), channel_id=1, source_target_pairs={{0,4},{1,2},{2,1},{3,7},{4,0},{5,6},{6,5},{7,3},{8,12},{9,10},{10,... | collective-permute-start | bytes 196616 | tf_op jit(solution)/shard_map/ppermute | solution.py:406
  5.7 5.1 %collective-permute-start.3 = (f32[16,1024]{1,0:T(8,128)S(1)}, f32[16,1024]{1,0:T(8,128)S(1)}, u32[]{:S(2)}, u32[]{:S(2)}) collective-permute-start(f32[16,1024]{1,0:T(8,128)S(1)} %get-tuple-element.36.own_first_ref), channel_id=1, source_target_pairs={{0,1},{1,0},{2,3},{3,2},{4,5},{5,4},{6,7},{7,6},{8,9},{9,8},{10,11... | collective-permute-start | bytes 196616 | tf_op jit(solution)/shard_map/ppermute | solution.py:406
  12.5 9.4 %all-to-all-start = ((f32[16,4,128]{2,1,0:T(4,128)}), f32[16,4,128]{2,1,0:T(4,128)S(1)}, u32[]{:S(2)}, u32[]{:S(2)}) async-start(f32[16,4,128]{2,1,0:T(4,128)} %broadcast_in_dim.2), calls=%async_computation | async-start | bytes 65536 | tf_op jit(solution)/shard_map/all_to_all | solution.py:416
  16.9 3.8 %collective-permute-start.4 = (f32[4,1024]{1,0:T(4,128)S(1)}, f32[4,1024]{1,0:T(4,128)S(1)}, u32[]{:S(2)}, u32[]{:S(2)}) collective-permute-start(f32[4,1024]{1,0:T(4,128)S(1)} %get-tuple-element.50), channel_id=1, source_target_pairs={{0,1},{1,0},{2,3},{3,2},{4,5},{5,4},{6,7},{7,6},{8,9},{9,8},{10,11... | collective-permute-start | bytes 49160 | tf_op jit(solution)/shard_map/ppermute | solution.py:406
  17.8 2.9 %collective-permute-start.5 = (f32[4,1024]{1,0:T(4,128)S(1)}, f32[4,1024]{1,0:T(4,128)S(1)}, u32[]{:S(2)}, u32[]{:S(2)}) collective-permute-start(f32[4,1024]{1,0:T(4,128)S(1)} %get-tuple-element.51), channel_id=1, source_target_pairs={{0,4},{1,2},{2,1},{3,7},{4,0},{5,6},{6,5},{7,3},{8,12},{9,10},{10,... | collective-permute-start | bytes 49160 | tf_op jit(solution)/shard_map/ppermute | solution.py:406

commit v5 on v2

--- a/solution.py
+++ b/solution.py
@@ -256,8 +256,8 @@
 def third_kernel(
     b_ref, cap_ref, y_link_ref, z_link_ref, draw_ref, low_ref, high_ref, own_second_ref,
     own_first_ref, wide_ref, x_link_ref, beside_ref, x_second_ref, x_first_ref, y_second_ref,
-    y_first_ref, b_sketch_ref, inside_ref, image_ref, twice_ref, sketch_ref, corner_first_ref,
-    corner_second_ref, ends_ref, cells_ref, extra_ref,
+    y_first_ref, b_sketch_ref, inside_ref, image_ref, twice_ref, sketch_hbm, corner_first_ref,
+    corner_second_ref, ends_ref, cells_ref, extra_ref, copies_ref, sent,
 ):
     planes, rows, depth = b_ref.shape
     index = lax.broadcasted_iota(jnp.int32, (rows, depth), 0)
@@ -271,7 +271,7 @@
     x_tails = by_turn(x_first_ref[3 * rows :], x_second_ref[3 * rows :], "gx")
     own_lines = by_turn(own_first_ref[...], own_second_ref[...], "gy")
     y_lines = by_turn(y_first_ref[...], y_second_ref[...], "gy")
-    beside = []
+    beside, ends = [], []
     for side, (j, here, own, line) in enumerate(
         zip((0, rows - 1), has_beside("gy"), own_lines, y_lines)
     ):
@@ -295,11 +295,9 @@
             values = -y_link[line_at] * x_flow[row], tail[end:][:1], tail[2 + end :][:1]
             for k, value in enumerate(values):
                 extra_ref[k, at + 1 : at + 2] = value
-            at = 6 * (2 * side + end)
             values = x_link[row], b_beside[end][row], c_beside[end][row]
             values += y_link[line_at], b_line[line_at], c_line[line_at]
-            for k, value in enumerate(values):
-                ends_ref[at + k : at + k + 1] = value
+            ends.append(values)
     links = [(y_link_ref[i], z_link_ref[i]) for i in range(planes)]
     twice = apply_inside(images, x_links, links, [cap_ref[i] for i in range(planes)])
     for i, conductance, value in beside:
@@ -318,14 +316,21 @@
         mask = one_hot(high, j, HIGH, 2 * PAIR)
         left.append(masked_cells(mask, start, j, cells_ref))
         right.append(one_hot(low, j, LOW, 1))
-    sketch_ref[1 : 1 + PAIR] = as_sketch(total + product(left, right))
-    sketch_ref[:1] = b_sketch_ref[:1]
-    sketch_ref[1 + PAIR :] = b_sketch_ref[:1]
+    sketch = as_sketch(total + product(left, right))
+    for device in range(copies_ref.shape[0]):
+        copies_ref[device, 1 : 1 + PAIR] = sketch
+        copies_ref[device, :1] = b_sketch_ref[:1]
+        copies_ref[device, 1 + PAIR :] = b_sketch_ref[:1]
+    copy = pltpu.make_async_copy(copies_ref, sketch_hbm, sent)
+    copy.start()
+    for at, value in enumerate(sum(ends, ())):
+        ends_ref[at : at + 1] = value
     for k, plane in enumerate(b_beside + c_beside):
         at = slice(k, k + 1)
         corner_first_ref[at], corner_second_ref[at] = by_turn(
             plane[:1], plane[rows - 1 :], "gy"
         )
+    copy.wait()
 
 
 def last_kernel(
@@ -376,7 +381,7 @@
             residual_ref[i, j : j + 1] = residual_ref[i, j : j + 1] + c1 * lacked
 
 
-def call(kernel, shapes, *operands, scratch=(), inputs=pltpu.VMEM, flops=0):
+def call(kernel, shapes, *operands, scratch=(), inputs=pltpu.VMEM, in_hbm=(), flops=0):
     return pl.pallas_call(
         kernel,
         out_shape=[
@@ -384,7 +389,10 @@
             for shape in shapes
         ],
         in_specs=[pl.BlockSpec(memory_space=inputs)] * len(operands),
-        out_specs=[pl.BlockSpec(memory_space=pltpu.VMEM)] * len(shapes),
+        out_specs=[
+            pl.BlockSpec(memory_space=pltpu.HBM if k in in_hbm else pltpu.VMEM)
+            for k in range(len(shapes))
+        ],
         scratch_shapes=scratch,
         compiler_params=pltpu.CompilerParams(vmem_limit_bytes=48 * 1024 * 1024),
         cost_estimate=pl.CostEstimate(flops=flops, bytes_accessed=0, transcendentals=0),
@@ -406,13 +414,12 @@
     return lax.ppermute(array, ("gx", "gy"), pairs)
 
 
-def everyones(sketch):
+def everyones(copies):
     nx, ny = lax.axis_size("gx"), lax.axis_size("gy")
     middle = nx // 2 - 1, ny // 2
     places = [(x, y) for x in range(nx) for y in range(ny)]
     places.sort(key=lambda at: (abs(at[1] - middle[1]), abs(at[0] - middle[0]), at))
     group = [x * ny + y for x, y in places]
-    copies = jnp.broadcast_to(sketch[None], (nx * ny,) + sketch.shape)
     return lax.all_to_all(copies, ("gx", "gy"), 0, 0, axis_index_groups=[group])
 
 
@@ -454,16 +461,23 @@
         scratch=[cells],
         flops=work,
     )
-    image, twice, sketch, first, second, ends = call(
+    copies = lax.axis_size("gx") * lax.axis_size("gy"), FIELDS + 1, SKETCH
+    image, twice, copies, first, second, ends = call(
         third_kernel,
-        [block, block, (FIELDS + 1, SKETCH), corner, corner, (24, depth)],
+        [block, block, copies, corner, corner, (24, depth)],
         b, cap, y_link, z_link, draw, *hots, y_second, y_first, image_wide, x_link, beside,
         *got_x, *got_y, b_sketch, inside,
-        scratch=[cells, pltpu.VMEM((3, 8, depth), jnp.float32)],
+        scratch=[
+            cells,
+            pltpu.VMEM((3, 8, depth), jnp.float32),
+            pltpu.VMEM(copies, jnp.float32),
+            pltpu.SemaphoreType.DMA,
+        ],
+        in_hbm=(2,),
         flops=work,
     )
     got_corners = [swap(array, "gy", turn) for turn, array in enumerate((first, second))]
-    sketches = everyones(sketch)
+    sketches = everyones(copies)
     return tuple(
         call(last_kernel, [block, block], sketches, b, image, twice, ends, *got_corners)
     )

time: 22.7 us -> 22.8 us (level)
  Pallas kernels: 5.13 us -> 5.84 us
  local copies, waits for them, and re-layouts: 0.64 us -> 0 us
    pallas_call x5, Pallas kernels: 5.13 us -> 5.84 us  [call(): pl.pallas_call(kernel, out_shape=[shape if hasattr(shape, 'dtype') else j...]
    broadcast_in_dim x1 -> x0, local copies, waits for them, and re-layouts: 0.64 us -> none  [everyones(): copies = jnp.broadcast_to(sketch[None], (nx * ny,) + sketch.shape)]
where the time goes in v5:
time: 22.8 us; the launch traced here: 22.6 us
  starting transfers between devices  11.7 us (51%)
  Pallas kernels  5.84 us (26%)
  waiting for transfers between devices  4.35 us (19%)
  between operations  0.66 us (3%)
    ppermute x6, starting transfers between devices, swap(): return lax.ppermute(array, ('gx', 'gy'), pairs)  6.89 us
    pallas_call x5, Pallas kernels, call(): pl.pallas_call(kernel, out_shape=[shape if hasattr(shape, 'dtype') else j...  5.84 us
    all_to_all x1, starting transfers between devices, everyones(): return lax.all_to_all(copies, ('gx', 'gy'), 0, 0, axis_index_groups=[group])  4.81 us
    ppermute x6, waiting for transfers between devices, swap(): return lax.ppermute(array, ('gx', 'gy'), pairs)  4 us
  transfers between devices with their start and end apart: 7, of which 3 were waited for; matrix products, arithmetic and copies ran while one was open for 0% of the time, Pallas kernels for 7%

profile of v5, /device:TPU:0, one launch (start us, length us, event | category | flops | bytes accessed | tf_op | source)
XLA Modules:
  0.0 22.6 jit_solution(18172079380246162391)
XLA Ops:
  0.6 1.5 %shard_map.68 = (f32[4,8,1024]{2,1,0:T(8,128)S(1)}, f32[4,8,1024]{2,1,0:T(8,128)S(1)}, f32[4,8,1024]{2,1,0:T(8,128)S(1)}, f32[4,8,1024]{2,1,0:T(8,128)S(1)}, f32...) custom-call(f32[4,8,1024]{2,1,0:T(8,128)} %b_hbm.1, ...), custom_call_target="tpu_custom_call" | custom-call | tf_op jit(solution)/shard_map/pallas_call | solution.py:385
  2.1 3.1 %collective-permute-start = (f32[28,1024]{1,0:T(8,128)S(1)}, f32[28,1024]{1,0:T(8,128)S(1)}, u32[]{:S(2)}, u32[]{:S(2)}) collective-permute-start(f32[28,1024]{1,0:T(8,128)S(1)} %get-tuple-element.39), channel_id=1, source_target_pairs={{0,1},{1,0},{2,3},{3,2},{4,8},{5,9},{6,10},{7,11},{8,4},{9,5},{10,... | collective-permute-start | bytes 344072 | tf_op jit(solution)/shard_map/ppermute | solution.py:414
  5.2 0.1 collective-permute-start.1
  5.3 0.5 %collective-permute-start.2 = (f32[16,1024]{1,0:T(8,128)S(1)}, f32[16,1024]{1,0:T(8,128)S(1)}, u32[]{:S(2)}, u32[]{:S(2)}) collective-permute-start(f32[16,1024]{1,0:T(8,128)S(1)} %get-tuple-element.35.own_second_ref), channel_id=1, source_target_pairs={{0,4},{1,2},{2,1},{3,7},{4,0},{5,6},{6,5},{7,3},{8,12},{9,10},{10,... | collective-permute-start | bytes 196616 | tf_op jit(solution)/shard_map/ppermute | solution.py:414
  5.7 2.7 %collective-permute-start.3 = (f32[16,1024]{1,0:T(8,128)S(1)}, f32[16,1024]{1,0:T(8,128)S(1)}, u32[]{:S(2)}, u32[]{:S(2)}) collective-permute-start(f32[16,1024]{1,0:T(8,128)S(1)} %get-tuple-element.36.own_first_ref), channel_id=1, source_target_pairs={{0,1},{1,0},{2,3},{3,2},{4,5},{5,4},{6,7},{7,6},{8,9},{9,8},{10,11... | collective-permute-start | bytes 196616 | tf_op jit(solution)/shard_map/ppermute | solution.py:414
  8.4 0.9 %shard_map.69 = (bf16[1024,1024]{1,0:T(8,128)(2,1)S(1)}, bf16[512,1024]{1,0:T(8,128)(2,1)S(1)}, f32[2,128]{1,0:T(2,128)S(1)}) custom-call(f32[4,8,1024]{2,1,0:T(8,128)S(1)} %get-tuple-element.27.b_ref, f32[4,8,1024]{2,1,0:T(8,128)S(1)} %get-tuple-element.31.draw_ref, f32[4,8,1024]{2,1,0:T(8,128)S(1)} %get-tuple-element.32.slot_ref), custom_call_target="tpu_custom_call" | custom-call | flops 25165824 | tf_op jit(solution)/shard_map/pallas_call | solution.py:385
  9.3 0.0 collective-permute-done.got_second_ref.x_second_ref
  9.3 0.0 collective-permute-done.1.got_first_ref.x_first_ref
  9.3 0.7 %shard_map.70 = (f32[6,8,1024]{2,1,0:T(8,128)S(1)}, f32[5,8,1024]{2,1,0:T(8,128)S(1)}, f32[4,8,1024]{2,1,0:T(8,128)S(1)}, f32[16,32]{1,0:T(8,128)S(1)}) custom-call(f32[4,8,1024]{2,1,0:T(8,128)S(1)} %get-tuple-element.27.b_ref, f32[4,8,1024]{2,1,0:T(8,128)S(1)} %get-tuple-element.37.cond_ref, f32[4,8,1024]{2,1,0:T(8,128)S(1)} %get-tuple-element.28.cap_ref, ...), custom_call_target="tpu_custom_call" | custom-call | flops 25165824 | tf_op jit(solution)/shard_map/pallas_call | solution.py:385
  10.0 0.0 collective-permute-done.2.y_second_ref
  10.0 0.8 %collective-permute-done.3.y_first_ref = f32[16,1024]{1,0:T(8,128)S(1)} collective-permute-done((f32[16,1024]{1,0:T(8,128)S(1)}, f32[16,1024]{1,0:T(8,128)S(1)}, u32[]{:S(2)}, u32[]{:S(2)}) %collective-permute-start.3) | collective-permute-done | bytes 65568 | tf_op jit(solution)/shard_map/ppermute | solution.py:414
  10.8 1.7 %shard_map.71 = (f32[4,8,1024]{2,1,0:T(8,128)S(1)}, f32[4,8,1024]{2,1,0:T(8,128)S(1)}, f32[16,4,128]{2,1,0:T(4,128)}, f32[4,1024]{1,0:T(4,128)S(1)}, f32[4,1024]{1,0:T(4,128)S(1)}, /*index=5*/f32[24,1024]{1,0:T(8,128)S(1)}) custom-call(f32[4,8,1024]{2,1,0:T(8,128)S(1)} %get-tuple-element.27.b_ref, f32[4,8,1024]{2,1,0:T(8,128)S(1)} %get-tuple-element.28.cap_ref, ...), custom_call_target="tpu_custom_call" | custom-call | flops 25165824 | tf_op jit(solution)/shard_map/pallas_call | solution.py:385
  12.5 4.8 %all-to-all-start = ((f32[16,4,128]{2,1,0:T(4,128)}), f32[16,4,128]{2,1,0:T(4,128)S(1)}, u32[]{:S(2)}, u32[]{:S(2)}) async-start(f32[16,4,128]{2,1,0:T(4,128)} %get-tuple-element.46), calls=%async_computation | async-start | bytes 65536 | tf_op jit(solution)/shard_map/all_to_all | solution.py:423
  17.3 0.6 %collective-permute-start.4 = (f32[4,1024]{1,0:T(4,128)S(1)}, f32[4,1024]{1,0:T(4,128)S(1)}, u32[]{:S(2)}, u32[]{:S(2)}) collective-permute-start(f32[4,1024]{1,0:T(4,128)S(1)} %get-tuple-element.50), channel_id=1, source_target_pairs={{0,1},{1,0},{2,3},{3,2},{4,5},{5,4},{6,7},{7,6},{8,9},{9,8},{10,11... | collective-permute-start | bytes 49160 | tf_op jit(solution)/shard_map/ppermute | solution.py:414
  17.9 0.0 collective-permute-start.5
  17.9 3.1 %collective-permute-done.4.corner_first_ref = f32[4,1024]{1,0:T(4,128)S(1)} collective-permute-done((f32[4,1024]{1,0:T(4,128)S(1)}, f32[4,1024]{1,0:T(4,128)S(1)}, u32[]{:S(2)}, u32[]{:S(2)}) %collective-permute-start.4) | collective-permute-done | bytes 16416 | tf_op jit(solution)/shard_map/ppermute | solution.py:414
  21.1 0.0 collective-permute-done.5.corner_second_ref
  21.1 0.3 %all-to-all-done.sketch_ref = f32[16,4,128]{2,1,0:T(4,128)S(1)} async-done(((f32[16,4,128]{2,1,0:T(4,128)}), f32[16,4,128]{2,1,0:T(4,128)S(1)}, u32[]{:S(2)}, u32[]{:S(2)}) %all-to-all-start) | async-done | bytes 32800 | tf_op jit(solution)/shard_map/all_to_all | solution.py:423
  21.4 1.1 %shard_map.72 = (f32[4,8,1024]{2,1,0:T(8,128)}, f32[4,8,1024]{2,1,0:T(8,128)}) custom-call(f32[16,4,128]{2,1,0:T(4,128)S(1)} %all-to-all-done.sketch_ref, f32[4,8,1024]{2,1,0:T(8,128)S(1)} %get-tuple-element.27.b_ref, f32[4,8,1024]{2,1,0:T(8,128)S(1)} %get-tuple-element.47.image_ref, f32[4,8,1024]{2,1,0:T(8,128)S(1)} %get-tuple-element.48.twice_ref, ...), custom_call_target="tpu_custom_call" | custom-call | tf_op jit(solution)/shard_map/pallas_call | solution.py:385
Async XLA Ops:
  2.1 7.2 %collective-permute-start = (f32[28,1024]{1,0:T(8,128)S(1)}, f32[28,1024]{1,0:T(8,128)S(1)}, u32[]{:S(2)}, u32[]{:S(2)}) collective-permute-start(f32[28,1024]{1,0:T(8,128)S(1)} %get-tuple-element.39), channel_id=1, source_target_pairs={{0,1},{1,0},{2,3},{3,2},{4,8},{5,9},{6,10},{7,11},{8,4},{9,5},{10,... | collective-permute-start | bytes 344072 | tf_op jit(solution)/shard_map/ppermute | solution.py:414
  5.2 4.1 %collective-permute-start.1 = (f32[28,1024]{1,0:T(8,128)S(1)}, f32[28,1024]{1,0:T(8,128)S(1)}, u32[]{:S(2)}, u32[]{:S(2)}) collective-permute-start(f32[28,1024]{1,0:T(8,128)S(1)} %get-tuple-element.40), channel_id=1, source_target_pairs={{0,4},{1,5},{2,6},{3,7},{4,0},{5,1},{6,2},{7,3},{8,12},{9,13},{10,... | collective-permute-start | bytes 344072 | tf_op jit(solution)/shard_map/ppermute | solution.py:414
  5.3 4.7 %collective-permute-start.2 = (f32[16,1024]{1,0:T(8,128)S(1)}, f32[16,1024]{1,0:T(8,128)S(1)}, u32[]{:S(2)}, u32[]{:S(2)}) collective-permute-start(f32[16,1024]{1,0:T(8,128)S(1)} %get-tuple-element.35.own_second_ref), channel_id=1, source_target_pairs={{0,4},{1,2},{2,1},{3,7},{4,0},{5,6},{6,5},{7,3},{8,12},{9,10},{10,... | collective-permute-start | bytes 196616 | tf_op jit(solution)/shard_map/ppermute | solution.py:414
  5.7 5.1 %collective-permute-start.3 = (f32[16,1024]{1,0:T(8,128)S(1)}, f32[16,1024]{1,0:T(8,128)S(1)}, u32[]{:S(2)}, u32[]{:S(2)}) collective-permute-start(f32[16,1024]{1,0:T(8,128)S(1)} %get-tuple-element.36.own_first_ref), channel_id=1, source_target_pairs={{0,1},{1,0},{2,3},{3,2},{4,5},{5,4},{6,7},{7,6},{8,9},{9,8},{10,11... | collective-permute-start | bytes 196616 | tf_op jit(solution)/shard_map/ppermute | solution.py:414
  12.5 8.9 %all-to-all-start = ((f32[16,4,128]{2,1,0:T(4,128)}), f32[16,4,128]{2,1,0:T(4,128)S(1)}, u32[]{:S(2)}, u32[]{:S(2)}) async-start(f32[16,4,128]{2,1,0:T(4,128)} %get-tuple-element.46), calls=%async_computation | async-start | bytes 65536 | tf_op jit(solution)/shard_map/all_to_all | solution.py:423
  17.3 3.7 %collective-permute-start.4 = (f32[4,1024]{1,0:T(4,128)S(1)}, f32[4,1024]{1,0:T(4,128)S(1)}, u32[]{:S(2)}, u32[]{:S(2)}) collective-permute-start(f32[4,1024]{1,0:T(4,128)S(1)} %get-tuple-element.50), channel_id=1, source_target_pairs={{0,1},{1,0},{2,3},{3,2},{4,5},{5,4},{6,7},{7,6},{8,9},{9,8},{10,11... | collective-permute-start | bytes 49160 | tf_op jit(solution)/shard_map/ppermute | solution.py:414
  17.9 3.2 %collective-permute-start.5 = (f32[4,1024]{1,0:T(4,128)S(1)}, f32[4,1024]{1,0:T(4,128)S(1)}, u32[]{:S(2)}, u32[]{:S(2)}) collective-permute-start(f32[4,1024]{1,0:T(4,128)S(1)} %get-tuple-element.51), channel_id=1, source_target_pairs={{0,4},{1,2},{2,1},{3,7},{4,0},{5,6},{6,5},{7,3},{8,12},{9,10},{10,... | collective-permute-start | bytes 49160 | tf_op jit(solution)/shard_map/ppermute | solution.py:414

commit v6 on v2

--- a/solution.py
+++ b/solution.py
@@ -89,7 +89,7 @@
 
 
 def masked_cells(mask, start, j, cells_ref):
-    at = pl.ds(start + j * 8, 8)
+    at = pl.ds(pl.multiple_of(start + j * 8, 8), 8)
     cells = jnp.concatenate([cells_ref[t, at, :] for t in range(cells_ref.shape[0])], axis=1)
     return jnp.concatenate([cells, cells], axis=0).astype(jnp.bfloat16) * mask
 
@@ -119,9 +119,9 @@
         left, right = [], []
         for j in chosen:
             at = i * rows + j
-            mask = high_ref[at * each : (at + 1) * each]
+            mask = high_ref[pl.ds(pl.multiple_of(at * each, each), each)]
             left.append(masked_cells(mask, start, j, cells_ref))
-            right.append(low_ref[at * LOW : (at + 1) * LOW])
+            right.append(low_ref[pl.ds(pl.multiple_of(at * LOW, LOW), LOW)])
         total = total + product(left, right)
     return total
 
@@ -253,84 +253,137 @@
     sketch_ref[...] = sketch_rows(cells, low_ref, high_ref, cells_ref)
 
 
-def third_kernel(
-    b_ref, cap_ref, y_link_ref, z_link_ref, draw_ref, low_ref, high_ref, own_second_ref,
-    own_first_ref, wide_ref, x_link_ref, beside_ref, x_second_ref, x_first_ref, y_second_ref,
-    y_first_ref, b_sketch_ref, inside_ref, image_ref, twice_ref, sketch_ref, corner_first_ref,
-    corner_second_ref, ends_ref, cells_ref, extra_ref,
+def side_of(turn):
+    is_low = (lax.axis_index("gy") + turn) % 2 == 1
+    below, above = has_beside("gy")
+    return is_low, jnp.where(is_low, below, above)
+
+
+def at_row(plane, is_low):
+    return jnp.where(is_low, plane[:1], plane[plane.shape[0] - 1 :])
+
+
+def add_side(
+    turn, images, b_ref, x_links, beside_ref, own_ref, line_ref, x_first_ref, x_second_ref,
+    extra_ref, ends_ref,
 ):
     planes, rows, depth = b_ref.shape
+    is_low, here = side_of(turn)
     index = lax.broadcasted_iota(jnp.int32, (rows, depth), 0)
-    images = [wide_ref[i] for i in range(planes + 2)]
-    x_links = [x_link_ref[i] for i in range(planes + 1)]
-    b_beside, c_beside = (beside_ref[0], beside_ref[1]), (beside_ref[2], beside_ref[3])
-    x_ends = []
-    for end, i in enumerate((0, planes - 1)):
-        conductance = x_links[-end]
-        x_ends.append((i, conductance, conductance * (b_ref[i] - b_beside[end])))
-    x_tails = by_turn(x_first_ref[3 * rows :], x_second_ref[3 * rows :], "gx")
-    own_lines = by_turn(own_first_ref[...], own_second_ref[...], "gy")
-    y_lines = by_turn(y_first_ref[...], y_second_ref[...], "gy")
-    beside = []
-    for side, (j, here, own, line) in enumerate(
-        zip((0, rows - 1), has_beside("gy"), own_lines, y_lines)
-    ):
-        row = slice(j, j + 1)
-        beyond, b_line, c_line = (line[k * planes : (k + 1) * planes] for k in range(3))
-        c_line = jnp.where(here, c_line, 0.0)
-        y_link = link(own[2 * planes : 3 * planes], c_line)
-        y_flow = y_link * (own[planes : 2 * planes] - b_line)
-        beyond = beyond - y_flow
-        for i in range(planes):
-            at = slice(i, i + 1)
-            images[i + 1] = images[i + 1] + jnp.where(index == j, y_flow[at], 0.0)
-            beside.append((i, jnp.where(index == j, y_link[at], 0.0), beyond[at]))
-        for end, (i, x_link, x_flow) in enumerate(x_ends):
-            line_at, at = slice(i, i + 1), 4 * side + 2 * end
-            tail = x_tails[end]
-            values = -x_link[row] * y_flow[line_at], tail[side:][:1], tail[2 + side :][:1]
-            for k, value in enumerate(values):
-                extra_ref[k, at : at + 1] = value
-            tail = line[3 * planes :]
-            values = -y_link[line_at] * x_flow[row], tail[end:][:1], tail[2 + end :][:1]
-            for k, value in enumerate(values):
-                extra_ref[k, at + 1 : at + 2] = value
-            at = 6 * (2 * side + end)
-            values = x_link[row], b_beside[end][row], c_beside[end][row]
-            values += y_link[line_at], b_line[line_at], c_line[line_at]
-            for k, value in enumerate(values):
-                ends_ref[at + k : at + k + 1] = value
-    links = [(y_link_ref[i], z_link_ref[i]) for i in range(planes)]
-    twice = apply_inside(images, x_links, links, [cap_ref[i] for i in range(planes)])
-    for i, conductance, value in beside:
-        twice[i] = twice[i] + conductance * (images[i + 1] - value)
-    for i in range(planes):
-        image_ref[i] = images[i + 1]
-        twice_ref[i] = twice[i]
-    chosen = reached(rows)[0]
-    cells = [((images[i + 1], twice[i]), draw_ref[i], chosen) for i in range(planes)]
-    total = inside_ref[...] + sketch_rows(cells, low_ref, high_ref, cells_ref)
+    edge = index == jnp.where(is_low, 0, rows - 1)
+    beyond, b_line, c_line = (line_ref[k * planes : (k + 1) * planes] for k in range(3))
+    c_line = jnp.where(here, c_line, 0.0)
+    y_link = link(own_ref[2 * planes : 3 * planes], c_line)
+    y_flow = y_link * (own_ref[planes : 2 * planes] - b_line)
+    for i in range(planes):
+        images[i + 1] = images[i + 1] + jnp.where(edge, y_flow[i : i + 1], 0.0)
+    tails = by_turn(x_first_ref[3 * rows :], x_second_ref[3 * rows :], "gx")
+    for end, (i, tail) in enumerate(zip((0, planes - 1), tails)):
+        at = slice(i, i + 1)
+        x_link = at_row(x_links[-end], is_low)
+        x_b, x_cond = at_row(beside_ref[end], is_low), at_row(beside_ref[2 + end], is_low)
+        x_flow = x_link * (at_row(b_ref[i], is_low) - x_b)
+        values = -x_link * y_flow[at], at_row(tail[:2], is_low), at_row(tail[2:], is_low)
+        for k, value in enumerate(values):
+            extra_ref[k, 2 * end : 2 * end + 1] = value
+        tail = line_ref[3 * planes :]
+        values = -y_link[at] * x_flow, tail[end:][:1], tail[2 + end :][:1]
+        for k, value in enumerate(values):
+            extra_ref[k, 2 * end + 1 : 2 * end + 2] = value
+        values = x_link, x_b, x_cond, y_link[at], b_line[at], c_line[at]
+        for k, value in enumerate(values):
+            ends_ref[6 * end + k : 6 * end + k + 1] = value
+    return y_link, beyond - y_flow
+
+
+def add_beside(turn, twice, images, y_link, beyond):
+    rows, depth = twice[0].shape
+    is_low, unused = side_of(turn)
+    index = lax.broadcasted_iota(jnp.int32, (rows, depth), 0)
+    edge = index == jnp.where(is_low, 0, rows - 1)
+    for i in range(len(twice)):
+        at = slice(i, i + 1)
+        conductance = jnp.where(edge, y_link[at], 0.0)
+        twice[i] = twice[i] + conductance * (images[i + 1] - beyond[at])
+
+
+def side_sketch(turn, images, twice, draw_ref, low_ref, high_ref, cells_ref, extra_ref):
+    planes, rows, depth = draw_ref.shape
+    is_low, unused = side_of(turn)
+    first = jnp.where(is_low, 0, rows - 2)
+    cells = [((images[i + 1], twice[i]), draw_ref[i], (first, first + 1)) for i in range(planes)]
+    total = sketch_rows(cells, low_ref, high_ref, cells_ref)
     start = planes * rows * 8
-    put_cells((jnp.zeros((8, depth), jnp.float32), extra_ref[0]), extra_ref[1], start, cells_ref)
+    nothing = jnp.zeros(extra_ref.shape[1:], jnp.float32)
+    put_cells((nothing, extra_ref[0]), extra_ref[1], start, cells_ref)
     low, high = parts_of(extra_ref[2])
     left, right = [], []
-    for j in range(8):
+    for j in range(extra_ref.shape[1]):
         mask = one_hot(high, j, HIGH, 2 * PAIR)
         left.append(masked_cells(mask, start, j, cells_ref))
         right.append(one_hot(low, j, LOW, 1))
-    sketch_ref[1 : 1 + PAIR] = as_sketch(total + product(left, right))
+    return total + product(left, right)
+
+
+def third_kernel(
+    b_ref, cap_ref, y_link_ref, z_link_ref, draw_ref, low_ref, high_ref, own_ref, wide_ref,
+    x_link_ref, beside_ref, x_second_ref, x_first_ref, line_ref, inside_ref, more_ref, edge_ref,
+    ends_ref, sketch_ref, cells_ref, extra_ref,
+):
+    planes = b_ref.shape[0]
+    images = [wide_ref[i] for i in range(planes + 2)]
+    x_links = [x_link_ref[i] for i in range(planes + 1)]
+    y_link, beyond = add_side(
+        1, images, b_ref, x_links, beside_ref, own_ref, line_ref, x_first_ref, x_second_ref,
+        extra_ref, ends_ref,
+    )
+    edge_ref[0], edge_ref[1] = y_link, beyond
+    links = [(y_link_ref[i], z_link_ref[i]) for i in range(planes)]
+    twice = apply_inside(images, x_links, links, [cap_ref[i] for i in range(planes)])
+    add_beside(1, twice, images, y_link, beyond)
+    for i, image in enumerate(images):
+        more_ref[i] = image
+    sketch_ref[...] = inside_ref[...] + side_sketch(
+        1, images, twice, draw_ref, low_ref, high_ref, cells_ref, extra_ref
+    )
+
+
+def fourth_kernel(
+    b_ref, cap_ref, y_link_ref, z_link_ref, draw_ref, low_ref, high_ref, own_ref, more_ref,
+    x_link_ref, beside_ref, x_second_ref, x_first_ref, line_ref, edge_ref, b_sketch_ref,
+    others_ref, image_ref, twice_ref, sketch_ref, corner_first_ref, corner_second_ref, ends_ref,
+    cells_ref, extra_ref,
+):
+    planes, rows, depth = b_ref.shape
+    images = [more_ref[i] for i in range(planes + 2)]
+    x_links = [x_link_ref[i] for i in range(planes + 1)]
+    y_link, beyond = add_side(
+        0, images, b_ref, x_links, beside_ref, own_ref, line_ref, x_first_ref, x_second_ref,
+        extra_ref, ends_ref,
+    )
+    links = [(y_link_ref[i], z_link_ref[i]) for i in range(planes)]
+    twice = apply_inside(images, x_links, links, [cap_ref[i] for i in range(planes)])
+    add_beside(1, twice, images, edge_ref[0], edge_ref[1])
+    add_beside(0, twice, images, y_link, beyond)
+    for i in range(planes):
+        image_ref[i] = images[i + 1]
+        twice_ref[i] = twice[i]
+    total = others_ref[...] + side_sketch(
+        0, images, twice, draw_ref, low_ref, high_ref, cells_ref, extra_ref
+    )
+    sketch_ref[1 : 1 + PAIR] = as_sketch(total)
     sketch_ref[:1] = b_sketch_ref[:1]
     sketch_ref[1 + PAIR :] = b_sketch_ref[:1]
-    for k, plane in enumerate(b_beside + c_beside):
+    for k in range(4):
         at = slice(k, k + 1)
         corner_first_ref[at], corner_second_ref[at] = by_turn(
-            plane[:1], plane[rows - 1 :], "gy"
+            beside_ref[k, :1], beside_ref[k, rows - 1 :], "gy"
         )
 
 
 def last_kernel(
-    sketch_ref, b_ref, image_ref, twice_ref, ends_ref, corner_first_ref, corner_second_ref,
-    solution_ref, residual_ref,
+    sketch_ref, b_ref, image_ref, twice_ref, ends_first_ref, ends_second_ref, corner_first_ref,
+    corner_second_ref, solution_ref, residual_ref,
 ):
     sketches = jnp.sum(sketch_ref[...], axis=0)
 
@@ -363,13 +416,13 @@
         solution_ref[i] = c0 * b + c1 * image
         residual_ref[i] = b - c0 * image - c1 * twice_ref[i]
     corners = by_turn(corner_first_ref[...], corner_second_ref[...], "gy")
-    for side, (j, here, corner) in enumerate(zip((0, rows - 1), has_beside("gy"), corners)):
+    ends = by_turn(ends_first_ref[...], ends_second_ref[...], "gy")
+    for j, here, corner, known in zip((0, rows - 1), has_beside("gy"), corners, ends):
         for end, i in enumerate((0, planes - 1)):
             b, cond = corner[end : end + 1], corner[2 + end : 3 + end]
             cond = jnp.where(here, cond, 0.0)
-            at = 6 * (2 * side + end)
             x_link, x_b, x_cond, y_link, y_b, y_cond = (
-                ends_ref[at + k : at + k + 1] for k in range(6)
+                known[6 * end + k :][:1] for k in range(6)
             )
             lacked = x_link * link(x_cond, cond) * (x_b - b)
             lacked = lacked + y_link * link(y_cond, cond) * (y_b - b)
@@ -454,18 +507,31 @@
         scratch=[cells],
         flops=work,
     )
-    image, twice, sketch, first, second, ends = call(
+    extra = pltpu.VMEM((3, 4, depth), jnp.float32)
+    more, edge, ends_second, others = call(
         third_kernel,
-        [block, block, (FIELDS + 1, SKETCH), corner, corner, (24, depth)],
-        b, cap, y_link, z_link, draw, *hots, y_second, y_first, image_wide, x_link, beside,
-        *got_x, *got_y, b_sketch, inside,
-        scratch=[cells, pltpu.VMEM((3, 8, depth), jnp.float32)],
+        [wide, (2, planes, depth), (12, depth), total],
+        b, cap, y_link, z_link, draw, *hots, y_second, image_wide, x_link, beside, *got_x,
+        got_y[0], inside,
+        scratch=[cells, extra],
+        flops=work,
+    )
+    image, twice, sketch, first, second, ends_first = call(
+        fourth_kernel,
+        [block, block, (FIELDS + 1, SKETCH), corner, corner, (12, depth)],
+        b, cap, y_link, z_link, draw, *hots, y_first, more, x_link, beside, *got_x, got_y[1],
+        edge, b_sketch, others,
+        scratch=[cells, extra],
         flops=work,
     )
     got_corners = [swap(array, "gy", turn) for turn, array in enumerate((first, second))]
     sketches = everyones(sketch)
     return tuple(
-        call(last_kernel, [block, block], sketches, b, image, twice, ends, *got_corners)
+        call(
+            last_kernel,
+            [block, block],
+            sketches, b, image, twice, ends_first, ends_second, *got_corners,
+        )
     )
 
 

time: 22.7 us -> 22.6 us (level)
  waiting for transfers between devices: 4.39 us -> 3.67 us
  Pallas kernels: 5.13 us -> 5.77 us
    ppermute x6, waiting for transfers between devices: 4.04 us -> 3.34 us  [swap(): return lax.ppermute(array, ('gx', 'gy'), pairs)]
    pallas_call x5 -> x6, Pallas kernels: 5.13 us -> 5.77 us  [call(): pl.pallas_call(kernel, out_shape=[shape if hasattr(shape, 'dtype') else j...]
  transfers between devices with their start and end apart: 7 -> 7, of which waited for: 3 -> 3; matrix products, arithmetic and copies ran while one was open for 0% -> 0% of each run, Pallas kernels for 7% -> 10%
where the time goes in v6:
time: 22.6 us; the launch traced here: 22.5 us
  starting transfers between devices  11.7 us (52%)
  Pallas kernels  5.77 us (26%)
  waiting for transfers between devices  3.67 us (16%)
  between operations  0.66 us (3%)
  local copies, waits for them, and re-layouts  0.63 us (3%)
    ppermute x6, starting transfers between devices, swap(): return lax.ppermute(array, ('gx', 'gy'), pairs)  6.83 us
    pallas_call x6, Pallas kernels, call(): pl.pallas_call(kernel, out_shape=[shape if hasattr(shape, 'dtype') else j...  5.77 us
    all_to_all x1, starting transfers between devices, everyones(): return lax.all_to_all(copies, ('gx', 'gy'), 0, 0, axis_index_groups=[group])  4.89 us
    ppermute x6, waiting for transfers between devices, swap(): return lax.ppermute(array, ('gx', 'gy'), pairs)  3.34 us
    broadcast_in_dim x1, local copies, waits for them, and re-layouts, everyones(): copies = jnp.broadcast_to(sketch[None], (nx * ny,) + sketch.shape)  0.63 us
  transfers between devices with their start and end apart: 7, of which 3 were waited for; matrix products, arithmetic and copies ran while one was open for 0% of the time, Pallas kernels for 10%

profile of v6, /device:TPU:0, one launch (start us, length us, event | category | flops | bytes accessed | tf_op | source)
XLA Modules:
  0.0 22.5 jit_solution(14508077314610960878)
XLA Ops:
  0.6 1.5 %shard_map.68 = (f32[4,8,1024]{2,1,0:T(8,128)S(1)}, f32[4,8,1024]{2,1,0:T(8,128)S(1)}, f32[4,8,1024]{2,1,0:T(8,128)S(1)}, f32[4,8,1024]{2,1,0:T(8,128)S(1)}, f32...) custom-call(f32[4,8,1024]{2,1,0:T(8,128)} %b_hbm.1, ...), custom_call_target="tpu_custom_call" | custom-call | tf_op jit(solution)/shard_map/pallas_call | solution.py:433
  2.1 3.1 %collective-permute-start = (f32[28,1024]{1,0:T(8,128)S(1)}, f32[28,1024]{1,0:T(8,128)S(1)}, u32[]{:S(2)}, u32[]{:S(2)}) collective-permute-start(f32[28,1024]{1,0:T(8,128)S(1)} %get-tuple-element.43), channel_id=1, source_target_pairs={{0,1},{1,0},{2,3},{3,2},{4,8},{5,9},{6,10},{7,11},{8,4},{9,5},{10,... | collective-permute-start | bytes 344072 | tf_op jit(solution)/shard_map/ppermute | solution.py:459
  5.2 0.1 collective-permute-start.1
  5.3 0.5 %collective-permute-start.2 = (f32[16,1024]{1,0:T(8,128)S(1)}, f32[16,1024]{1,0:T(8,128)S(1)}, u32[]{:S(2)}, u32[]{:S(2)}) collective-permute-start(f32[16,1024]{1,0:T(8,128)S(1)} %get-tuple-element.40.own_ref), channel_id=1, source_target_pairs={{0,4},{1,2},{2,1},{3,7},{4,0},{5,6},{6,5},{7,3},{8,12},{9,10},{10,... | collective-permute-start | bytes 196616 | tf_op jit(solution)/shard_map/ppermute | solution.py:459
  5.7 2.7 %collective-permute-start.3 = (f32[16,1024]{1,0:T(8,128)S(1)}, f32[16,1024]{1,0:T(8,128)S(1)}, u32[]{:S(2)}, u32[]{:S(2)}) collective-permute-start(f32[16,1024]{1,0:T(8,128)S(1)} %get-tuple-element.39.own_ref), channel_id=1, source_target_pairs={{0,1},{1,0},{2,3},{3,2},{4,5},{5,4},{6,7},{7,6},{8,9},{9,8},{10,11... | collective-permute-start | bytes 196616 | tf_op jit(solution)/shard_map/ppermute | solution.py:459
  8.4 0.9 %shard_map.69 = (bf16[1024,1024]{1,0:T(8,128)(2,1)S(1)}, bf16[512,1024]{1,0:T(8,128)(2,1)S(1)}, f32[2,128]{1,0:T(2,128)S(1)}) custom-call(f32[4,8,1024]{2,1,0:T(8,128)S(1)} %get-tuple-element.31.b_ref, f32[4,8,1024]{2,1,0:T(8,128)S(1)} %get-tuple-element.35.draw_ref, f32[4,8,1024]{2,1,0:T(8,128)S(1)} %get-tuple-element.36.slot_ref), custom_call_target="tpu_custom_call" | custom-call | flops 25165824 | tf_op jit(solution)/shard_map/pallas_call | solution.py:433
  9.3 0.0 collective-permute-done.got_second_ref.x_second_ref
  9.3 0.0 collective-permute-done.1.got_first_ref.x_first_ref
  9.3 0.6 %shard_map.70 = (f32[6,8,1024]{2,1,0:T(8,128)S(1)}, f32[5,8,1024]{2,1,0:T(8,128)S(1)}, f32[4,8,1024]{2,1,0:T(8,128)S(1)}, f32[16,32]{1,0:T(8,128)S(1)}) custom-call(f32[4,8,1024]{2,1,0:T(8,128)S(1)} %get-tuple-element.31.b_ref, f32[4,8,1024]{2,1,0:T(8,128)S(1)} %get-tuple-element.41.cond_ref, f32[4,8,1024]{2,1,0:T(8,128)S(1)} %get-tuple-element.32.cap_ref, ...), custom_call_target="tpu_custom_call" | custom-call | flops 25165824 | tf_op jit(solution)/shard_map/pallas_call | solution.py:433
  9.9 0.0 collective-permute-done.2.line_ref
  10.0 0.8 %shard_map.71 = (f32[6,8,1024]{2,1,0:T(8,128)S(1)}, f32[2,4,1024]{2,1,0:T(4,128)S(1)}, f32[12,1024]{1,0:T(8,128)S(1)}, f32[16,32]{1,0:T(8,128)S(1)}) custom-call(f32[4,8,1024]{2,1,0:T(8,128)S(1)} %get-tuple-element.31.b_ref, f32[4,8,1024]{2,1,0:T(8,128)S(1)} %get-tuple-element.32.cap_ref, f32[4,8,1024]{2,1,0:T(8,128)S(1)} %get-tuple-element.33.y_link_ref, ...), custom_call_target="tpu_custom_call" | custom-call | flops 25165824 | tf_op jit(solution)/shard_map/pallas_call | solution.py:433
  10.7 0.1 collective-permute-done.3.line_ref
  10.8 0.8 %shard_map.72 = (f32[4,8,1024]{2,1,0:T(8,128)S(1)}, f32[4,8,1024]{2,1,0:T(8,128)S(1)}, f32[4,128]{1,0:T(4,128)S(1)}, f32[4,1024]{1,0:T(4,128)S(1)}, f32[4,1024]{1,0:T(4,128)S(1)}, /*index=5*/f32[12,1024]{1,0:T(8,128)S(1)}) custom-call(f32[4,8,1024]{2,1,0:T(8,128)S(1)} %get-tuple-element.31.b_ref, f32[4,8,1024]{2,1,0:T(8,128)S(1)} %get-tuple-element.32.cap_ref, ...), custom_call_target="tpu_custom_call" | custom-call | flops 25165824 | tf_op jit(solution)/shard_map/pallas_call | solution.py:433
  11.7 0.6 %broadcast_in_dim.2 = f32[16,4,128]{2,1,0:T(4,128)} broadcast(f32[4,128]{1,0:T(4,128)S(1)} %get-tuple-element.53), dimensions={1,2} | broadcast | bytes 34816 | tf_op jit(solution)/shard_map/broadcast_in_dim | solution.py:468
  12.3 4.9 %all-to-all-start = ((f32[16,4,128]{2,1,0:T(4,128)}), f32[16,4,128]{2,1,0:T(4,128)S(1)}, u32[]{:S(2)}, u32[]{:S(2)}) async-start(f32[16,4,128]{2,1,0:T(4,128)} %broadcast_in_dim.2), calls=%async_computation | async-start | bytes 65536 | tf_op jit(solution)/shard_map/all_to_all | solution.py:469
  17.2 0.5 %collective-permute-start.4 = (f32[4,1024]{1,0:T(4,128)S(1)}, f32[4,1024]{1,0:T(4,128)S(1)}, u32[]{:S(2)}, u32[]{:S(2)}) collective-permute-start(f32[4,1024]{1,0:T(4,128)S(1)} %get-tuple-element.58), channel_id=1, source_target_pairs={{0,1},{1,0},{2,3},{3,2},{4,5},{5,4},{6,7},{7,6},{8,9},{9,8},{10,11... | collective-permute-start | bytes 49160 | tf_op jit(solution)/shard_map/ppermute | solution.py:459
  17.7 0.0 collective-permute-start.5
  17.7 3.2 %collective-permute-done.4.corner_first_ref = f32[4,1024]{1,0:T(4,128)S(1)} collective-permute-done((f32[4,1024]{1,0:T(4,128)S(1)}, f32[4,1024]{1,0:T(4,128)S(1)}, u32[]{:S(2)}, u32[]{:S(2)}) %collective-permute-start.4) | collective-permute-done | bytes 16416 | tf_op jit(solution)/shard_map/ppermute | solution.py:459
  20.9 0.0 collective-permute-done.5.corner_second_ref
  20.9 0.3 %all-to-all-done.sketch_ref = f32[16,4,128]{2,1,0:T(4,128)S(1)} async-done(((f32[16,4,128]{2,1,0:T(4,128)}), f32[16,4,128]{2,1,0:T(4,128)S(1)}, u32[]{:S(2)}, u32[]{:S(2)}) %all-to-all-start) | async-done | bytes 32800 | tf_op jit(solution)/shard_map/all_to_all | solution.py:469
  21.3 1.2 %shard_map.73 = (f32[4,8,1024]{2,1,0:T(8,128)}, f32[4,8,1024]{2,1,0:T(8,128)}) custom-call(f32[16,4,128]{2,1,0:T(4,128)S(1)} %all-to-all-done.sketch_ref, f32[4,8,1024]{2,1,0:T(8,128)S(1)} %get-tuple-element.31.b_ref, f32[4,8,1024]{2,1,0:T(8,128)S(1)} %get-tuple-element.54.image_ref, f32[4,8,1024]{2,1,0:T(8,128)S(1)} %get-tuple-element.55.twice_ref, ...), custom_call_target="tpu_custom_call" | custom-call | tf_op jit(solution)/shard_map/pallas_call | solution.py:433
Async XLA Ops:
  2.1 7.2 %collective-permute-start = (f32[28,1024]{1,0:T(8,128)S(1)}, f32[28,1024]{1,0:T(8,128)S(1)}, u32[]{:S(2)}, u32[]{:S(2)}) collective-permute-start(f32[28,1024]{1,0:T(8,128)S(1)} %get-tuple-element.43), channel_id=1, source_target_pairs={{0,1},{1,0},{2,3},{3,2},{4,8},{5,9},{6,10},{7,11},{8,4},{9,5},{10,... | collective-permute-start | bytes 344072 | tf_op jit(solution)/shard_map/ppermute | solution.py:459
  5.2 4.1 %collective-permute-start.1 = (f32[28,1024]{1,0:T(8,128)S(1)}, f32[28,1024]{1,0:T(8,128)S(1)}, u32[]{:S(2)}, u32[]{:S(2)}) collective-permute-start(f32[28,1024]{1,0:T(8,128)S(1)} %get-tuple-element.44), channel_id=1, source_target_pairs={{0,4},{1,5},{2,6},{3,7},{4,0},{5,1},{6,2},{7,3},{8,12},{9,13},{10,... | collective-permute-start | bytes 344072 | tf_op jit(solution)/shard_map/ppermute | solution.py:459
  5.3 4.7 %collective-permute-start.2 = (f32[16,1024]{1,0:T(8,128)S(1)}, f32[16,1024]{1,0:T(8,128)S(1)}, u32[]{:S(2)}, u32[]{:S(2)}) collective-permute-start(f32[16,1024]{1,0:T(8,128)S(1)} %get-tuple-element.40.own_ref), channel_id=1, source_target_pairs={{0,4},{1,2},{2,1},{3,7},{4,0},{5,6},{6,5},{7,3},{8,12},{9,10},{10,... | collective-permute-start | bytes 196616 | tf_op jit(solution)/shard_map/ppermute | solution.py:459
  5.7 5.1 %collective-permute-start.3 = (f32[16,1024]{1,0:T(8,128)S(1)}, f32[16,1024]{1,0:T(8,128)S(1)}, u32[]{:S(2)}, u32[]{:S(2)}) collective-permute-start(f32[16,1024]{1,0:T(8,128)S(1)} %get-tuple-element.39.own_ref), channel_id=1, source_target_pairs={{0,1},{1,0},{2,3},{3,2},{4,5},{5,4},{6,7},{7,6},{8,9},{9,8},{10,11... | collective-permute-start | bytes 196616 | tf_op jit(solution)/shard_map/ppermute | solution.py:459
  12.3 9.0 %all-to-all-start = ((f32[16,4,128]{2,1,0:T(4,128)}), f32[16,4,128]{2,1,0:T(4,128)S(1)}, u32[]{:S(2)}, u32[]{:S(2)}) async-start(f32[16,4,128]{2,1,0:T(4,128)} %broadcast_in_dim.2), calls=%async_computation | async-start | bytes 65536 | tf_op jit(solution)/shard_map/all_to_all | solution.py:469
  17.2 3.7 %collective-permute-start.4 = (f32[4,1024]{1,0:T(4,128)S(1)}, f32[4,1024]{1,0:T(4,128)S(1)}, u32[]{:S(2)}, u32[]{:S(2)}) collective-permute-start(f32[4,1024]{1,0:T(4,128)S(1)} %get-tuple-element.58), channel_id=1, source_target_pairs={{0,1},{1,0},{2,3},{3,2},{4,5},{5,4},{6,7},{7,6},{8,9},{9,8},{10,11... | collective-permute-start | bytes 49160 | tf_op jit(solution)/shard_map/ppermute | solution.py:459
  17.7 3.2 %collective-permute-start.5 = (f32[4,1024]{1,0:T(4,128)S(1)}, f32[4,1024]{1,0:T(4,128)S(1)}, u32[]{:S(2)}, u32[]{:S(2)}) collective-permute-start(f32[4,1024]{1,0:T(4,128)S(1)} %get-tuple-element.59), channel_id=1, source_target_pairs={{0,4},{1,2},{2,1},{3,7},{4,0},{5,6},{6,5},{7,3},{8,12},{9,10},{10,... | collective-permute-start | bytes 49160 | tf_op jit(solution)/shard_map/ppermute | solution.py:459

commit v7 on v0

--- a/solution.py
+++ b/solution.py
@@ -407,9 +407,15 @@
 
 
 def everyones(sketch):
-    count = lax.axis_size("gx") * lax.axis_size("gy")
-    copies = jnp.broadcast_to(sketch[None], (count,) + sketch.shape)
-    return lax.all_to_all(copies, ("gx", "gy"), 0, 0)
+    nx, ny = lax.axis_size("gx"), lax.axis_size("gy")
+    sketch = sketch + swap(sketch, "gx", 0)
+    groups = []
+    for turn, middle in enumerate(((1, ny // 2), (1, ny // 2 - 1))):
+        places = [(x, y) for x in range(nx) for y in range(ny) if (x + y // (ny // 2)) % 2 == turn]
+        places.sort(key=lambda at: (at != middle, at))
+        groups.append([x * ny + y for x, y in places])
+    copies = jnp.broadcast_to(sketch[None], (nx * ny // 2,) + sketch.shape)
+    return lax.all_to_all(copies, ("gx", "gy"), 0, 0, axis_index_groups=groups)
 
 
 def body(b, warmth, phase, slots, draw):

time: 24.5 us -> 24.3 us (level)
  the two profiles are of different devices: /device:TPU:0 before, /device:TPU:1 now
where the time goes in v7:
time: 24.3 us; the launch traced here: 24.1 us
  starting transfers between devices  12.3 us (51%)
  waiting for transfers between devices  5.42 us (22%)
  Pallas kernels  5.13 us (21%)
  between operations  0.66 us (3%)
  local copies, waits for them, and re-layouts  0.61 us (3%)
    ppermute x7, starting transfers between devices, swap(): return lax.ppermute(array, ('gx', 'gy'), pairs)  7.46 us
    pallas_call x5, Pallas kernels, call(): pl.pallas_call(kernel, out_shape=[shape if hasattr(shape, 'dtype') else j...  5.13 us
    all_to_all x1, starting transfers between devices, everyones(): return lax.all_to_all(copies, ('gx', 'gy'), 0, 0, axis_index_groups=groups)  4.81 us
    ppermute x7, waiting for transfers between devices, swap(): return lax.ppermute(array, ('gx', 'gy'), pairs)  3.52 us
    all_to_all x1, waiting for transfers between devices, everyones(): return lax.all_to_all(copies, ('gx', 'gy'), 0, 0, axis_index_groups=groups)  1.9 us
    broadcast_in_dim x1, local copies, waits for them, and re-layouts, everyones(): copies = jnp.broadcast_to(sketch[None], (nx * ny // 2,) + sketch.shape)  0.61 us
  transfers between devices with their start and end apart: 8, of which 4 were waited for; matrix products, arithmetic and copies ran while one was open for 0% of the time, Pallas kernels for 6%

profile of v7, /device:TPU:1, one launch (start us, length us, event | category | flops | bytes accessed | tf_op | source)
XLA Modules:
  0.0 24.1 jit_solution(7783974905449002762)
XLA Ops:
  0.6 1.5 %shard_map.68 = (f32[4,8,1024]{2,1,0:T(8,128)S(1)}, f32[4,8,1024]{2,1,0:T(8,128)S(1)}, f32[4,8,1024]{2,1,0:T(8,128)S(1)}, f32[4,8,1024]{2,1,0:T(8,128)S(1)}, f32...) custom-call(f32[4,8,1024]{2,1,0:T(8,128)} %b_hbm.1, ...), custom_call_target="tpu_custom_call" | custom-call | tf_op jit(solution)/shard_map/pallas_call | solution.py:380
  2.1 2.7 %collective-permute-start = (f32[28,1024]{1,0:T(8,128)S(1)}, f32[28,1024]{1,0:T(8,128)S(1)}, u32[]{:S(2)}, u32[]{:S(2)}) collective-permute-start(f32[28,1024]{1,0:T(8,128)S(1)} %get-tuple-element.39), channel_id=1, source_target_pairs={{0,1},{1,0},{2,3},{3,2},{4,8},{5,9},{6,10},{7,11},{8,4},{9,5},{10,... | collective-permute-start | bytes 344072 | tf_op jit(solution)/shard_map/ppermute | solution.py:406
  4.8 0.5 %collective-permute-start.1 = (f32[28,1024]{1,0:T(8,128)S(1)}, f32[28,1024]{1,0:T(8,128)S(1)}, u32[]{:S(2)}, u32[]{:S(2)}) collective-permute-start(f32[28,1024]{1,0:T(8,128)S(1)} %get-tuple-element.40), channel_id=1, source_target_pairs={{0,4},{1,5},{2,6},{3,7},{4,0},{5,1},{6,2},{7,3},{8,12},{9,13},{10,... | collective-permute-start | bytes 344072 | tf_op jit(solution)/shard_map/ppermute | solution.py:406
  5.2 0.1 collective-permute-start.2
  5.3 2.5 %collective-permute-start.3 = (f32[16,1024]{1,0:T(8,128)S(1)}, f32[16,1024]{1,0:T(8,128)S(1)}, u32[]{:S(2)}, u32[]{:S(2)}) collective-permute-start(f32[16,1024]{1,0:T(8,128)S(1)} %get-tuple-element.36.own_first_ref), channel_id=1, source_target_pairs={{0,1},{1,0},{2,3},{3,2},{4,5},{5,4},{6,7},{7,6},{8,9},{9,8},{10,11... | collective-permute-start | bytes 196616 | tf_op jit(solution)/shard_map/ppermute | solution.py:406
  7.8 0.9 %shard_map.69 = (bf16[1024,1024]{1,0:T(8,128)(2,1)S(1)}, bf16[512,1024]{1,0:T(8,128)(2,1)S(1)}, f32[2,128]{1,0:T(2,128)S(1)}) custom-call(f32[4,8,1024]{2,1,0:T(8,128)S(1)} %get-tuple-element.27.b_ref, f32[4,8,1024]{2,1,0:T(8,128)S(1)} %get-tuple-element.31.draw_ref, f32[4,8,1024]{2,1,0:T(8,128)S(1)} %get-tuple-element.32.slot_ref), custom_call_target="tpu_custom_call" | custom-call | flops 25165824 | tf_op jit(solution)/shard_map/pallas_call | solution.py:380
  8.7 0.0 collective-permute-done.got_second_ref.x_second_ref
  8.7 0.0 collective-permute-done.1.got_first_ref.x_first_ref
  8.8 0.6 %shard_map.70 = (f32[6,8,1024]{2,1,0:T(8,128)S(1)}, f32[5,8,1024]{2,1,0:T(8,128)S(1)}, f32[4,8,1024]{2,1,0:T(8,128)S(1)}, f32[16,32]{1,0:T(8,128)S(1)}) custom-call(f32[4,8,1024]{2,1,0:T(8,128)S(1)} %get-tuple-element.27.b_ref, f32[4,8,1024]{2,1,0:T(8,128)S(1)} %get-tuple-element.37.cond_ref, f32[4,8,1024]{2,1,0:T(8,128)S(1)} %get-tuple-element.28.cap_ref, ...), custom_call_target="tpu_custom_call" | custom-call | flops 25165824 | tf_op jit(solution)/shard_map/pallas_call | solution.py:380
  9.4 0.0 collective-permute-done.2.y_second_ref
  9.4 0.7 %collective-permute-done.3.y_first_ref = f32[16,1024]{1,0:T(8,128)S(1)} collective-permute-done((f32[16,1024]{1,0:T(8,128)S(1)}, f32[16,1024]{1,0:T(8,128)S(1)}, u32[]{:S(2)}, u32[]{:S(2)}) %collective-permute-start.3) | collective-permute-done | bytes 65568 | tf_op jit(solution)/shard_map/ppermute | solution.py:406
  10.0 1.0 %shard_map.71 = (f32[4,8,1024]{2,1,0:T(8,128)S(1)}, f32[4,8,1024]{2,1,0:T(8,128)S(1)}, f32[4,128]{1,0:T(4,128)S(1)}, f32[4,1024]{1,0:T(4,128)S(1)}, f32[4,1024]{1,0:T(4,128)S(1)}, /*index=5*/f32[24,1024]{1,0:T(8,128)S(1)}) custom-call(f32[4,8,1024]{2,1,0:T(8,128)S(1)} %get-tuple-element.27.b_ref, f32[4,8,1024]{2,1,0:T(8,128)S(1)} %get-tuple-element.28.cap_ref, ...), custom_call_target="tpu_custom_call" | custom-call | flops 25165824 | tf_op jit(solution)/shard_map/pallas_call | solution.py:380
  11.1 0.9 %collective-permute-start.4 = (f32[4,128]{1,0:T(4,128)S(1)}, f32[4,128]{1,0:T(4,128)S(1)}, u32[]{:S(2)}, u32[]{:S(2)}) collective-permute-start(f32[4,128]{1,0:T(4,128)S(1)} %get-tuple-element.46), channel_id=1, source_target_pairs={{0,4},{1,5},{2,6},{3,7},{4,0},{5,1},{6,2},{7,3},{8,12},{9,13},{10,... | collective-permute-start | bytes 6152 | tf_op jit(solution)/shard_map/ppermute | solution.py:406
  11.9 0.8 %collective-permute-done.4 = f32[4,128]{1,0:T(4,128)S(1)} collective-permute-done((f32[4,128]{1,0:T(4,128)S(1)}, f32[4,128]{1,0:T(4,128)S(1)}, u32[]{:S(2)}, u32[]{:S(2)}) %collective-permute-start.4) | collective-permute-done | bytes 2080 | tf_op jit(solution)/shard_map/ppermute | solution.py:406
  12.7 0.6 %broadcast_in_dim.2 = f32[8,4,128]{2,1,0:T(4,128)} broadcast(f32[4,128]{1,0:T(4,128)S(1)} %add.3), dimensions={1,2} | broadcast | bytes 18432 | tf_op jit(solution)/shard_map/broadcast_in_dim | solution.py:417
  13.4 4.8 %all-to-all-start = ((f32[8,4,128]{2,1,0:T(4,128)}), f32[8,4,128]{2,1,0:T(4,128)S(1)}, u32[]{:S(2)}, u32[]{:S(2)}) async-start(f32[8,4,128]{2,1,0:T(4,128)} %broadcast_in_dim.2), calls=%async_computation | async-start | bytes 32768 | tf_op jit(solution)/shard_map/all_to_all | solution.py:418
  18.2 0.2 collective-permute-start.5
  18.3 0.7 %collective-permute-start.6 = (f32[4,1024]{1,0:T(4,128)S(1)}, f32[4,1024]{1,0:T(4,128)S(1)}, u32[]{:S(2)}, u32[]{:S(2)}) collective-permute-start(f32[4,1024]{1,0:T(4,128)S(1)} %get-tuple-element.51), channel_id=1, source_target_pairs={{0,4},{1,2},{2,1},{3,7},{4,0},{5,6},{6,5},{7,3},{8,12},{9,10},{10,... | collective-permute-start | bytes 49160 | tf_op jit(solution)/shard_map/ppermute | solution.py:406
  19.0 2.0 %collective-permute-done.5.corner_first_ref = f32[4,1024]{1,0:T(4,128)S(1)} collective-permute-done((f32[4,1024]{1,0:T(4,128)S(1)}, f32[4,1024]{1,0:T(4,128)S(1)}, u32[]{:S(2)}, u32[]{:S(2)}) %collective-permute-start.5) | collective-permute-done | bytes 16416 | tf_op jit(solution)/shard_map/ppermute | solution.py:406
  21.1 0.0 collective-permute-done.6.corner_second_ref
  21.1 1.9 %all-to-all-done.sketch_ref = f32[8,4,128]{2,1,0:T(4,128)S(1)} async-done(((f32[8,4,128]{2,1,0:T(4,128)}), f32[8,4,128]{2,1,0:T(4,128)S(1)}, u32[]{:S(2)}, u32[]{:S(2)}) %all-to-all-start) | async-done | bytes 16416 | tf_op jit(solution)/shard_map/all_to_all | solution.py:418
  23.0 1.1 %shard_map.72 = (f32[4,8,1024]{2,1,0:T(8,128)}, f32[4,8,1024]{2,1,0:T(8,128)}) custom-call(f32[8,4,128]{2,1,0:T(4,128)S(1)} %all-to-all-done.sketch_ref, f32[4,8,1024]{2,1,0:T(8,128)S(1)} %get-tuple-element.27.b_ref, f32[4,8,1024]{2,1,0:T(8,128)S(1)} %get-tuple-element.47.image_ref, f32[4,8,1024]{2,1,0:T(8,128)S(1)} %get-tuple-element.48.twice_ref, ...), custom_call_target="tpu_custom_call" | custom-call | tf_op jit(solution)/shard_map/pallas_call | solution.py:380
  (1 shorter events, 0.0 us)
Async XLA Ops:
  2.1 6.6 %collective-permute-start = (f32[28,1024]{1,0:T(8,128)S(1)}, f32[28,1024]{1,0:T(8,128)S(1)}, u32[]{:S(2)}, u32[]{:S(2)}) collective-permute-start(f32[28,1024]{1,0:T(8,128)S(1)} %get-tuple-element.39), channel_id=1, source_target_pairs={{0,1},{1,0},{2,3},{3,2},{4,8},{5,9},{6,10},{7,11},{8,4},{9,5},{10,... | collective-permute-start | bytes 344072 | tf_op jit(solution)/shard_map/ppermute | solution.py:406
  4.8 4.0 %collective-permute-start.1 = (f32[28,1024]{1,0:T(8,128)S(1)}, f32[28,1024]{1,0:T(8,128)S(1)}, u32[]{:S(2)}, u32[]{:S(2)}) collective-permute-start(f32[28,1024]{1,0:T(8,128)S(1)} %get-tuple-element.40), channel_id=1, source_target_pairs={{0,4},{1,5},{2,6},{3,7},{4,0},{5,1},{6,2},{7,3},{8,12},{9,13},{10,... | collective-permute-start | bytes 344072 | tf_op jit(solution)/shard_map/ppermute | solution.py:406
  5.2 4.1 %collective-permute-start.2 = (f32[16,1024]{1,0:T(8,128)S(1)}, f32[16,1024]{1,0:T(8,128)S(1)}, u32[]{:S(2)}, u32[]{:S(2)}) collective-permute-start(f32[16,1024]{1,0:T(8,128)S(1)} %get-tuple-element.35.own_second_ref), channel_id=1, source_target_pairs={{0,4},{1,2},{2,1},{3,7},{4,0},{5,6},{6,5},{7,3},{8,12},{9,10},{10,... | collective-permute-start | bytes 196616 | tf_op jit(solution)/shard_map/ppermute | solution.py:406
  5.3 4.7 %collective-permute-start.3 = (f32[16,1024]{1,0:T(8,128)S(1)}, f32[16,1024]{1,0:T(8,128)S(1)}, u32[]{:S(2)}, u32[]{:S(2)}) collective-permute-start(f32[16,1024]{1,0:T(8,128)S(1)} %get-tuple-element.36.own_first_ref), channel_id=1, source_target_pairs={{0,1},{1,0},{2,3},{3,2},{4,5},{5,4},{6,7},{7,6},{8,9},{9,8},{10,11... | collective-permute-start | bytes 196616 | tf_op jit(solution)/shard_map/ppermute | solution.py:406
  11.1 1.7 %collective-permute-start.4 = (f32[4,128]{1,0:T(4,128)S(1)}, f32[4,128]{1,0:T(4,128)S(1)}, u32[]{:S(2)}, u32[]{:S(2)}) collective-permute-start(f32[4,128]{1,0:T(4,128)S(1)} %get-tuple-element.46), channel_id=1, source_target_pairs={{0,4},{1,5},{2,6},{3,7},{4,0},{5,1},{6,2},{7,3},{8,12},{9,13},{10,... | collective-permute-start | bytes 6152 | tf_op jit(solution)/shard_map/ppermute | solution.py:406
  13.4 9.6 %all-to-all-start = ((f32[8,4,128]{2,1,0:T(4,128)}), f32[8,4,128]{2,1,0:T(4,128)S(1)}, u32[]{:S(2)}, u32[]{:S(2)}) async-start(f32[8,4,128]{2,1,0:T(4,128)} %broadcast_in_dim.2), calls=%async_computation | async-start | bytes 32768 | tf_op jit(solution)/shard_map/all_to_all | solution.py:418
  18.2 2.9 %collective-permute-start.5 = (f32[4,1024]{1,0:T(4,128)S(1)}, f32[4,1024]{1,0:T(4,128)S(1)}, u32[]{:S(2)}, u32[]{:S(2)}) collective-permute-start(f32[4,1024]{1,0:T(4,128)S(1)} %get-tuple-element.50), channel_id=1, source_target_pairs={{0,1},{1,0},{2,3},{3,2},{4,5},{5,4},{6,7},{7,6},{8,9},{9,8},{10,11... | collective-permute-start | bytes 49160 | tf_op jit(solution)/shard_map/ppermute | solution.py:406
  18.3 2.7 %collective-permute-start.6 = (f32[4,1024]{1,0:T(4,128)S(1)}, f32[4,1024]{1,0:T(4,128)S(1)}, u32[]{:S(2)}, u32[]{:S(2)}) collective-permute-start(f32[4,1024]{1,0:T(4,128)S(1)} %get-tuple-element.51), channel_id=1, source_target_pairs={{0,4},{1,2},{2,1},{3,7},{4,0},{5,6},{6,5},{7,3},{8,12},{9,10},{10,... | collective-permute-start | bytes 49160 | tf_op jit(solution)/shard_map/ppermute | solution.py:406

commit v8 on v2

--- a/solution.py
+++ b/solution.py
@@ -350,13 +350,10 @@
     t1 = p1 * n0_inverse - h01 * q0 - h11 * (t0 * n0_inverse)
     n1_square = inner(t1, t1) + epsilon
     first = h00 * h00 + n0 * n0
-    cross = h00 * h01 + n0 * h11
+    cross = h00 * h11 - n0 * h01
     ratio = cross / first
-    second = h01 * h01 + h11 * h11 + n1_square - cross * ratio
-    y1 = (h01 - ratio * h00) / second
-    y0 = h00 / first - ratio * y1
-    c1 = y1 * n0_inverse
-    c0 = y0 - h00 * c1
+    c1 = -ratio / (cross * ratio + n1_square)
+    c0 = h00 / first - (h00 * h01 + n0 * h11) / first * (n0 * c1) - h00 * c1
     planes, rows, depth = b_ref.shape
     for i in range(planes):
         b, image = b_ref[i], image_ref[i]

time: 22.7 us -> 22.7 us (level)
  no operation moved by 1% of the time
where the time goes in v8:
time: 22.7 us; the launch traced here: 22.5 us
  starting transfers between devices  11.7 us (52%)
  Pallas kernels  5.13 us (23%)
  waiting for transfers between devices  4.39 us (19%)
  between operations  0.66 us (3%)
  local copies, waits for them, and re-layouts  0.64 us (3%)
    ppermute x6, starting transfers between devices, swap(): return lax.ppermute(array, ('gx', 'gy'), pairs)  6.89 us
    pallas_call x5, Pallas kernels, call(): pl.pallas_call(kernel, out_shape=[shape if hasattr(shape, 'dtype') else j...  5.13 us
    all_to_all x1, starting transfers between devices, everyones(): return lax.all_to_all(copies, ('gx', 'gy'), 0, 0, axis_index_groups=[group])  4.8 us
    ppermute x6, waiting for transfers between devices, swap(): return lax.ppermute(array, ('gx', 'gy'), pairs)  4.04 us
    broadcast_in_dim x1, local copies, waits for them, and re-layouts, everyones(): copies = jnp.broadcast_to(sketch[None], (nx * ny,) + sketch.shape)  0.64 us
  transfers between devices with their start and end apart: 7, of which 3 were waited for; matrix products, arithmetic and copies ran while one was open for 0% of the time, Pallas kernels for 7%

profile of v8, /device:TPU:0, one launch (start us, length us, event | category | flops | bytes accessed | tf_op | source)
XLA Modules:
  0.0 22.5 jit_solution(11551174753715561484)
XLA Ops:
  0.6 1.5 %shard_map.68 = (f32[4,8,1024]{2,1,0:T(8,128)S(1)}, f32[4,8,1024]{2,1,0:T(8,128)S(1)}, f32[4,8,1024]{2,1,0:T(8,128)S(1)}, f32[4,8,1024]{2,1,0:T(8,128)S(1)}, f32...) custom-call(f32[4,8,1024]{2,1,0:T(8,128)} %b_hbm.1, ...), custom_call_target="tpu_custom_call" | custom-call | tf_op jit(solution)/shard_map/pallas_call | solution.py:377
  2.1 3.1 %collective-permute-start = (f32[28,1024]{1,0:T(8,128)S(1)}, f32[28,1024]{1,0:T(8,128)S(1)}, u32[]{:S(2)}, u32[]{:S(2)}) collective-permute-start(f32[28,1024]{1,0:T(8,128)S(1)} %get-tuple-element.39), channel_id=1, source_target_pairs={{0,1},{1,0},{2,3},{3,2},{4,8},{5,9},{6,10},{7,11},{8,4},{9,5},{10,... | collective-permute-start | bytes 344072 | tf_op jit(solution)/shard_map/ppermute | solution.py:403
  5.2 0.1 collective-permute-start.1
  5.3 0.5 %collective-permute-start.2 = (f32[16,1024]{1,0:T(8,128)S(1)}, f32[16,1024]{1,0:T(8,128)S(1)}, u32[]{:S(2)}, u32[]{:S(2)}) collective-permute-start(f32[16,1024]{1,0:T(8,128)S(1)} %get-tuple-element.35.own_second_ref), channel_id=1, source_target_pairs={{0,4},{1,2},{2,1},{3,7},{4,0},{5,6},{6,5},{7,3},{8,12},{9,10},{10,... | collective-permute-start | bytes 196616 | tf_op jit(solution)/shard_map/ppermute | solution.py:403
  5.7 2.7 %collective-permute-start.3 = (f32[16,1024]{1,0:T(8,128)S(1)}, f32[16,1024]{1,0:T(8,128)S(1)}, u32[]{:S(2)}, u32[]{:S(2)}) collective-permute-start(f32[16,1024]{1,0:T(8,128)S(1)} %get-tuple-element.36.own_first_ref), channel_id=1, source_target_pairs={{0,1},{1,0},{2,3},{3,2},{4,5},{5,4},{6,7},{7,6},{8,9},{9,8},{10,11... | collective-permute-start | bytes 196616 | tf_op jit(solution)/shard_map/ppermute | solution.py:403
  8.4 0.9 %shard_map.69 = (bf16[1024,1024]{1,0:T(8,128)(2,1)S(1)}, bf16[512,1024]{1,0:T(8,128)(2,1)S(1)}, f32[2,128]{1,0:T(2,128)S(1)}) custom-call(f32[4,8,1024]{2,1,0:T(8,128)S(1)} %get-tuple-element.27.b_ref, f32[4,8,1024]{2,1,0:T(8,128)S(1)} %get-tuple-element.31.draw_ref, f32[4,8,1024]{2,1,0:T(8,128)S(1)} %get-tuple-element.32.slot_ref), custom_call_target="tpu_custom_call" | custom-call | flops 25165824 | tf_op jit(solution)/shard_map/pallas_call | solution.py:377
  9.3 0.0 collective-permute-done.got_second_ref.x_second_ref
  9.3 0.0 collective-permute-done.1.got_first_ref.x_first_ref
  9.3 0.6 %shard_map.70 = (f32[6,8,1024]{2,1,0:T(8,128)S(1)}, f32[5,8,1024]{2,1,0:T(8,128)S(1)}, f32[4,8,1024]{2,1,0:T(8,128)S(1)}, f32[16,32]{1,0:T(8,128)S(1)}) custom-call(f32[4,8,1024]{2,1,0:T(8,128)S(1)} %get-tuple-element.27.b_ref, f32[4,8,1024]{2,1,0:T(8,128)S(1)} %get-tuple-element.37.cond_ref, f32[4,8,1024]{2,1,0:T(8,128)S(1)} %get-tuple-element.28.cap_ref, ...), custom_call_target="tpu_custom_call" | custom-call | flops 25165824 | tf_op jit(solution)/shard_map/pallas_call | solution.py:377
  9.9 0.0 collective-permute-done.2.y_second_ref
  10.0 0.9 %collective-permute-done.3.y_first_ref = f32[16,1024]{1,0:T(8,128)S(1)} collective-permute-done((f32[16,1024]{1,0:T(8,128)S(1)}, f32[16,1024]{1,0:T(8,128)S(1)}, u32[]{:S(2)}, u32[]{:S(2)}) %collective-permute-start.3) | collective-permute-done | bytes 65568 | tf_op jit(solution)/shard_map/ppermute | solution.py:403
  10.8 1.0 %shard_map.71 = (f32[4,8,1024]{2,1,0:T(8,128)S(1)}, f32[4,8,1024]{2,1,0:T(8,128)S(1)}, f32[4,128]{1,0:T(4,128)S(1)}, f32[4,1024]{1,0:T(4,128)S(1)}, f32[4,1024]{1,0:T(4,128)S(1)}, /*index=5*/f32[24,1024]{1,0:T(8,128)S(1)}) custom-call(f32[4,8,1024]{2,1,0:T(8,128)S(1)} %get-tuple-element.27.b_ref, f32[4,8,1024]{2,1,0:T(8,128)S(1)} %get-tuple-element.28.cap_ref, ...), custom_call_target="tpu_custom_call" | custom-call | flops 25165824 | tf_op jit(solution)/shard_map/pallas_call | solution.py:377
  11.8 0.6 %broadcast_in_dim.2 = f32[16,4,128]{2,1,0:T(4,128)} broadcast(f32[4,128]{1,0:T(4,128)S(1)} %get-tuple-element.46), dimensions={1,2} | broadcast | bytes 34816 | tf_op jit(solution)/shard_map/broadcast_in_dim | solution.py:412
  12.5 4.8 %all-to-all-start = ((f32[16,4,128]{2,1,0:T(4,128)}), f32[16,4,128]{2,1,0:T(4,128)S(1)}, u32[]{:S(2)}, u32[]{:S(2)}) async-start(f32[16,4,128]{2,1,0:T(4,128)} %broadcast_in_dim.2), calls=%async_computation | async-start | bytes 65536 | tf_op jit(solution)/shard_map/all_to_all | solution.py:413
  17.3 0.6 %collective-permute-start.4 = (f32[4,1024]{1,0:T(4,128)S(1)}, f32[4,1024]{1,0:T(4,128)S(1)}, u32[]{:S(2)}, u32[]{:S(2)}) collective-permute-start(f32[4,1024]{1,0:T(4,128)S(1)} %get-tuple-element.50), channel_id=1, source_target_pairs={{0,1},{1,0},{2,3},{3,2},{4,5},{5,4},{6,7},{7,6},{8,9},{9,8},{10,11... | collective-permute-start | bytes 49160 | tf_op jit(solution)/shard_map/ppermute | solution.py:403
  17.9 0.0 collective-permute-start.5
  17.9 3.1 %collective-permute-done.4.corner_first_ref = f32[4,1024]{1,0:T(4,128)S(1)} collective-permute-done((f32[4,1024]{1,0:T(4,128)S(1)}, f32[4,1024]{1,0:T(4,128)S(1)}, u32[]{:S(2)}, u32[]{:S(2)}) %collective-permute-start.4) | collective-permute-done | bytes 16416 | tf_op jit(solution)/shard_map/ppermute | solution.py:403
  21.0 0.0 collective-permute-done.5.corner_second_ref
  21.0 0.3 %all-to-all-done.sketch_ref = f32[16,4,128]{2,1,0:T(4,128)S(1)} async-done(((f32[16,4,128]{2,1,0:T(4,128)}), f32[16,4,128]{2,1,0:T(4,128)S(1)}, u32[]{:S(2)}, u32[]{:S(2)}) %all-to-all-start) | async-done | bytes 32800 | tf_op jit(solution)/shard_map/all_to_all | solution.py:413
  21.4 1.1 %shard_map.72 = (f32[4,8,1024]{2,1,0:T(8,128)}, f32[4,8,1024]{2,1,0:T(8,128)}) custom-call(f32[16,4,128]{2,1,0:T(4,128)S(1)} %all-to-all-done.sketch_ref, f32[4,8,1024]{2,1,0:T(8,128)S(1)} %get-tuple-element.27.b_ref, f32[4,8,1024]{2,1,0:T(8,128)S(1)} %get-tuple-element.47.image_ref, f32[4,8,1024]{2,1,0:T(8,128)S(1)} %get-tuple-element.48.twice_ref, ...), custom_call_target="tpu_custom_call" | custom-call | tf_op jit(solution)/shard_map/pallas_call | solution.py:377
Async XLA Ops:
  2.1 7.2 %collective-permute-start = (f32[28,1024]{1,0:T(8,128)S(1)}, f32[28,1024]{1,0:T(8,128)S(1)}, u32[]{:S(2)}, u32[]{:S(2)}) collective-permute-start(f32[28,1024]{1,0:T(8,128)S(1)} %get-tuple-element.39), channel_id=1, source_target_pairs={{0,1},{1,0},{2,3},{3,2},{4,8},{5,9},{6,10},{7,11},{8,4},{9,5},{10,... | collective-permute-start | bytes 344072 | tf_op jit(solution)/shard_map/ppermute | solution.py:403
  5.2 4.1 %collective-permute-start.1 = (f32[28,1024]{1,0:T(8,128)S(1)}, f32[28,1024]{1,0:T(8,128)S(1)}, u32[]{:S(2)}, u32[]{:S(2)}) collective-permute-start(f32[28,1024]{1,0:T(8,128)S(1)} %get-tuple-element.40), channel_id=1, source_target_pairs={{0,4},{1,5},{2,6},{3,7},{4,0},{5,1},{6,2},{7,3},{8,12},{9,13},{10,... | collective-permute-start | bytes 344072 | tf_op jit(solution)/shard_map/ppermute | solution.py:403
  5.3 4.7 %collective-permute-start.2 = (f32[16,1024]{1,0:T(8,128)S(1)}, f32[16,1024]{1,0:T(8,128)S(1)}, u32[]{:S(2)}, u32[]{:S(2)}) collective-permute-start(f32[16,1024]{1,0:T(8,128)S(1)} %get-tuple-element.35.own_second_ref), channel_id=1, source_target_pairs={{0,4},{1,2},{2,1},{3,7},{4,0},{5,6},{6,5},{7,3},{8,12},{9,10},{10,... | collective-permute-start | bytes 196616 | tf_op jit(solution)/shard_map/ppermute | solution.py:403
  5.7 5.1 %collective-permute-start.3 = (f32[16,1024]{1,0:T(8,128)S(1)}, f32[16,1024]{1,0:T(8,128)S(1)}, u32[]{:S(2)}, u32[]{:S(2)}) collective-permute-start(f32[16,1024]{1,0:T(8,128)S(1)} %get-tuple-element.36.own_first_ref), channel_id=1, source_target_pairs={{0,1},{1,0},{2,3},{3,2},{4,5},{5,4},{6,7},{7,6},{8,9},{9,8},{10,11... | collective-permute-start | bytes 196616 | tf_op jit(solution)/shard_map/ppermute | solution.py:403
  12.5 8.9 %all-to-all-start = ((f32[16,4,128]{2,1,0:T(4,128)}), f32[16,4,128]{2,1,0:T(4,128)S(1)}, u32[]{:S(2)}, u32[]{:S(2)}) async-start(f32[16,4,128]{2,1,0:T(4,128)} %broadcast_in_dim.2), calls=%async_computation | async-start | bytes 65536 | tf_op jit(solution)/shard_map/all_to_all | solution.py:413
  17.3 3.7 %collective-permute-start.4 = (f32[4,1024]{1,0:T(4,128)S(1)}, f32[4,1024]{1,0:T(4,128)S(1)}, u32[]{:S(2)}, u32[]{:S(2)}) collective-permute-start(f32[4,1024]{1,0:T(4,128)S(1)} %get-tuple-element.50), channel_id=1, source_target_pairs={{0,1},{1,0},{2,3},{3,2},{4,5},{5,4},{6,7},{7,6},{8,9},{9,8},{10,11... | collective-permute-start | bytes 49160 | tf_op jit(solution)/shard_map/ppermute | solution.py:403
  17.9 3.2 %collective-permute-start.5 = (f32[4,1024]{1,0:T(4,128)S(1)}, f32[4,1024]{1,0:T(4,128)S(1)}, u32[]{:S(2)}, u32[]{:S(2)}) collective-permute-start(f32[4,1024]{1,0:T(4,128)S(1)} %get-tuple-element.51), channel_id=1, source_target_pairs={{0,4},{1,2},{2,1},{3,7},{4,0},{5,6},{6,5},{7,3},{8,12},{9,10},{10,... | collective-permute-start | bytes 49160 | tf_op jit(solution)/shard_map/ppermute | solution.py:403

commit v9 on v8

--- a/solution.py
+++ b/solution.py
@@ -81,7 +81,7 @@
         head = weighted.astype(jnp.bfloat16).astype(jnp.float32)
         coarse.append(head)
         fine.append(weighted - head)
-    for f, part in enumerate((coarse + fine) * 2):
+    for f, part in enumerate(coarse + fine):
         for t in range(cells_ref.shape[0]):
             cells_ref[t, pl.ds(start + f, draw.shape[0], stride=8), :] = part[
                 :, t * LANES : (t + 1) * LANES
@@ -91,6 +91,8 @@
 def masked_cells(mask, start, j, cells_ref):
     at = pl.ds(start + j * 8, 8)
     cells = jnp.concatenate([cells_ref[t, at, :] for t in range(cells_ref.shape[0])], axis=1)
+    filled = lax.broadcasted_iota(jnp.int32, cells.shape, 0) < 2 * PAIR
+    cells = jnp.where(filled, cells, pltpu.roll(cells, 2 * PAIR, 0))
     return jnp.concatenate([cells, cells], axis=0).astype(jnp.bfloat16) * mask
 
 

time: 22.7 us -> 22.6 us (level)
  no operation moved by 1% of the time
where the time goes in v9:
time: 22.6 us; the launch traced here: 22.5 us
  starting transfers between devices  11.7 us (52%)
  Pallas kernels  5.03 us (22%)
  waiting for transfers between devices  4.44 us (20%)
  between operations  0.66 us (3%)
  local copies, waits for them, and re-layouts  0.64 us (3%)
    ppermute x6, starting transfers between devices, swap(): return lax.ppermute(array, ('gx', 'gy'), pairs)  6.89 us
    pallas_call x5, Pallas kernels, call(): pl.pallas_call(kernel, out_shape=[shape if hasattr(shape, 'dtype') else j...  5.03 us
    all_to_all x1, starting transfers between devices, everyones(): return lax.all_to_all(copies, ('gx', 'gy'), 0, 0, axis_index_groups=[group])  4.8 us
    ppermute x6, waiting for transfers between devices, swap(): return lax.ppermute(array, ('gx', 'gy'), pairs)  4.09 us
    broadcast_in_dim x1, local copies, waits for them, and re-layouts, everyones(): copies = jnp.broadcast_to(sketch[None], (nx * ny,) + sketch.shape)  0.64 us
  transfers between devices with their start and end apart: 7, of which 3 were waited for; matrix products, arithmetic and copies ran while one was open for 0% of the time, Pallas kernels for 7%

profile of v9, /device:TPU:0, one launch (start us, length us, event | category | flops | bytes accessed | tf_op | source)
XLA Modules:
  0.0 22.5 jit_solution(7918929144121173679)
XLA Ops:
  0.6 1.5 %shard_map.68 = (f32[4,8,1024]{2,1,0:T(8,128)S(1)}, f32[4,8,1024]{2,1,0:T(8,128)S(1)}, f32[4,8,1024]{2,1,0:T(8,128)S(1)}, f32[4,8,1024]{2,1,0:T(8,128)S(1)}, f32...) custom-call(f32[4,8,1024]{2,1,0:T(8,128)} %b_hbm.1, ...), custom_call_target="tpu_custom_call" | custom-call | tf_op jit(solution)/shard_map/pallas_call | solution.py:379
  2.1 3.1 %collective-permute-start = (f32[28,1024]{1,0:T(8,128)S(1)}, f32[28,1024]{1,0:T(8,128)S(1)}, u32[]{:S(2)}, u32[]{:S(2)}) collective-permute-start(f32[28,1024]{1,0:T(8,128)S(1)} %get-tuple-element.39), channel_id=1, source_target_pairs={{0,1},{1,0},{2,3},{3,2},{4,8},{5,9},{6,10},{7,11},{8,4},{9,5},{10,... | collective-permute-start | bytes 344072 | tf_op jit(solution)/shard_map/ppermute | solution.py:405
  5.2 0.1 collective-permute-start.1
  5.3 0.5 %collective-permute-start.2 = (f32[16,1024]{1,0:T(8,128)S(1)}, f32[16,1024]{1,0:T(8,128)S(1)}, u32[]{:S(2)}, u32[]{:S(2)}) collective-permute-start(f32[16,1024]{1,0:T(8,128)S(1)} %get-tuple-element.35.own_second_ref), channel_id=1, source_target_pairs={{0,4},{1,2},{2,1},{3,7},{4,0},{5,6},{6,5},{7,3},{8,12},{9,10},{10,... | collective-permute-start | bytes 196616 | tf_op jit(solution)/shard_map/ppermute | solution.py:405
  5.7 2.7 %collective-permute-start.3 = (f32[16,1024]{1,0:T(8,128)S(1)}, f32[16,1024]{1,0:T(8,128)S(1)}, u32[]{:S(2)}, u32[]{:S(2)}) collective-permute-start(f32[16,1024]{1,0:T(8,128)S(1)} %get-tuple-element.36.own_first_ref), channel_id=1, source_target_pairs={{0,1},{1,0},{2,3},{3,2},{4,5},{5,4},{6,7},{7,6},{8,9},{9,8},{10,11... | collective-permute-start | bytes 196616 | tf_op jit(solution)/shard_map/ppermute | solution.py:405
  8.4 0.9 %shard_map.69 = (bf16[1024,1024]{1,0:T(8,128)(2,1)S(1)}, bf16[512,1024]{1,0:T(8,128)(2,1)S(1)}, f32[2,128]{1,0:T(2,128)S(1)}) custom-call(f32[4,8,1024]{2,1,0:T(8,128)S(1)} %get-tuple-element.27.b_ref, f32[4,8,1024]{2,1,0:T(8,128)S(1)} %get-tuple-element.31.draw_ref, f32[4,8,1024]{2,1,0:T(8,128)S(1)} %get-tuple-element.32.slot_ref), custom_call_target="tpu_custom_call" | custom-call | flops 25165824 | tf_op jit(solution)/shard_map/pallas_call | solution.py:379
  9.3 0.0 collective-permute-done.got_second_ref.x_second_ref
  9.3 0.0 collective-permute-done.1.got_first_ref.x_first_ref
  9.3 0.6 %shard_map.70 = (f32[6,8,1024]{2,1,0:T(8,128)S(1)}, f32[5,8,1024]{2,1,0:T(8,128)S(1)}, f32[4,8,1024]{2,1,0:T(8,128)S(1)}, f32[16,32]{1,0:T(8,128)S(1)}) custom-call(f32[4,8,1024]{2,1,0:T(8,128)S(1)} %get-tuple-element.27.b_ref, f32[4,8,1024]{2,1,0:T(8,128)S(1)} %get-tuple-element.37.cond_ref, f32[4,8,1024]{2,1,0:T(8,128)S(1)} %get-tuple-element.28.cap_ref, ...), custom_call_target="tpu_custom_call" | custom-call | flops 25165824 | tf_op jit(solution)/shard_map/pallas_call | solution.py:379
  9.9 0.0 collective-permute-done.2.y_second_ref
  9.9 0.9 %collective-permute-done.3.y_first_ref = f32[16,1024]{1,0:T(8,128)S(1)} collective-permute-done((f32[16,1024]{1,0:T(8,128)S(1)}, f32[16,1024]{1,0:T(8,128)S(1)}, u32[]{:S(2)}, u32[]{:S(2)}) %collective-permute-start.3) | collective-permute-done | bytes 65568 | tf_op jit(solution)/shard_map/ppermute | solution.py:405
  10.8 1.0 %shard_map.71 = (f32[4,8,1024]{2,1,0:T(8,128)S(1)}, f32[4,8,1024]{2,1,0:T(8,128)S(1)}, f32[4,128]{1,0:T(4,128)S(1)}, f32[4,1024]{1,0:T(4,128)S(1)}, f32[4,1024]{1,0:T(4,128)S(1)}, /*index=5*/f32[24,1024]{1,0:T(8,128)S(1)}) custom-call(f32[4,8,1024]{2,1,0:T(8,128)S(1)} %get-tuple-element.27.b_ref, f32[4,8,1024]{2,1,0:T(8,128)S(1)} %get-tuple-element.28.cap_ref, ...), custom_call_target="tpu_custom_call" | custom-call | flops 25165824 | tf_op jit(solution)/shard_map/pallas_call | solution.py:379
  11.8 0.6 %broadcast_in_dim.2 = f32[16,4,128]{2,1,0:T(4,128)} broadcast(f32[4,128]{1,0:T(4,128)S(1)} %get-tuple-element.46), dimensions={1,2} | broadcast | bytes 34816 | tf_op jit(solution)/shard_map/broadcast_in_dim | solution.py:414
  12.4 4.8 %all-to-all-start = ((f32[16,4,128]{2,1,0:T(4,128)}), f32[16,4,128]{2,1,0:T(4,128)S(1)}, u32[]{:S(2)}, u32[]{:S(2)}) async-start(f32[16,4,128]{2,1,0:T(4,128)} %broadcast_in_dim.2), calls=%async_computation | async-start | bytes 65536 | tf_op jit(solution)/shard_map/all_to_all | solution.py:415
  17.2 0.6 %collective-permute-start.4 = (f32[4,1024]{1,0:T(4,128)S(1)}, f32[4,1024]{1,0:T(4,128)S(1)}, u32[]{:S(2)}, u32[]{:S(2)}) collective-permute-start(f32[4,1024]{1,0:T(4,128)S(1)} %get-tuple-element.50), channel_id=1, source_target_pairs={{0,1},{1,0},{2,3},{3,2},{4,5},{5,4},{6,7},{7,6},{8,9},{9,8},{10,11... | collective-permute-start | bytes 49160 | tf_op jit(solution)/shard_map/ppermute | solution.py:405
  17.8 0.0 collective-permute-start.5
  17.8 3.1 %collective-permute-done.4.corner_first_ref = f32[4,1024]{1,0:T(4,128)S(1)} collective-permute-done((f32[4,1024]{1,0:T(4,128)S(1)}, f32[4,1024]{1,0:T(4,128)S(1)}, u32[]{:S(2)}, u32[]{:S(2)}) %collective-permute-start.4) | collective-permute-done | bytes 16416 | tf_op jit(solution)/shard_map/ppermute | solution.py:405
  21.0 0.0 collective-permute-done.5.corner_second_ref
  21.0 0.3 %all-to-all-done.sketch_ref = f32[16,4,128]{2,1,0:T(4,128)S(1)} async-done(((f32[16,4,128]{2,1,0:T(4,128)}), f32[16,4,128]{2,1,0:T(4,128)S(1)}, u32[]{:S(2)}, u32[]{:S(2)}) %all-to-all-start) | async-done | bytes 32800 | tf_op jit(solution)/shard_map/all_to_all | solution.py:415
  21.3 1.1 %shard_map.72 = (f32[4,8,1024]{2,1,0:T(8,128)}, f32[4,8,1024]{2,1,0:T(8,128)}) custom-call(f32[16,4,128]{2,1,0:T(4,128)S(1)} %all-to-all-done.sketch_ref, f32[4,8,1024]{2,1,0:T(8,128)S(1)} %get-tuple-element.27.b_ref, f32[4,8,1024]{2,1,0:T(8,128)S(1)} %get-tuple-element.47.image_ref, f32[4,8,1024]{2,1,0:T(8,128)S(1)} %get-tuple-element.48.twice_ref, ...), custom_call_target="tpu_custom_call" | custom-call | tf_op jit(solution)/shard_map/pallas_call | solution.py:379
Async XLA Ops:
  2.1 7.2 %collective-permute-start = (f32[28,1024]{1,0:T(8,128)S(1)}, f32[28,1024]{1,0:T(8,128)S(1)}, u32[]{:S(2)}, u32[]{:S(2)}) collective-permute-start(f32[28,1024]{1,0:T(8,128)S(1)} %get-tuple-element.39), channel_id=1, source_target_pairs={{0,1},{1,0},{2,3},{3,2},{4,8},{5,9},{6,10},{7,11},{8,4},{9,5},{10,... | collective-permute-start | bytes 344072 | tf_op jit(solution)/shard_map/ppermute | solution.py:405
  5.2 4.1 %collective-permute-start.1 = (f32[28,1024]{1,0:T(8,128)S(1)}, f32[28,1024]{1,0:T(8,128)S(1)}, u32[]{:S(2)}, u32[]{:S(2)}) collective-permute-start(f32[28,1024]{1,0:T(8,128)S(1)} %get-tuple-element.40), channel_id=1, source_target_pairs={{0,4},{1,5},{2,6},{3,7},{4,0},{5,1},{6,2},{7,3},{8,12},{9,13},{10,... | collective-permute-start | bytes 344072 | tf_op jit(solution)/shard_map/ppermute | solution.py:405
  5.3 4.6 %collective-permute-start.2 = (f32[16,1024]{1,0:T(8,128)S(1)}, f32[16,1024]{1,0:T(8,128)S(1)}, u32[]{:S(2)}, u32[]{:S(2)}) collective-permute-start(f32[16,1024]{1,0:T(8,128)S(1)} %get-tuple-element.35.own_second_ref), channel_id=1, source_target_pairs={{0,4},{1,2},{2,1},{3,7},{4,0},{5,6},{6,5},{7,3},{8,12},{9,10},{10,... | collective-permute-start | bytes 196616 | tf_op jit(solution)/shard_map/ppermute | solution.py:405
  5.7 5.1 %collective-permute-start.3 = (f32[16,1024]{1,0:T(8,128)S(1)}, f32[16,1024]{1,0:T(8,128)S(1)}, u32[]{:S(2)}, u32[]{:S(2)}) collective-permute-start(f32[16,1024]{1,0:T(8,128)S(1)} %get-tuple-element.36.own_first_ref), channel_id=1, source_target_pairs={{0,1},{1,0},{2,3},{3,2},{4,5},{5,4},{6,7},{7,6},{8,9},{9,8},{10,11... | collective-permute-start | bytes 196616 | tf_op jit(solution)/shard_map/ppermute | solution.py:405
  12.4 8.9 %all-to-all-start = ((f32[16,4,128]{2,1,0:T(4,128)}), f32[16,4,128]{2,1,0:T(4,128)S(1)}, u32[]{:S(2)}, u32[]{:S(2)}) async-start(f32[16,4,128]{2,1,0:T(4,128)} %broadcast_in_dim.2), calls=%async_computation | async-start | bytes 65536 | tf_op jit(solution)/shard_map/all_to_all | solution.py:415
  17.2 3.7 %collective-permute-start.4 = (f32[4,1024]{1,0:T(4,128)S(1)}, f32[4,1024]{1,0:T(4,128)S(1)}, u32[]{:S(2)}, u32[]{:S(2)}) collective-permute-start(f32[4,1024]{1,0:T(4,128)S(1)} %get-tuple-element.50), channel_id=1, source_target_pairs={{0,1},{1,0},{2,3},{3,2},{4,5},{5,4},{6,7},{7,6},{8,9},{9,8},{10,11... | collective-permute-start | bytes 49160 | tf_op jit(solution)/shard_map/ppermute | solution.py:405
  17.8 3.2 %collective-permute-start.5 = (f32[4,1024]{1,0:T(4,128)S(1)}, f32[4,1024]{1,0:T(4,128)S(1)}, u32[]{:S(2)}, u32[]{:S(2)}) collective-permute-start(f32[4,1024]{1,0:T(4,128)S(1)} %get-tuple-element.51), channel_id=1, source_target_pairs={{0,4},{1,2},{2,1},{3,7},{4,0},{5,6},{6,5},{7,3},{8,12},{9,10},{10,... | collective-permute-start | bytes 49160 | tf_op jit(solution)/shard_map/ppermute | solution.py:405

commit v10 on v9

--- a/solution.py
+++ b/solution.py
@@ -225,7 +225,8 @@
 
 def inside_kernel(
     b_ref, cond_ref, cap_ref, y_link_ref, z_link_ref, inner_ref, draw_ref, low_ref, high_ref,
-    got_second_ref, got_first_ref, wide_ref, x_link_ref, beside_ref, sketch_ref, cells_ref,
+    got_second_ref, got_first_ref, wide_ref, x_link_ref, beside_ref, sketch_ref, corner_first_ref,
+    cells_ref,
 ):
     planes, rows = b_ref.shape[:2]
     (image_low, image_high), (b_low, b_high), (c_low, c_high) = (
@@ -236,6 +237,7 @@
     c_low, c_high = jnp.where(below, c_low, 0.0), jnp.where(above, c_high, 0.0)
     for k, plane in enumerate((b_low, b_high, c_low, c_high)):
         beside_ref[k] = plane
+        corner_first_ref[k : k + 1] = by_turn(plane[:1], plane[rows - 1 :], "gy")[0]
     conds = [c_low] + [cond_ref[i] for i in range(planes)] + [c_high]
     x_links = [link(conds[i], conds[i + 1]) for i in range(planes + 1)]
     for i, conductance in enumerate(x_links):
@@ -258,8 +260,8 @@
 def third_kernel(
     b_ref, cap_ref, y_link_ref, z_link_ref, draw_ref, low_ref, high_ref, own_second_ref,
     own_first_ref, wide_ref, x_link_ref, beside_ref, x_second_ref, x_first_ref, y_second_ref,
-    y_first_ref, b_sketch_ref, inside_ref, image_ref, twice_ref, sketch_ref, corner_first_ref,
-    corner_second_ref, ends_ref, cells_ref, extra_ref,
+    y_first_ref, b_sketch_ref, inside_ref, image_ref, twice_ref, sketch_ref, corner_second_ref,
+    ends_ref, cells_ref, extra_ref,
 ):
     planes, rows, depth = b_ref.shape
     index = lax.broadcasted_iota(jnp.int32, (rows, depth), 0)
@@ -324,10 +326,7 @@
     sketch_ref[:1] = b_sketch_ref[:1]
     sketch_ref[1 + PAIR :] = b_sketch_ref[:1]
     for k, plane in enumerate(b_beside + c_beside):
-        at = slice(k, k + 1)
-        corner_first_ref[at], corner_second_ref[at] = by_turn(
-            plane[:1], plane[rows - 1 :], "gy"
-        )
+        corner_second_ref[k : k + 1] = by_turn(plane[:1], plane[rows - 1 :], "gy")[1]
 
 
 def last_kernel(
@@ -446,16 +445,16 @@
     *hots, b_sketch = call(
         slot_kernel, [*hots, (PAIR, SKETCH)], b, draw, slots, scratch=[cells], flops=work
     )
-    image_wide, x_link, beside, inside = call(
+    image_wide, x_link, beside, inside, first = call(
         inside_kernel,
-        [wide, (planes + 1, rows, depth), (4, rows, depth), total],
+        [wide, (planes + 1, rows, depth), (4, rows, depth), total, corner],
         b, cond, cap, y_link, z_link, inner, draw, *hots, *got_x,
         scratch=[cells],
         flops=work,
     )
-    image, twice, sketch, first, second, ends = call(
+    image, twice, sketch, second, ends = call(
         third_kernel,
-        [block, block, (FIELDS + 1, SKETCH), corner, corner, (24, depth)],
+        [block, block, (FIELDS + 1, SKETCH), corner, (24, depth)],
         b, cap, y_link, z_link, draw, *hots, y_second, y_first, image_wide, x_link, beside,
         *got_x, *got_y, b_sketch, inside,
         scratch=[cells, pltpu.VMEM((3, 8, depth), jnp.float32)],

time: 22.6 us -> 22.6 us (level)
  starting transfers between devices: 11.7 us -> 12.1 us
  waiting for transfers between devices: 4.44 us -> 4.05 us
    ppermute x6, starting transfers between devices: 6.89 us -> 7.28 us  [swap(): return lax.ppermute(array, ('gx', 'gy'), pairs)]
    ppermute x6, waiting for transfers between devices: 4.09 us -> 3.79 us  [swap(): return lax.ppermute(array, ('gx', 'gy'), pairs)]
  transfers between devices with their start and end apart: 7 -> 7, of which waited for: 3 -> 4; matrix products, arithmetic and copies ran while one was open for 0% -> 0% of each run, Pallas kernels for 7% -> 7%
where the time goes in v10:
time: 22.6 us; the launch traced here: 22.4 us
  starting transfers between devices  12.1 us (54%)
  Pallas kernels  5.01 us (22%)
  waiting for transfers between devices  4.05 us (18%)
  between operations  0.66 us (3%)
  local copies, waits for them, and re-layouts  0.64 us (3%)
    ppermute x6, starting transfers between devices, swap(): return lax.ppermute(array, ('gx', 'gy'), pairs)  7.28 us
    pallas_call x5, Pallas kernels, call(): pl.pallas_call(kernel, out_shape=[shape if hasattr(shape, 'dtype') else j...  5.01 us
    all_to_all x1, starting transfers between devices, everyones(): return lax.all_to_all(copies, ('gx', 'gy'), 0, 0, axis_index_groups=[group])  4.8 us
    ppermute x6, waiting for transfers between devices, swap(): return lax.ppermute(array, ('gx', 'gy'), pairs)  3.79 us
    broadcast_in_dim x1, local copies, waits for them, and re-layouts, everyones(): copies = jnp.broadcast_to(sketch[None], (nx * ny,) + sketch.shape)  0.64 us
  transfers between devices with their start and end apart: 7, of which 4 were waited for; matrix products, arithmetic and copies ran while one was open for 0% of the time, Pallas kernels for 7%

profile of v10, /device:TPU:0, one launch (start us, length us, event | category | flops | bytes accessed | tf_op | source)
XLA Modules:
  0.0 22.4 jit_solution(4451444652487889100)
XLA Ops:
  0.6 1.5 %shard_map.68 = (f32[4,8,1024]{2,1,0:T(8,128)S(1)}, f32[4,8,1024]{2,1,0:T(8,128)S(1)}, f32[4,8,1024]{2,1,0:T(8,128)S(1)}, f32[4,8,1024]{2,1,0:T(8,128)S(1)}, f32...) custom-call(f32[4,8,1024]{2,1,0:T(8,128)} %b_hbm.1, ...), custom_call_target="tpu_custom_call" | custom-call | tf_op jit(solution)/shard_map/pallas_call | solution.py:378
  2.1 3.1 %collective-permute-start = (f32[28,1024]{1,0:T(8,128)S(1)}, f32[28,1024]{1,0:T(8,128)S(1)}, u32[]{:S(2)}, u32[]{:S(2)}) collective-permute-start(f32[28,1024]{1,0:T(8,128)S(1)} %get-tuple-element.39), channel_id=1, source_target_pairs={{0,1},{1,0},{2,3},{3,2},{4,8},{5,9},{6,10},{7,11},{8,4},{9,5},{10,... | collective-permute-start | bytes 344072 | tf_op jit(solution)/shard_map/ppermute | solution.py:404
  5.2 0.1 collective-permute-start.1
  5.3 0.5 %collective-permute-start.2 = (f32[16,1024]{1,0:T(8,128)S(1)}, f32[16,1024]{1,0:T(8,128)S(1)}, u32[]{:S(2)}, u32[]{:S(2)}) collective-permute-start(f32[16,1024]{1,0:T(8,128)S(1)} %get-tuple-element.35.own_second_ref), channel_id=1, source_target_pairs={{0,4},{1,2},{2,1},{3,7},{4,0},{5,6},{6,5},{7,3},{8,12},{9,10},{10,... | collective-permute-start | bytes 196616 | tf_op jit(solution)/shard_map/ppermute | solution.py:404
  5.7 2.7 %collective-permute-start.3 = (f32[16,1024]{1,0:T(8,128)S(1)}, f32[16,1024]{1,0:T(8,128)S(1)}, u32[]{:S(2)}, u32[]{:S(2)}) collective-permute-start(f32[16,1024]{1,0:T(8,128)S(1)} %get-tuple-element.36.own_first_ref), channel_id=1, source_target_pairs={{0,1},{1,0},{2,3},{3,2},{4,5},{5,4},{6,7},{7,6},{8,9},{9,8},{10,11... | collective-permute-start | bytes 196616 | tf_op jit(solution)/shard_map/ppermute | solution.py:404
  8.4 0.9 %shard_map.69 = (bf16[1024,1024]{1,0:T(8,128)(2,1)S(1)}, bf16[512,1024]{1,0:T(8,128)(2,1)S(1)}, f32[2,128]{1,0:T(2,128)S(1)}) custom-call(f32[4,8,1024]{2,1,0:T(8,128)S(1)} %get-tuple-element.27.b_ref, f32[4,8,1024]{2,1,0:T(8,128)S(1)} %get-tuple-element.31.draw_ref, f32[4,8,1024]{2,1,0:T(8,128)S(1)} %get-tuple-element.32.slot_ref), custom_call_target="tpu_custom_call" | custom-call | flops 25165824 | tf_op jit(solution)/shard_map/pallas_call | solution.py:378
  9.3 0.0 collective-permute-done.got_second_ref.x_second_ref
  9.3 0.0 collective-permute-done.1.got_first_ref.x_first_ref
  9.3 0.6 %shard_map.70 = (f32[6,8,1024]{2,1,0:T(8,128)S(1)}, f32[5,8,1024]{2,1,0:T(8,128)S(1)}, f32[4,8,1024]{2,1,0:T(8,128)S(1)}, f32[16,32]{1,0:T(8,128)S(1)}, f32[4,1024]{1,0:T(4,128)S(1)}) custom-call(f32[4,8,1024]{2,1,0:T(8,128)S(1)} %get-tuple-element.27.b_ref, f32[4,8,1024]{2,1,0:T(8,128)S(1)} %get-tuple-element.37.cond_ref, ...), custom_call_target="tpu_custom_call" | custom-call | flops 25165824 | tf_op jit(solution)/shard_map/pallas_call | solution.py:378
  9.9 0.0 collective-permute-done.2.y_second_ref
  9.9 0.9 %collective-permute-done.3.y_first_ref = f32[16,1024]{1,0:T(8,128)S(1)} collective-permute-done((f32[16,1024]{1,0:T(8,128)S(1)}, f32[16,1024]{1,0:T(8,128)S(1)}, u32[]{:S(2)}, u32[]{:S(2)}) %collective-permute-start.3) | collective-permute-done | bytes 65568 | tf_op jit(solution)/shard_map/ppermute | solution.py:404
  10.8 0.9 %shard_map.71 = (f32[4,8,1024]{2,1,0:T(8,128)S(1)}, f32[4,8,1024]{2,1,0:T(8,128)S(1)}, f32[4,128]{1,0:T(4,128)S(1)}, f32[4,1024]{1,0:T(4,128)S(1)}, f32[24,1024]{1,0:T(8,128)S(1)}) custom-call(f32[4,8,1024]{2,1,0:T(8,128)S(1)} %get-tuple-element.27.b_ref, f32[4,8,1024]{2,1,0:T(8,128)S(1)} %get-tuple-element.28.cap_ref, ...), custom_call_target="tpu_custom_call" | custom-call | flops 25165824 | tf_op jit(solution)/shard_map/pallas_call | solution.py:378
  11.8 0.6 %broadcast_in_dim.2 = f32[16,4,128]{2,1,0:T(4,128)} broadcast(f32[4,128]{1,0:T(4,128)S(1)} %get-tuple-element.46), dimensions={1,2} | broadcast | bytes 34816 | tf_op jit(solution)/shard_map/broadcast_in_dim | solution.py:413
  12.4 4.8 %all-to-all-start = ((f32[16,4,128]{2,1,0:T(4,128)}), f32[16,4,128]{2,1,0:T(4,128)S(1)}, u32[]{:S(2)}, u32[]{:S(2)}) async-start(f32[16,4,128]{2,1,0:T(4,128)} %broadcast_in_dim.2), calls=%async_computation | async-start | bytes 65536 | tf_op jit(solution)/shard_map/all_to_all | solution.py:414
  17.2 0.1 collective-permute-start.5
  17.3 0.9 %collective-permute-start.4 = (f32[4,1024]{1,0:T(4,128)S(1)}, f32[4,1024]{1,0:T(4,128)S(1)}, u32[]{:S(2)}, u32[]{:S(2)}) collective-permute-start(f32[4,1024]{1,0:T(4,128)S(1)} %get-tuple-element.50), channel_id=1, source_target_pairs={{0,1},{1,0},{2,3},{3,2},{4,5},{5,4},{6,7},{7,6},{8,9},{9,8},{10,11... | collective-permute-start | bytes 49160 | tf_op jit(solution)/shard_map/ppermute | solution.py:404
  18.2 0.2 collective-permute-done.5.corner_second_ref
  18.4 2.6 %collective-permute-done.4.corner_first_ref = f32[4,1024]{1,0:T(4,128)S(1)} collective-permute-done((f32[4,1024]{1,0:T(4,128)S(1)}, f32[4,1024]{1,0:T(4,128)S(1)}, u32[]{:S(2)}, u32[]{:S(2)}) %collective-permute-start.4) | collective-permute-done | bytes 16416 | tf_op jit(solution)/shard_map/ppermute | solution.py:404
  21.0 0.3 %all-to-all-done.sketch_ref = f32[16,4,128]{2,1,0:T(4,128)S(1)} async-done(((f32[16,4,128]{2,1,0:T(4,128)}), f32[16,4,128]{2,1,0:T(4,128)S(1)}, u32[]{:S(2)}, u32[]{:S(2)}) %all-to-all-start) | async-done | bytes 32800 | tf_op jit(solution)/shard_map/all_to_all | solution.py:414
  21.3 1.1 %shard_map.72 = (f32[4,8,1024]{2,1,0:T(8,128)}, f32[4,8,1024]{2,1,0:T(8,128)}) custom-call(f32[16,4,128]{2,1,0:T(4,128)S(1)} %all-to-all-done.sketch_ref, f32[4,8,1024]{2,1,0:T(8,128)S(1)} %get-tuple-element.27.b_ref, f32[4,8,1024]{2,1,0:T(8,128)S(1)} %get-tuple-element.47.image_ref, f32[4,8,1024]{2,1,0:T(8,128)S(1)} %get-tuple-element.48.twice_ref, ...), custom_call_target="tpu_custom_call" | custom-call | tf_op jit(solution)/shard_map/pallas_call | solution.py:378
Async XLA Ops:
  2.1 7.2 %collective-permute-start = (f32[28,1024]{1,0:T(8,128)S(1)}, f32[28,1024]{1,0:T(8,128)S(1)}, u32[]{:S(2)}, u32[]{:S(2)}) collective-permute-start(f32[28,1024]{1,0:T(8,128)S(1)} %get-tuple-element.39), channel_id=1, source_target_pairs={{0,1},{1,0},{2,3},{3,2},{4,8},{5,9},{6,10},{7,11},{8,4},{9,5},{10,... | collective-permute-start | bytes 344072 | tf_op jit(solution)/shard_map/ppermute | solution.py:404
  5.2 4.1 %collective-permute-start.1 = (f32[28,1024]{1,0:T(8,128)S(1)}, f32[28,1024]{1,0:T(8,128)S(1)}, u32[]{:S(2)}, u32[]{:S(2)}) collective-permute-start(f32[28,1024]{1,0:T(8,128)S(1)} %get-tuple-element.40), channel_id=1, source_target_pairs={{0,4},{1,5},{2,6},{3,7},{4,0},{5,1},{6,2},{7,3},{8,12},{9,13},{10,... | collective-permute-start | bytes 344072 | tf_op jit(solution)/shard_map/ppermute | solution.py:404
  5.3 4.6 %collective-permute-start.2 = (f32[16,1024]{1,0:T(8,128)S(1)}, f32[16,1024]{1,0:T(8,128)S(1)}, u32[]{:S(2)}, u32[]{:S(2)}) collective-permute-start(f32[16,1024]{1,0:T(8,128)S(1)} %get-tuple-element.35.own_second_ref), channel_id=1, source_target_pairs={{0,4},{1,2},{2,1},{3,7},{4,0},{5,6},{6,5},{7,3},{8,12},{9,10},{10,... | collective-permute-start | bytes 196616 | tf_op jit(solution)/shard_map/ppermute | solution.py:404
  5.7 5.1 %collective-permute-start.3 = (f32[16,1024]{1,0:T(8,128)S(1)}, f32[16,1024]{1,0:T(8,128)S(1)}, u32[]{:S(2)}, u32[]{:S(2)}) collective-permute-start(f32[16,1024]{1,0:T(8,128)S(1)} %get-tuple-element.36.own_first_ref), channel_id=1, source_target_pairs={{0,1},{1,0},{2,3},{3,2},{4,5},{5,4},{6,7},{7,6},{8,9},{9,8},{10,11... | collective-permute-start | bytes 196616 | tf_op jit(solution)/shard_map/ppermute | solution.py:404
  12.4 8.9 %all-to-all-start = ((f32[16,4,128]{2,1,0:T(4,128)}), f32[16,4,128]{2,1,0:T(4,128)S(1)}, u32[]{:S(2)}, u32[]{:S(2)}) async-start(f32[16,4,128]{2,1,0:T(4,128)} %broadcast_in_dim.2), calls=%async_computation | async-start | bytes 65536 | tf_op jit(solution)/shard_map/all_to_all | solution.py:414
  17.2 1.2 %collective-permute-start.5 = (f32[4,1024]{1,0:T(4,128)S(1)}, f32[4,1024]{1,0:T(4,128)S(1)}, u32[]{:S(2)}, u32[]{:S(2)}) collective-permute-start(f32[4,1024]{1,0:T(4,128)S(1)} %get-tuple-element.51), channel_id=1, source_target_pairs={{0,4},{1,2},{2,1},{3,7},{4,0},{5,6},{6,5},{7,3},{8,12},{9,10},{10,... | collective-permute-start | bytes 49160 | tf_op jit(solution)/shard_map/ppermute | solution.py:404
  17.3 3.7 %collective-permute-start.4 = (f32[4,1024]{1,0:T(4,128)S(1)}, f32[4,1024]{1,0:T(4,128)S(1)}, u32[]{:S(2)}, u32[]{:S(2)}) collective-permute-start(f32[4,1024]{1,0:T(4,128)S(1)} %get-tuple-element.50), channel_id=1, source_target_pairs={{0,1},{1,0},{2,3},{3,2},{4,5},{5,4},{6,7},{7,6},{8,9},{9,8},{10,11... | collective-permute-start | bytes 49160 | tf_op jit(solution)/shard_map/ppermute | solution.py:404

commit v11 on v9

--- a/solution.py
+++ b/solution.py
@@ -225,7 +225,8 @@
 
 def inside_kernel(
     b_ref, cond_ref, cap_ref, y_link_ref, z_link_ref, inner_ref, draw_ref, low_ref, high_ref,
-    got_second_ref, got_first_ref, wide_ref, x_link_ref, beside_ref, sketch_ref, cells_ref,
+    got_second_ref, got_first_ref, wide_ref, x_link_ref, beside_ref, sketch_ref, end_low_ref,
+    end_high_ref, cells_ref,
 ):
     planes, rows = b_ref.shape[:2]
     (image_low, image_high), (b_low, b_high), (c_low, c_high) = (
@@ -253,12 +254,20 @@
     chosen = reached(rows)[1]
     cells = [((images[i + 1], twice[i]), draw_ref[i], chosen) for i in range(planes)]
     sketch_ref[...] = sketch_rows(cells, low_ref, high_ref, cells_ref)
+    each = HIGH * 2 * PAIR
+    tails = by_turn(got_first_ref[3 * rows :], got_second_ref[3 * rows :], "gx")
+    for side in range(2):
+        for end, tail in enumerate(tails):
+            at = 2 * side + end
+            low, high = parts_of(tail[2 + side :][:1])
+            end_low_ref[at * LOW : (at + 1) * LOW] = one_hot(low, 0, LOW, 1)
+            end_high_ref[at * each : (at + 1) * each] = one_hot(high, 0, HIGH, 2 * PAIR)
 
 
 def third_kernel(
     b_ref, cap_ref, y_link_ref, z_link_ref, draw_ref, low_ref, high_ref, own_second_ref,
     own_first_ref, wide_ref, x_link_ref, beside_ref, x_second_ref, x_first_ref, y_second_ref,
-    y_first_ref, b_sketch_ref, inside_ref, image_ref, twice_ref, sketch_ref, corner_first_ref,
+    y_first_ref, b_sketch_ref, inside_ref, end_low_ref, end_high_ref, image_ref, twice_ref, sketch_ref, corner_first_ref,
     corner_second_ref, ends_ref, cells_ref, extra_ref,
 ):
     planes, rows, depth = b_ref.shape
@@ -288,7 +297,7 @@
             images[i + 1] = images[i + 1] + jnp.where(index == j, y_flow[at], 0.0)
             beside.append((i, jnp.where(index == j, y_link[at], 0.0), beyond[at]))
         for end, (i, x_link, x_flow) in enumerate(x_ends):
-            line_at, at = slice(i, i + 1), 4 * side + 2 * end
+            line_at, at = slice(i, i + 1), 2 * side + end
             tail = x_tails[end]
             values = -x_link[row] * y_flow[line_at], tail[side:][:1], tail[2 + side :][:1]
             for k, value in enumerate(values):
@@ -296,7 +305,7 @@
             tail = line[3 * planes :]
             values = -y_link[line_at] * x_flow[row], tail[end:][:1], tail[2 + end :][:1]
             for k, value in enumerate(values):
-                extra_ref[k, at + 1 : at + 2] = value
+                extra_ref[k, at + 4 : at + 5] = value
             at = 6 * (2 * side + end)
             values = x_link[row], b_beside[end][row], c_beside[end][row]
             values += y_link[line_at], b_line[line_at], c_line[line_at]
@@ -316,10 +325,15 @@
     put_cells((jnp.zeros((8, depth), jnp.float32), extra_ref[0]), extra_ref[1], start, cells_ref)
     low, high = parts_of(extra_ref[2])
     left, right = [], []
+    each = HIGH * 2 * PAIR
     for j in range(8):
-        mask = one_hot(high, j, HIGH, 2 * PAIR)
+        if j < 4:
+            mask = end_high_ref[j * each : (j + 1) * each]
+            hot = end_low_ref[j * LOW : (j + 1) * LOW]
+        else:
+            mask, hot = one_hot(high, j, HIGH, 2 * PAIR), one_hot(low, j, LOW, 1)
         left.append(masked_cells(mask, start, j, cells_ref))
-        right.append(one_hot(low, j, LOW, 1))
+        right.append(hot)
     sketch_ref[1 : 1 + PAIR] = as_sketch(total + product(left, right))
     sketch_ref[:1] = b_sketch_ref[:1]
     sketch_ref[1 + PAIR :] = b_sketch_ref[:1]
@@ -425,6 +439,10 @@
         jax.ShapeDtypeStruct((planes * rows * count, depth), jnp.bfloat16)
         for count in (LOW, HIGH * 2 * PAIR)
     ]
+    end_hots = [
+        jax.ShapeDtypeStruct((4 * count, depth), jnp.bfloat16)
+        for count in (LOW, HIGH * 2 * PAIR)
+    ]
     work = b.size * SKETCH * 6
     b, cond, cap, y_link, z_link, inner, draw, slots, x_first, x_second, y_first, y_second = call(
         first_kernel,
@@ -446,9 +464,9 @@
     *hots, b_sketch = call(
         slot_kernel, [*hots, (PAIR, SKETCH)], b, draw, slots, scratch=[cells], flops=work
     )
-    image_wide, x_link, beside, inside = call(
+    image_wide, x_link, beside, inside, *end_hots = call(
         inside_kernel,
-        [wide, (planes + 1, rows, depth), (4, rows, depth), total],
+        [wide, (planes + 1, rows, depth), (4, rows, depth), total, *end_hots],
         b, cond, cap, y_link, z_link, inner, draw, *hots, *got_x,
         scratch=[cells],
         flops=work,
@@ -457,7 +475,7 @@
         third_kernel,
         [block, block, (FIELDS + 1, SKETCH), corner, corner, (24, depth)],
         b, cap, y_link, z_link, draw, *hots, y_second, y_first, image_wide, x_link, beside,
-        *got_x, *got_y, b_sketch, inside,
+        *got_x, *got_y, b_sketch, inside, *end_hots,
         scratch=[cells, pltpu.VMEM((3, 8, depth), jnp.float32)],
         flops=work,
     )

time: 22.6 us -> 22.6 us (level)
  no operation moved by 1% of the time
where the time goes in v11:
time: 22.6 us; the launch traced here: 22.4 us
  starting transfers between devices  11.7 us (52%)
  Pallas kernels  5.07 us (22%)
  waiting for transfers between devices  4.39 us (19%)
  between operations  0.66 us (3%)
  local copies, waits for them, and re-layouts  0.64 us (3%)
    ppermute x6, starting transfers between devices, swap(): return lax.ppermute(array, ('gx', 'gy'), pairs)  6.89 us
    pallas_call x5, Pallas kernels, call(): pl.pallas_call(kernel, out_shape=[shape if hasattr(shape, 'dtype') else j...  5.07 us
    all_to_all x1, starting transfers between devices, everyones(): return lax.all_to_all(copies, ('gx', 'gy'), 0, 0, axis_index_groups=[group])  4.8 us
    ppermute x6, waiting for transfers between devices, swap(): return lax.ppermute(array, ('gx', 'gy'), pairs)  4.04 us
    broadcast_in_dim x1, local copies, waits for them, and re-layouts, everyones(): copies = jnp.broadcast_to(sketch[None], (nx * ny,) + sketch.shape)  0.64 us
  transfers between devices with their start and end apart: 7, of which 3 were waited for; matrix products, arithmetic and copies ran while one was open for 0% of the time, Pallas kernels for 7%

profile of v11, /device:TPU:0, one launch (start us, length us, event | category | flops | bytes accessed | tf_op | source)
XLA Modules:
  0.0 22.4 jit_solution(7494082800383990390)
XLA Ops:
  0.6 1.5 %shard_map.68 = (f32[4,8,1024]{2,1,0:T(8,128)S(1)}, f32[4,8,1024]{2,1,0:T(8,128)S(1)}, f32[4,8,1024]{2,1,0:T(8,128)S(1)}, f32[4,8,1024]{2,1,0:T(8,128)S(1)}, f32...) custom-call(f32[4,8,1024]{2,1,0:T(8,128)} %b_hbm.1, ...), custom_call_target="tpu_custom_call" | custom-call | tf_op jit(solution)/shard_map/pallas_call | solution.py:393
  2.1 3.1 %collective-permute-start = (f32[28,1024]{1,0:T(8,128)S(1)}, f32[28,1024]{1,0:T(8,128)S(1)}, u32[]{:S(2)}, u32[]{:S(2)}) collective-permute-start(f32[28,1024]{1,0:T(8,128)S(1)} %get-tuple-element.41), channel_id=1, source_target_pairs={{0,1},{1,0},{2,3},{3,2},{4,8},{5,9},{6,10},{7,11},{8,4},{9,5},{10,... | collective-permute-start | bytes 344072 | tf_op jit(solution)/shard_map/ppermute | solution.py:419
  5.2 0.1 collective-permute-start.1
  5.3 0.5 %collective-permute-start.2 = (f32[16,1024]{1,0:T(8,128)S(1)}, f32[16,1024]{1,0:T(8,128)S(1)}, u32[]{:S(2)}, u32[]{:S(2)}) collective-permute-start(f32[16,1024]{1,0:T(8,128)S(1)} %get-tuple-element.37.own_second_ref), channel_id=1, source_target_pairs={{0,4},{1,2},{2,1},{3,7},{4,0},{5,6},{6,5},{7,3},{8,12},{9,10},{10,... | collective-permute-start | bytes 196616 | tf_op jit(solution)/shard_map/ppermute | solution.py:419
  5.7 2.7 %collective-permute-start.3 = (f32[16,1024]{1,0:T(8,128)S(1)}, f32[16,1024]{1,0:T(8,128)S(1)}, u32[]{:S(2)}, u32[]{:S(2)}) collective-permute-start(f32[16,1024]{1,0:T(8,128)S(1)} %get-tuple-element.38.own_first_ref), channel_id=1, source_target_pairs={{0,1},{1,0},{2,3},{3,2},{4,5},{5,4},{6,7},{7,6},{8,9},{9,8},{10,11... | collective-permute-start | bytes 196616 | tf_op jit(solution)/shard_map/ppermute | solution.py:419
  8.4 0.9 %shard_map.69 = (bf16[1024,1024]{1,0:T(8,128)(2,1)S(1)}, bf16[512,1024]{1,0:T(8,128)(2,1)S(1)}, f32[2,128]{1,0:T(2,128)S(1)}) custom-call(f32[4,8,1024]{2,1,0:T(8,128)S(1)} %get-tuple-element.29.b_ref, f32[4,8,1024]{2,1,0:T(8,128)S(1)} %get-tuple-element.33.draw_ref, f32[4,8,1024]{2,1,0:T(8,128)S(1)} %get-tuple-element.34.slot_ref), custom_call_target="tpu_custom_call" | custom-call | flops 25165824 | tf_op jit(solution)/shard_map/pallas_call | solution.py:393
  9.3 0.0 collective-permute-done.got_second_ref.x_second_ref
  9.3 0.0 collective-permute-done.1.got_first_ref.x_first_ref
  9.3 0.7 %shard_map.70 = (f32[6,8,1024]{2,1,0:T(8,128)S(1)}, f32[5,8,1024]{2,1,0:T(8,128)S(1)}, f32[4,8,1024]{2,1,0:T(8,128)S(1)}, f32[16,32]{1,0:T(8,128)S(1)}, bf16[128...) custom-call(f32[4,8,1024]{2,1,0:T(8,128)S(1)} %get-tuple-element.29.b_ref, ...), custom_call_target="tpu_custom_call" | custom-call | flops 25165824 | tf_op jit(solution)/shard_map/pallas_call | solution.py:393
  9.9 0.0 collective-permute-done.2.y_second_ref
  9.9 0.9 %collective-permute-done.3.y_first_ref = f32[16,1024]{1,0:T(8,128)S(1)} collective-permute-done((f32[16,1024]{1,0:T(8,128)S(1)}, f32[16,1024]{1,0:T(8,128)S(1)}, u32[]{:S(2)}, u32[]{:S(2)}) %collective-permute-start.3) | collective-permute-done | bytes 65568 | tf_op jit(solution)/shard_map/ppermute | solution.py:419
  10.8 0.9 %shard_map.71 = (f32[4,8,1024]{2,1,0:T(8,128)S(1)}, f32[4,8,1024]{2,1,0:T(8,128)S(1)}, f32[4,128]{1,0:T(4,128)S(1)}, f32[4,1024]{1,0:T(4,128)S(1)}, f32[4,1024]{1,0:T(4,128)S(1)}, /*index=5*/f32[24,1024]{1,0:T(8,128)S(1)}) custom-call(f32[4,8,1024]{2,1,0:T(8,128)S(1)} %get-tuple-element.29.b_ref, f32[4,8,1024]{2,1,0:T(8,128)S(1)} %get-tuple-element.30.cap_ref, ...), custom_call_target="tpu_custom_call" | custom-call | flops 25165824 | tf_op jit(solution)/shard_map/pallas_call | solution.py:393
  11.8 0.6 %broadcast_in_dim.2 = f32[16,4,128]{2,1,0:T(4,128)} broadcast(f32[4,128]{1,0:T(4,128)S(1)} %get-tuple-element.50), dimensions={1,2} | broadcast | bytes 34816 | tf_op jit(solution)/shard_map/broadcast_in_dim | solution.py:428
  12.4 4.8 %all-to-all-start = ((f32[16,4,128]{2,1,0:T(4,128)}), f32[16,4,128]{2,1,0:T(4,128)S(1)}, u32[]{:S(2)}, u32[]{:S(2)}) async-start(f32[16,4,128]{2,1,0:T(4,128)} %broadcast_in_dim.2), calls=%async_computation | async-start | bytes 65536 | tf_op jit(solution)/shard_map/all_to_all | solution.py:429
  17.2 0.6 %collective-permute-start.4 = (f32[4,1024]{1,0:T(4,128)S(1)}, f32[4,1024]{1,0:T(4,128)S(1)}, u32[]{:S(2)}, u32[]{:S(2)}) collective-permute-start(f32[4,1024]{1,0:T(4,128)S(1)} %get-tuple-element.54), channel_id=1, source_target_pairs={{0,1},{1,0},{2,3},{3,2},{4,5},{5,4},{6,7},{7,6},{8,9},{9,8},{10,11... | collective-permute-start | bytes 49160 | tf_op jit(solution)/shard_map/ppermute | solution.py:419
  17.8 0.0 collective-permute-start.5
  17.8 3.1 %collective-permute-done.4.corner_first_ref = f32[4,1024]{1,0:T(4,128)S(1)} collective-permute-done((f32[4,1024]{1,0:T(4,128)S(1)}, f32[4,1024]{1,0:T(4,128)S(1)}, u32[]{:S(2)}, u32[]{:S(2)}) %collective-permute-start.4) | collective-permute-done | bytes 16416 | tf_op jit(solution)/shard_map/ppermute | solution.py:419
  21.0 0.0 collective-permute-done.5.corner_second_ref
  21.0 0.3 %all-to-all-done.sketch_ref = f32[16,4,128]{2,1,0:T(4,128)S(1)} async-done(((f32[16,4,128]{2,1,0:T(4,128)}), f32[16,4,128]{2,1,0:T(4,128)S(1)}, u32[]{:S(2)}, u32[]{:S(2)}) %all-to-all-start) | async-done | bytes 32800 | tf_op jit(solution)/shard_map/all_to_all | solution.py:429
  21.3 1.1 %shard_map.72 = (f32[4,8,1024]{2,1,0:T(8,128)}, f32[4,8,1024]{2,1,0:T(8,128)}) custom-call(f32[16,4,128]{2,1,0:T(4,128)S(1)} %all-to-all-done.sketch_ref, f32[4,8,1024]{2,1,0:T(8,128)S(1)} %get-tuple-element.29.b_ref, f32[4,8,1024]{2,1,0:T(8,128)S(1)} %get-tuple-element.51.image_ref, f32[4,8,1024]{2,1,0:T(8,128)S(1)} %get-tuple-element.52.twice_ref, ...), custom_call_target="tpu_custom_call" | custom-call | tf_op jit(solution)/shard_map/pallas_call | solution.py:393
Async XLA Ops:
  2.1 7.2 %collective-permute-start = (f32[28,1024]{1,0:T(8,128)S(1)}, f32[28,1024]{1,0:T(8,128)S(1)}, u32[]{:S(2)}, u32[]{:S(2)}) collective-permute-start(f32[28,1024]{1,0:T(8,128)S(1)} %get-tuple-element.41), channel_id=1, source_target_pairs={{0,1},{1,0},{2,3},{3,2},{4,8},{5,9},{6,10},{7,11},{8,4},{9,5},{10,... | collective-permute-start | bytes 344072 | tf_op jit(solution)/shard_map/ppermute | solution.py:419
  5.2 4.1 %collective-permute-start.1 = (f32[28,1024]{1,0:T(8,128)S(1)}, f32[28,1024]{1,0:T(8,128)S(1)}, u32[]{:S(2)}, u32[]{:S(2)}) collective-permute-start(f32[28,1024]{1,0:T(8,128)S(1)} %get-tuple-element.42), channel_id=1, source_target_pairs={{0,4},{1,5},{2,6},{3,7},{4,0},{5,1},{6,2},{7,3},{8,12},{9,13},{10,... | collective-permute-start | bytes 344072 | tf_op jit(solution)/shard_map/ppermute | solution.py:419
  5.3 4.7 %collective-permute-start.2 = (f32[16,1024]{1,0:T(8,128)S(1)}, f32[16,1024]{1,0:T(8,128)S(1)}, u32[]{:S(2)}, u32[]{:S(2)}) collective-permute-start(f32[16,1024]{1,0:T(8,128)S(1)} %get-tuple-element.37.own_second_ref), channel_id=1, source_target_pairs={{0,4},{1,2},{2,1},{3,7},{4,0},{5,6},{6,5},{7,3},{8,12},{9,10},{10,... | collective-permute-start | bytes 196616 | tf_op jit(solution)/shard_map/ppermute | solution.py:419
  5.7 5.1 %collective-permute-start.3 = (f32[16,1024]{1,0:T(8,128)S(1)}, f32[16,1024]{1,0:T(8,128)S(1)}, u32[]{:S(2)}, u32[]{:S(2)}) collective-permute-start(f32[16,1024]{1,0:T(8,128)S(1)} %get-tuple-element.38.own_first_ref), channel_id=1, source_target_pairs={{0,1},{1,0},{2,3},{3,2},{4,5},{5,4},{6,7},{7,6},{8,9},{9,8},{10,11... | collective-permute-start | bytes 196616 | tf_op jit(solution)/shard_map/ppermute | solution.py:419
  12.4 8.9 %all-to-all-start = ((f32[16,4,128]{2,1,0:T(4,128)}), f32[16,4,128]{2,1,0:T(4,128)S(1)}, u32[]{:S(2)}, u32[]{:S(2)}) async-start(f32[16,4,128]{2,1,0:T(4,128)} %broadcast_in_dim.2), calls=%async_computation | async-start | bytes 65536 | tf_op jit(solution)/shard_map/all_to_all | solution.py:429
  17.2 3.7 %collective-permute-start.4 = (f32[4,1024]{1,0:T(4,128)S(1)}, f32[4,1024]{1,0:T(4,128)S(1)}, u32[]{:S(2)}, u32[]{:S(2)}) collective-permute-start(f32[4,1024]{1,0:T(4,128)S(1)} %get-tuple-element.54), channel_id=1, source_target_pairs={{0,1},{1,0},{2,3},{3,2},{4,5},{5,4},{6,7},{7,6},{8,9},{9,8},{10,11... | collective-permute-start | bytes 49160 | tf_op jit(solution)/shard_map/ppermute | solution.py:419
  17.8 3.2 %collective-permute-start.5 = (f32[4,1024]{1,0:T(4,128)S(1)}, f32[4,1024]{1,0:T(4,128)S(1)}, u32[]{:S(2)}, u32[]{:S(2)}) collective-permute-start(f32[4,1024]{1,0:T(4,128)S(1)} %get-tuple-element.55), channel_id=1, source_target_pairs={{0,4},{1,2},{2,1},{3,7},{4,0},{5,6},{6,5},{7,3},{8,12},{9,10},{10,... | collective-permute-start | bytes 49160 | tf_op jit(solution)/shard_map/ppermute | solution.py:419

commit v12 on v9

--- a/solution.py
+++ b/solution.py
@@ -332,7 +332,7 @@
 
 def last_kernel(
     sketch_ref, b_ref, image_ref, twice_ref, ends_ref, corner_first_ref, corner_second_ref,
-    solution_ref, residual_ref,
+    solution_hbm, residual_hbm, solution_ref, residual_ref, sent,
 ):
     sketches = jnp.sum(sketch_ref[...], axis=0)
 
@@ -357,10 +357,17 @@
     c1 = -ratio / (cross * ratio + n1_square)
     c0 = h00 / first - (h00 * h01 + n0 * h11) / first * (n0 * c1) - h00 * c1
     planes, rows, depth = b_ref.shape
-    for i in range(planes):
-        b, image = b_ref[i], image_ref[i]
-        solution_ref[i] = c0 * b + c1 * image
-        residual_ref[i] = b - c0 * image - c1 * twice_ref[i]
+    copies = [
+        pltpu.make_async_copy(source, target, sent.at[k])
+        for k, (source, target) in enumerate(
+            ((solution_ref, solution_hbm), (residual_ref, residual_hbm))
+        )
+    ]
+    for i in range(planes):
+        solution_ref[i] = c0 * b_ref[i] + c1 * image_ref[i]
+    copies[0].start()
+    for i in range(planes):
+        residual_ref[i] = b_ref[i] - c0 * image_ref[i] - c1 * twice_ref[i]
     corners = by_turn(corner_first_ref[...], corner_second_ref[...], "gy")
     for side, (j, here, corner) in enumerate(zip((0, rows - 1), has_beside("gy"), corners)):
         for end, i in enumerate((0, planes - 1)):
@@ -373,9 +380,14 @@
             lacked = x_link * link(x_cond, cond) * (x_b - b)
             lacked = lacked + y_link * link(y_cond, cond) * (y_b - b)
             residual_ref[i, j : j + 1] = residual_ref[i, j : j + 1] + c1 * lacked
-
-
-def call(kernel, shapes, *operands, scratch=(), inputs=pltpu.VMEM, flops=0):
+    copies[1].start()
+    for copy in copies:
+        copy.wait()
+
+
+def call(
+    kernel, shapes, *operands, scratch=(), inputs=pltpu.VMEM, outputs=pltpu.VMEM, flops=0
+):
     return pl.pallas_call(
         kernel,
         out_shape=[
@@ -383,7 +395,7 @@
             for shape in shapes
         ],
         in_specs=[pl.BlockSpec(memory_space=inputs)] * len(operands),
-        out_specs=[pl.BlockSpec(memory_space=pltpu.VMEM)] * len(shapes),
+        out_specs=[pl.BlockSpec(memory_space=outputs)] * len(shapes),
         scratch_shapes=scratch,
         compiler_params=pltpu.CompilerParams(vmem_limit_bytes=48 * 1024 * 1024),
         cost_estimate=pl.CostEstimate(flops=flops, bytes_accessed=0, transcendentals=0),
@@ -464,7 +476,17 @@
     got_corners = [swap(array, "gy", turn) for turn, array in enumerate((first, second))]
     sketches = everyones(sketch)
     return tuple(
-        call(last_kernel, [block, block], sketches, b, image, twice, ends, *got_corners)
+        call(
+            last_kernel,
+            [block, block],
+            sketches, b, image, twice, ends, *got_corners,
+            scratch=[
+                pltpu.VMEM(block, jnp.float32),
+                pltpu.VMEM(block, jnp.float32),
+                pltpu.SemaphoreType.DMA((2,)),
+            ],
+            outputs=pltpu.HBM,
+        )
     )
 
 

time: 22.6 us -> 22.7 us (level)
  no operation moved by 1% of the time
where the time goes in v12:
time: 22.7 us; the launch traced here: 22.5 us
  starting transfers between devices  11.7 us (52%)
  Pallas kernels  5.04 us (22%)
  waiting for transfers between devices  4.44 us (20%)
  between operations  0.66 us (3%)
  local copies, waits for them, and re-layouts  0.64 us (3%)
    ppermute x6, starting transfers between devices, swap(): return lax.ppermute(array, ('gx', 'gy'), pairs)  6.89 us
    pallas_call x5, Pallas kernels, call(): pl.pallas_call(kernel, out_shape=[shape if hasattr(shape, 'dtype') else j...  5.04 us
    all_to_all x1, starting transfers between devices, everyones(): return lax.all_to_all(copies, ('gx', 'gy'), 0, 0, axis_index_groups=[group])  4.8 us
    ppermute x6, waiting for transfers between devices, swap(): return lax.ppermute(array, ('gx', 'gy'), pairs)  4.09 us
    broadcast_in_dim x1, local copies, waits for them, and re-layouts, everyones(): copies = jnp.broadcast_to(sketch[None], (nx * ny,) + sketch.shape)  0.64 us
  transfers between devices with their start and end apart: 7, of which 3 were waited for; matrix products, arithmetic and copies ran while one was open for 0% of the time, Pallas kernels for 7%

profile of v12, /device:TPU:0, one launch (start us, length us, event | category | flops | bytes accessed | tf_op | source)
XLA Modules:
  0.0 22.5 jit_solution(5190159652843941731)
XLA Ops:
  0.6 1.5 %shard_map.68 = (f32[4,8,1024]{2,1,0:T(8,128)S(1)}, f32[4,8,1024]{2,1,0:T(8,128)S(1)}, f32[4,8,1024]{2,1,0:T(8,128)S(1)}, f32[4,8,1024]{2,1,0:T(8,128)S(1)}, f32...) custom-call(f32[4,8,1024]{2,1,0:T(8,128)} %b_hbm.1, ...), custom_call_target="tpu_custom_call" | custom-call | tf_op jit(solution)/shard_map/pallas_call | solution.py:391
  2.1 3.1 %collective-permute-start = (f32[28,1024]{1,0:T(8,128)S(1)}, f32[28,1024]{1,0:T(8,128)S(1)}, u32[]{:S(2)}, u32[]{:S(2)}) collective-permute-start(f32[28,1024]{1,0:T(8,128)S(1)} %get-tuple-element.39), channel_id=1, source_target_pairs={{0,1},{1,0},{2,3},{3,2},{4,8},{5,9},{6,10},{7,11},{8,4},{9,5},{10,... | collective-permute-start | bytes 344072 | tf_op jit(solution)/shard_map/ppermute | solution.py:417
  5.2 0.1 collective-permute-start.1
  5.3 0.5 %collective-permute-start.2 = (f32[16,1024]{1,0:T(8,128)S(1)}, f32[16,1024]{1,0:T(8,128)S(1)}, u32[]{:S(2)}, u32[]{:S(2)}) collective-permute-start(f32[16,1024]{1,0:T(8,128)S(1)} %get-tuple-element.35.own_second_ref), channel_id=1, source_target_pairs={{0,4},{1,2},{2,1},{3,7},{4,0},{5,6},{6,5},{7,3},{8,12},{9,10},{10,... | collective-permute-start | bytes 196616 | tf_op jit(solution)/shard_map/ppermute | solution.py:417
  5.7 2.7 %collective-permute-start.3 = (f32[16,1024]{1,0:T(8,128)S(1)}, f32[16,1024]{1,0:T(8,128)S(1)}, u32[]{:S(2)}, u32[]{:S(2)}) collective-permute-start(f32[16,1024]{1,0:T(8,128)S(1)} %get-tuple-element.36.own_first_ref), channel_id=1, source_target_pairs={{0,1},{1,0},{2,3},{3,2},{4,5},{5,4},{6,7},{7,6},{8,9},{9,8},{10,11... | collective-permute-start | bytes 196616 | tf_op jit(solution)/shard_map/ppermute | solution.py:417
  8.4 0.9 %shard_map.69 = (bf16[1024,1024]{1,0:T(8,128)(2,1)S(1)}, bf16[512,1024]{1,0:T(8,128)(2,1)S(1)}, f32[2,128]{1,0:T(2,128)S(1)}) custom-call(f32[4,8,1024]{2,1,0:T(8,128)S(1)} %get-tuple-element.27.b_ref, f32[4,8,1024]{2,1,0:T(8,128)S(1)} %get-tuple-element.31.draw_ref, f32[4,8,1024]{2,1,0:T(8,128)S(1)} %get-tuple-element.32.slot_ref), custom_call_target="tpu_custom_call" | custom-call | flops 25165824 | tf_op jit(solution)/shard_map/pallas_call | solution.py:391
  9.3 0.0 collective-permute-done.got_second_ref.x_second_ref
  9.3 0.0 collective-permute-done.1.got_first_ref.x_first_ref
  9.3 0.6 %shard_map.70 = (f32[6,8,1024]{2,1,0:T(8,128)S(1)}, f32[5,8,1024]{2,1,0:T(8,128)S(1)}, f32[4,8,1024]{2,1,0:T(8,128)S(1)}, f32[16,32]{1,0:T(8,128)S(1)}) custom-call(f32[4,8,1024]{2,1,0:T(8,128)S(1)} %get-tuple-element.27.b_ref, f32[4,8,1024]{2,1,0:T(8,128)S(1)} %get-tuple-element.37.cond_ref, f32[4,8,1024]{2,1,0:T(8,128)S(1)} %get-tuple-element.28.cap_ref, ...), custom_call_target="tpu_custom_call" | custom-call | flops 25165824 | tf_op jit(solution)/shard_map/pallas_call | solution.py:391
  9.9 0.0 collective-permute-done.2.y_second_ref
  9.9 0.9 %collective-permute-done.3.y_first_ref = f32[16,1024]{1,0:T(8,128)S(1)} collective-permute-done((f32[16,1024]{1,0:T(8,128)S(1)}, f32[16,1024]{1,0:T(8,128)S(1)}, u32[]{:S(2)}, u32[]{:S(2)}) %collective-permute-start.3) | collective-permute-done | bytes 65568 | tf_op jit(solution)/shard_map/ppermute | solution.py:417
  10.8 1.0 %shard_map.71 = (f32[4,8,1024]{2,1,0:T(8,128)S(1)}, f32[4,8,1024]{2,1,0:T(8,128)S(1)}, f32[4,128]{1,0:T(4,128)S(1)}, f32[4,1024]{1,0:T(4,128)S(1)}, f32[4,1024]{1,0:T(4,128)S(1)}, /*index=5*/f32[24,1024]{1,0:T(8,128)S(1)}) custom-call(f32[4,8,1024]{2,1,0:T(8,128)S(1)} %get-tuple-element.27.b_ref, f32[4,8,1024]{2,1,0:T(8,128)S(1)} %get-tuple-element.28.cap_ref, ...), custom_call_target="tpu_custom_call" | custom-call | flops 25165824 | tf_op jit(solution)/shard_map/pallas_call | solution.py:391
  11.8 0.6 %broadcast_in_dim.2 = f32[16,4,128]{2,1,0:T(4,128)} broadcast(f32[4,128]{1,0:T(4,128)S(1)} %get-tuple-element.46), dimensions={1,2} | broadcast | bytes 34816 | tf_op jit(solution)/shard_map/broadcast_in_dim | solution.py:426
  12.4 4.8 %all-to-all-start = ((f32[16,4,128]{2,1,0:T(4,128)}), f32[16,4,128]{2,1,0:T(4,128)S(1)}, u32[]{:S(2)}, u32[]{:S(2)}) async-start(f32[16,4,128]{2,1,0:T(4,128)} %broadcast_in_dim.2), calls=%async_computation | async-start | bytes 65536 | tf_op jit(solution)/shard_map/all_to_all | solution.py:427
  17.2 0.6 %collective-permute-start.4 = (f32[4,1024]{1,0:T(4,128)S(1)}, f32[4,1024]{1,0:T(4,128)S(1)}, u32[]{:S(2)}, u32[]{:S(2)}) collective-permute-start(f32[4,1024]{1,0:T(4,128)S(1)} %get-tuple-element.50), channel_id=1, source_target_pairs={{0,1},{1,0},{2,3},{3,2},{4,5},{5,4},{6,7},{7,6},{8,9},{9,8},{10,11... | collective-permute-start | bytes 49160 | tf_op jit(solution)/shard_map/ppermute | solution.py:417
  17.8 0.0 collective-permute-start.5
  17.8 3.1 %collective-permute-done.4.corner_first_ref = f32[4,1024]{1,0:T(4,128)S(1)} collective-permute-done((f32[4,1024]{1,0:T(4,128)S(1)}, f32[4,1024]{1,0:T(4,128)S(1)}, u32[]{:S(2)}, u32[]{:S(2)}) %collective-permute-start.4) | collective-permute-done | bytes 16416 | tf_op jit(solution)/shard_map/ppermute | solution.py:417
  21.0 0.0 collective-permute-done.5.corner_second_ref
  21.0 0.3 %all-to-all-done.sketch_ref = f32[16,4,128]{2,1,0:T(4,128)S(1)} async-done(((f32[16,4,128]{2,1,0:T(4,128)}), f32[16,4,128]{2,1,0:T(4,128)S(1)}, u32[]{:S(2)}, u32[]{:S(2)}) %all-to-all-start) | async-done | bytes 32800 | tf_op jit(solution)/shard_map/all_to_all | solution.py:427
  21.3 1.1 %shard_map.72 = (f32[4,8,1024]{2,1,0:T(8,128)}, f32[4,8,1024]{2,1,0:T(8,128)}) custom-call(f32[16,4,128]{2,1,0:T(4,128)S(1)} %all-to-all-done.sketch_ref, f32[4,8,1024]{2,1,0:T(8,128)S(1)} %get-tuple-element.27.b_ref, f32[4,8,1024]{2,1,0:T(8,128)S(1)} %get-tuple-element.47.image_ref, f32[4,8,1024]{2,1,0:T(8,128)S(1)} %get-tuple-element.48.twice_ref, ...), custom_call_target="tpu_custom_call" | custom-call | tf_op jit(solution)/shard_map/pallas_call | solution.py:391
Async XLA Ops:
  2.1 7.2 %collective-permute-start = (f32[28,1024]{1,0:T(8,128)S(1)}, f32[28,1024]{1,0:T(8,128)S(1)}, u32[]{:S(2)}, u32[]{:S(2)}) collective-permute-start(f32[28,1024]{1,0:T(8,128)S(1)} %get-tuple-element.39), channel_id=1, source_target_pairs={{0,1},{1,0},{2,3},{3,2},{4,8},{5,9},{6,10},{7,11},{8,4},{9,5},{10,... | collective-permute-start | bytes 344072 | tf_op jit(solution)/shard_map/ppermute | solution.py:417
  5.2 4.1 %collective-permute-start.1 = (f32[28,1024]{1,0:T(8,128)S(1)}, f32[28,1024]{1,0:T(8,128)S(1)}, u32[]{:S(2)}, u32[]{:S(2)}) collective-permute-start(f32[28,1024]{1,0:T(8,128)S(1)} %get-tuple-element.40), channel_id=1, source_target_pairs={{0,4},{1,5},{2,6},{3,7},{4,0},{5,1},{6,2},{7,3},{8,12},{9,13},{10,... | collective-permute-start | bytes 344072 | tf_op jit(solution)/shard_map/ppermute | solution.py:417
  5.3 4.6 %collective-permute-start.2 = (f32[16,1024]{1,0:T(8,128)S(1)}, f32[16,1024]{1,0:T(8,128)S(1)}, u32[]{:S(2)}, u32[]{:S(2)}) collective-permute-start(f32[16,1024]{1,0:T(8,128)S(1)} %get-tuple-element.35.own_second_ref), channel_id=1, source_target_pairs={{0,4},{1,2},{2,1},{3,7},{4,0},{5,6},{6,5},{7,3},{8,12},{9,10},{10,... | collective-permute-start | bytes 196616 | tf_op jit(solution)/shard_map/ppermute | solution.py:417
  5.7 5.1 %collective-permute-start.3 = (f32[16,1024]{1,0:T(8,128)S(1)}, f32[16,1024]{1,0:T(8,128)S(1)}, u32[]{:S(2)}, u32[]{:S(2)}) collective-permute-start(f32[16,1024]{1,0:T(8,128)S(1)} %get-tuple-element.36.own_first_ref), channel_id=1, source_target_pairs={{0,1},{1,0},{2,3},{3,2},{4,5},{5,4},{6,7},{7,6},{8,9},{9,8},{10,11... | collective-permute-start | bytes 196616 | tf_op jit(solution)/shard_map/ppermute | solution.py:417
  12.4 8.9 %all-to-all-start = ((f32[16,4,128]{2,1,0:T(4,128)}), f32[16,4,128]{2,1,0:T(4,128)S(1)}, u32[]{:S(2)}, u32[]{:S(2)}) async-start(f32[16,4,128]{2,1,0:T(4,128)} %broadcast_in_dim.2), calls=%async_computation | async-start | bytes 65536 | tf_op jit(solution)/shard_map/all_to_all | solution.py:427
  17.2 3.7 %collective-permute-start.4 = (f32[4,1024]{1,0:T(4,128)S(1)}, f32[4,1024]{1,0:T(4,128)S(1)}, u32[]{:S(2)}, u32[]{:S(2)}) collective-permute-start(f32[4,1024]{1,0:T(4,128)S(1)} %get-tuple-element.50), channel_id=1, source_target_pairs={{0,1},{1,0},{2,3},{3,2},{4,5},{5,4},{6,7},{7,6},{8,9},{9,8},{10,11... | collective-permute-start | bytes 49160 | tf_op jit(solution)/shard_map/ppermute | solution.py:417
  17.8 3.2 %collective-permute-start.5 = (f32[4,1024]{1,0:T(4,128)S(1)}, f32[4,1024]{1,0:T(4,128)S(1)}, u32[]{:S(2)}, u32[]{:S(2)}) collective-permute-start(f32[4,1024]{1,0:T(4,128)S(1)} %get-tuple-element.51), channel_id=1, source_target_pairs={{0,4},{1,2},{2,1},{3,7},{4,0},{5,6},{6,5},{7,3},{8,12},{9,10},{10,... | collective-permute-start | bytes 49160 | tf_op jit(solution)/shard_map/ppermute | solution.py:417

commit v13 on v9

--- a/solution.py
+++ b/solution.py
@@ -111,21 +111,19 @@
     return total[:PAIR] + total[PAIR:]
 
 
-def sketch_rows(planes, low_ref, high_ref, cells_ref):
-    total = 0.0
+def sketch_rows(planes, low_ref, high_ref, cells_ref, left=(), right=()):
+    left, right = list(left), list(right)
     each = HIGH * 2 * PAIR
     for i, (fields, draw, chosen) in enumerate(planes):
         rows = draw.shape[0]
         start = i * rows * 8
         put_cells(fields, draw, start, cells_ref)
-        left, right = [], []
         for j in chosen:
             at = i * rows + j
             mask = high_ref[at * each : (at + 1) * each]
             left.append(masked_cells(mask, start, j, cells_ref))
             right.append(low_ref[at * LOW : (at + 1) * LOW])
-        total = total + product(left, right)
-    return total
+    return product(left, right)
 
 
 def slot_kernel(b_ref, draw_ref, slot_ref, low_ref, high_ref, sketch_ref, cells_ref):
@@ -311,7 +309,6 @@
         twice_ref[i] = twice[i]
     chosen = reached(rows)[0]
     cells = [((images[i + 1], twice[i]), draw_ref[i], chosen) for i in range(planes)]
-    total = inside_ref[...] + sketch_rows(cells, low_ref, high_ref, cells_ref)
     start = planes * rows * 8
     put_cells((jnp.zeros((8, depth), jnp.float32), extra_ref[0]), extra_ref[1], start, cells_ref)
     low, high = parts_of(extra_ref[2])
@@ -320,7 +317,9 @@
         mask = one_hot(high, j, HIGH, 2 * PAIR)
         left.append(masked_cells(mask, start, j, cells_ref))
         right.append(one_hot(low, j, LOW, 1))
-    sketch_ref[1 : 1 + PAIR] = as_sketch(total + product(left, right))
+    sketch_ref[1 : 1 + PAIR] = as_sketch(
+        inside_ref[...] + sketch_rows(cells, low_ref, high_ref, cells_ref, left, right)
+    )
     sketch_ref[:1] = b_sketch_ref[:1]
     sketch_ref[1 + PAIR :] = b_sketch_ref[:1]
     for k, plane in enumerate(b_beside + c_beside):

time: 22.6 us -> 22.6 us (level)
  no operation moved by 1% of the time
where the time goes in v13:
time: 22.6 us; the launch traced here: 22.4 us
  starting transfers between devices  11.7 us (52%)
  Pallas kernels  5.03 us (22%)
  waiting for transfers between devices  4.42 us (20%)
  between operations  0.66 us (3%)
  local copies, waits for them, and re-layouts  0.64 us (3%)
    ppermute x6, starting transfers between devices, swap(): return lax.ppermute(array, ('gx', 'gy'), pairs)  6.89 us
    pallas_call x5, Pallas kernels, call(): pl.pallas_call(kernel, out_shape=[shape if hasattr(shape, 'dtype') else j...  5.03 us
    all_to_all x1, starting transfers between devices, everyones(): return lax.all_to_all(copies, ('gx', 'gy'), 0, 0, axis_index_groups=[group])  4.8 us
    ppermute x6, waiting for transfers between devices, swap(): return lax.ppermute(array, ('gx', 'gy'), pairs)  4.08 us
    broadcast_in_dim x1, local copies, waits for them, and re-layouts, everyones(): copies = jnp.broadcast_to(sketch[None], (nx * ny,) + sketch.shape)  0.64 us
  transfers between devices with their start and end apart: 7, of which 3 were waited for; matrix products, arithmetic and copies ran while one was open for 0% of the time, Pallas kernels for 7%

profile of v13, /device:TPU:0, one launch (start us, length us, event | category | flops | bytes accessed | tf_op | source)
XLA Modules:
  0.0 22.4 jit_solution(8086064509378793582)
XLA Ops:
  0.6 1.5 %shard_map.68 = (f32[4,8,1024]{2,1,0:T(8,128)S(1)}, f32[4,8,1024]{2,1,0:T(8,128)S(1)}, f32[4,8,1024]{2,1,0:T(8,128)S(1)}, f32[4,8,1024]{2,1,0:T(8,128)S(1)}, f32...) custom-call(f32[4,8,1024]{2,1,0:T(8,128)} %b_hbm.1, ...), custom_call_target="tpu_custom_call" | custom-call | tf_op jit(solution)/shard_map/pallas_call | solution.py:378
  2.1 3.1 %collective-permute-start = (f32[28,1024]{1,0:T(8,128)S(1)}, f32[28,1024]{1,0:T(8,128)S(1)}, u32[]{:S(2)}, u32[]{:S(2)}) collective-permute-start(f32[28,1024]{1,0:T(8,128)S(1)} %get-tuple-element.39), channel_id=1, source_target_pairs={{0,1},{1,0},{2,3},{3,2},{4,8},{5,9},{6,10},{7,11},{8,4},{9,5},{10,... | collective-permute-start | bytes 344072 | tf_op jit(solution)/shard_map/ppermute | solution.py:404
  5.2 0.1 collective-permute-start.1
  5.3 0.5 %collective-permute-start.2 = (f32[16,1024]{1,0:T(8,128)S(1)}, f32[16,1024]{1,0:T(8,128)S(1)}, u32[]{:S(2)}, u32[]{:S(2)}) collective-permute-start(f32[16,1024]{1,0:T(8,128)S(1)} %get-tuple-element.35.own_second_ref), channel_id=1, source_target_pairs={{0,4},{1,2},{2,1},{3,7},{4,0},{5,6},{6,5},{7,3},{8,12},{9,10},{10,... | collective-permute-start | bytes 196616 | tf_op jit(solution)/shard_map/ppermute | solution.py:404
  5.7 2.7 %collective-permute-start.3 = (f32[16,1024]{1,0:T(8,128)S(1)}, f32[16,1024]{1,0:T(8,128)S(1)}, u32[]{:S(2)}, u32[]{:S(2)}) collective-permute-start(f32[16,1024]{1,0:T(8,128)S(1)} %get-tuple-element.36.own_first_ref), channel_id=1, source_target_pairs={{0,1},{1,0},{2,3},{3,2},{4,5},{5,4},{6,7},{7,6},{8,9},{9,8},{10,11... | collective-permute-start | bytes 196616 | tf_op jit(solution)/shard_map/ppermute | solution.py:404
  8.4 0.9 %shard_map.69 = (bf16[1024,1024]{1,0:T(8,128)(2,1)S(1)}, bf16[512,1024]{1,0:T(8,128)(2,1)S(1)}, f32[2,128]{1,0:T(2,128)S(1)}) custom-call(f32[4,8,1024]{2,1,0:T(8,128)S(1)} %get-tuple-element.27.b_ref, f32[4,8,1024]{2,1,0:T(8,128)S(1)} %get-tuple-element.31.draw_ref, f32[4,8,1024]{2,1,0:T(8,128)S(1)} %get-tuple-element.32.slot_ref), custom_call_target="tpu_custom_call" | custom-call | flops 25165824 | tf_op jit(solution)/shard_map/pallas_call | solution.py:378
  9.3 0.0 collective-permute-done.got_second_ref.x_second_ref
  9.3 0.0 collective-permute-done.1.got_first_ref.x_first_ref
  9.3 0.6 %shard_map.70 = (f32[6,8,1024]{2,1,0:T(8,128)S(1)}, f32[5,8,1024]{2,1,0:T(8,128)S(1)}, f32[4,8,1024]{2,1,0:T(8,128)S(1)}, f32[16,32]{1,0:T(8,128)S(1)}) custom-call(f32[4,8,1024]{2,1,0:T(8,128)S(1)} %get-tuple-element.27.b_ref, f32[4,8,1024]{2,1,0:T(8,128)S(1)} %get-tuple-element.37.cond_ref, f32[4,8,1024]{2,1,0:T(8,128)S(1)} %get-tuple-element.28.cap_ref, ...), custom_call_target="tpu_custom_call" | custom-call | flops 25165824 | tf_op jit(solution)/shard_map/pallas_call | solution.py:378
  9.9 0.0 collective-permute-done.2.y_second_ref
  9.9 0.9 %collective-permute-done.3.y_first_ref = f32[16,1024]{1,0:T(8,128)S(1)} collective-permute-done((f32[16,1024]{1,0:T(8,128)S(1)}, f32[16,1024]{1,0:T(8,128)S(1)}, u32[]{:S(2)}, u32[]{:S(2)}) %collective-permute-start.3) | collective-permute-done | bytes 65568 | tf_op jit(solution)/shard_map/ppermute | solution.py:404
  10.8 0.9 %shard_map.71 = (f32[4,8,1024]{2,1,0:T(8,128)S(1)}, f32[4,8,1024]{2,1,0:T(8,128)S(1)}, f32[4,128]{1,0:T(4,128)S(1)}, f32[4,1024]{1,0:T(4,128)S(1)}, f32[4,1024]{1,0:T(4,128)S(1)}, /*index=5*/f32[24,1024]{1,0:T(8,128)S(1)}) custom-call(f32[4,8,1024]{2,1,0:T(8,128)S(1)} %get-tuple-element.27.b_ref, f32[4,8,1024]{2,1,0:T(8,128)S(1)} %get-tuple-element.28.cap_ref, ...), custom_call_target="tpu_custom_call" | custom-call | flops 25165824 | tf_op jit(solution)/shard_map/pallas_call | solution.py:378
  11.8 0.6 %broadcast_in_dim.2 = f32[16,4,128]{2,1,0:T(4,128)} broadcast(f32[4,128]{1,0:T(4,128)S(1)} %get-tuple-element.46), dimensions={1,2} | broadcast | bytes 34816 | tf_op jit(solution)/shard_map/broadcast_in_dim | solution.py:413
  12.4 4.8 %all-to-all-start = ((f32[16,4,128]{2,1,0:T(4,128)}), f32[16,4,128]{2,1,0:T(4,128)S(1)}, u32[]{:S(2)}, u32[]{:S(2)}) async-start(f32[16,4,128]{2,1,0:T(4,128)} %broadcast_in_dim.2), calls=%async_computation | async-start | bytes 65536 | tf_op jit(solution)/shard_map/all_to_all | solution.py:414
  17.2 0.6 %collective-permute-start.4 = (f32[4,1024]{1,0:T(4,128)S(1)}, f32[4,1024]{1,0:T(4,128)S(1)}, u32[]{:S(2)}, u32[]{:S(2)}) collective-permute-start(f32[4,1024]{1,0:T(4,128)S(1)} %get-tuple-element.50), channel_id=1, source_target_pairs={{0,1},{1,0},{2,3},{3,2},{4,5},{5,4},{6,7},{7,6},{8,9},{9,8},{10,11... | collective-permute-start | bytes 49160 | tf_op jit(solution)/shard_map/ppermute | solution.py:404
  17.8 0.0 collective-permute-start.5
  17.8 3.1 %collective-permute-done.4.corner_first_ref = f32[4,1024]{1,0:T(4,128)S(1)} collective-permute-done((f32[4,1024]{1,0:T(4,128)S(1)}, f32[4,1024]{1,0:T(4,128)S(1)}, u32[]{:S(2)}, u32[]{:S(2)}) %collective-permute-start.4) | collective-permute-done | bytes 16416 | tf_op jit(solution)/shard_map/ppermute | solution.py:404
  21.0 0.0 collective-permute-done.5.corner_second_ref
  21.0 0.3 %all-to-all-done.sketch_ref = f32[16,4,128]{2,1,0:T(4,128)S(1)} async-done(((f32[16,4,128]{2,1,0:T(4,128)}), f32[16,4,128]{2,1,0:T(4,128)S(1)}, u32[]{:S(2)}, u32[]{:S(2)}) %all-to-all-start) | async-done | bytes 32800 | tf_op jit(solution)/shard_map/all_to_all | solution.py:414
  21.3 1.1 %shard_map.72 = (f32[4,8,1024]{2,1,0:T(8,128)}, f32[4,8,1024]{2,1,0:T(8,128)}) custom-call(f32[16,4,128]{2,1,0:T(4,128)S(1)} %all-to-all-done.sketch_ref, f32[4,8,1024]{2,1,0:T(8,128)S(1)} %get-tuple-element.27.b_ref, f32[4,8,1024]{2,1,0:T(8,128)S(1)} %get-tuple-element.47.image_ref, f32[4,8,1024]{2,1,0:T(8,128)S(1)} %get-tuple-element.48.twice_ref, ...), custom_call_target="tpu_custom_call" | custom-call | tf_op jit(solution)/shard_map/pallas_call | solution.py:378
Async XLA Ops:
  2.1 7.2 %collective-permute-start = (f32[28,1024]{1,0:T(8,128)S(1)}, f32[28,1024]{1,0:T(8,128)S(1)}, u32[]{:S(2)}, u32[]{:S(2)}) collective-permute-start(f32[28,1024]{1,0:T(8,128)S(1)} %get-tuple-element.39), channel_id=1, source_target_pairs={{0,1},{1,0},{2,3},{3,2},{4,8},{5,9},{6,10},{7,11},{8,4},{9,5},{10,... | collective-permute-start | bytes 344072 | tf_op jit(solution)/shard_map/ppermute | solution.py:404
  5.2 4.1 %collective-permute-start.1 = (f32[28,1024]{1,0:T(8,128)S(1)}, f32[28,1024]{1,0:T(8,128)S(1)}, u32[]{:S(2)}, u32[]{:S(2)}) collective-permute-start(f32[28,1024]{1,0:T(8,128)S(1)} %get-tuple-element.40), channel_id=1, source_target_pairs={{0,4},{1,5},{2,6},{3,7},{4,0},{5,1},{6,2},{7,3},{8,12},{9,13},{10,... | collective-permute-start | bytes 344072 | tf_op jit(solution)/shard_map/ppermute | solution.py:404
  5.3 4.7 %collective-permute-start.2 = (f32[16,1024]{1,0:T(8,128)S(1)}, f32[16,1024]{1,0:T(8,128)S(1)}, u32[]{:S(2)}, u32[]{:S(2)}) collective-permute-start(f32[16,1024]{1,0:T(8,128)S(1)} %get-tuple-element.35.own_second_ref), channel_id=1, source_target_pairs={{0,4},{1,2},{2,1},{3,7},{4,0},{5,6},{6,5},{7,3},{8,12},{9,10},{10,... | collective-permute-start | bytes 196616 | tf_op jit(solution)/shard_map/ppermute | solution.py:404
  5.7 5.1 %collective-permute-start.3 = (f32[16,1024]{1,0:T(8,128)S(1)}, f32[16,1024]{1,0:T(8,128)S(1)}, u32[]{:S(2)}, u32[]{:S(2)}) collective-permute-start(f32[16,1024]{1,0:T(8,128)S(1)} %get-tuple-element.36.own_first_ref), channel_id=1, source_target_pairs={{0,1},{1,0},{2,3},{3,2},{4,5},{5,4},{6,7},{7,6},{8,9},{9,8},{10,11... | collective-permute-start | bytes 196616 | tf_op jit(solution)/shard_map/ppermute | solution.py:404
  12.4 8.9 %all-to-all-start = ((f32[16,4,128]{2,1,0:T(4,128)}), f32[16,4,128]{2,1,0:T(4,128)S(1)}, u32[]{:S(2)}, u32[]{:S(2)}) async-start(f32[16,4,128]{2,1,0:T(4,128)} %broadcast_in_dim.2), calls=%async_computation | async-start | bytes 65536 | tf_op jit(solution)/shard_map/all_to_all | solution.py:414
  17.2 3.7 %collective-permute-start.4 = (f32[4,1024]{1,0:T(4,128)S(1)}, f32[4,1024]{1,0:T(4,128)S(1)}, u32[]{:S(2)}, u32[]{:S(2)}) collective-permute-start(f32[4,1024]{1,0:T(4,128)S(1)} %get-tuple-element.50), channel_id=1, source_target_pairs={{0,1},{1,0},{2,3},{3,2},{4,5},{5,4},{6,7},{7,6},{8,9},{9,8},{10,11... | collective-permute-start | bytes 49160 | tf_op jit(solution)/shard_map/ppermute | solution.py:404
  17.8 3.2 %collective-permute-start.5 = (f32[4,1024]{1,0:T(4,128)S(1)}, f32[4,1024]{1,0:T(4,128)S(1)}, u32[]{:S(2)}, u32[]{:S(2)}) collective-permute-start(f32[4,1024]{1,0:T(4,128)S(1)} %get-tuple-element.51), channel_id=1, source_target_pairs={{0,4},{1,2},{2,1},{3,7},{4,0},{5,6},{6,5},{7,3},{8,12},{9,10},{10,... | collective-permute-start | bytes 49160 | tf_op jit(solution)/shard_map/ppermute | solution.py:404

commit v14 on v9

--- a/solution.py
+++ b/solution.py
@@ -407,7 +407,7 @@
 
 def everyones(sketch):
     nx, ny = lax.axis_size("gx"), lax.axis_size("gy")
-    middle = nx // 2 - 1, ny // 2
+    middle = nx - 1, ny // 2
     places = [(x, y) for x in range(nx) for y in range(ny)]
     places.sort(key=lambda at: (abs(at[1] - middle[1]), abs(at[0] - middle[0]), at))
     group = [x * ny + y for x, y in places]

time: 22.6 us -> 22.8 us (level)
  starting transfers between devices: 11.7 us -> 12.1 us
  waiting for transfers between devices: 4.44 us -> 4.12 us
    all_to_all x1, starting transfers between devices: 4.8 us -> 5.27 us  [everyones(): return lax.all_to_all(copies, ('gx', 'gy'), 0, 0, axis_index_groups=[group])]
    all_to_all x1, waiting for transfers between devices: 0.35 us -> 0.01 us  [everyones(): return lax.all_to_all(copies, ('gx', 'gy'), 0, 0, axis_index_groups=[group])]
  transfers between devices with their start and end apart: 7 -> 7, of which waited for: 3 -> 2; matrix products, arithmetic and copies ran while one was open for 0% -> 0% of each run, Pallas kernels for 7% -> 7%
where the time goes in v14:
time: 22.8 us; the launch traced here: 22.6 us
  starting transfers between devices  12.1 us (53%)
  Pallas kernels  5.03 us (22%)
  waiting for transfers between devices  4.12 us (18%)
  between operations  0.66 us (3%)
  local copies, waits for them, and re-layouts  0.64 us (3%)
    ppermute x6, starting transfers between devices, swap(): return lax.ppermute(array, ('gx', 'gy'), pairs)  6.86 us
    all_to_all x1, starting transfers between devices, everyones(): return lax.all_to_all(copies, ('gx', 'gy'), 0, 0, axis_index_groups=[group])  5.27 us
    pallas_call x5, Pallas kernels, call(): pl.pallas_call(kernel, out_shape=[shape if hasattr(shape, 'dtype') else j...  5.03 us
    ppermute x6, waiting for transfers between devices, swap(): return lax.ppermute(array, ('gx', 'gy'), pairs)  4.12 us
    broadcast_in_dim x1, local copies, waits for them, and re-layouts, everyones(): copies = jnp.broadcast_to(sketch[None], (nx * ny,) + sketch.shape)  0.64 us
  transfers between devices with their start and end apart: 7, of which 2 were waited for; matrix products, arithmetic and copies ran while one was open for 0% of the time, Pallas kernels for 7%

profile of v14, /device:TPU:0, one launch (start us, length us, event | category | flops | bytes accessed | tf_op | source)
XLA Modules:
  0.0 22.6 jit_solution(9415641834586608083)
XLA Ops:
  0.6 1.5 %shard_map.68 = (f32[4,8,1024]{2,1,0:T(8,128)S(1)}, f32[4,8,1024]{2,1,0:T(8,128)S(1)}, f32[4,8,1024]{2,1,0:T(8,128)S(1)}, f32[4,8,1024]{2,1,0:T(8,128)S(1)}, f32...) custom-call(f32[4,8,1024]{2,1,0:T(8,128)} %b_hbm.1, ...), custom_call_target="tpu_custom_call" | custom-call | tf_op jit(solution)/shard_map/pallas_call | solution.py:379
  2.1 3.1 %collective-permute-start = (f32[28,1024]{1,0:T(8,128)S(1)}, f32[28,1024]{1,0:T(8,128)S(1)}, u32[]{:S(2)}, u32[]{:S(2)}) collective-permute-start(f32[28,1024]{1,0:T(8,128)S(1)} %get-tuple-element.39), channel_id=1, source_target_pairs={{0,1},{1,0},{2,3},{3,2},{4,8},{5,9},{6,10},{7,11},{8,4},{9,5},{10,... | collective-permute-start | bytes 344072 | tf_op jit(solution)/shard_map/ppermute | solution.py:405
  5.2 0.1 collective-permute-start.1
  5.3 0.5 %collective-permute-start.2 = (f32[16,1024]{1,0:T(8,128)S(1)}, f32[16,1024]{1,0:T(8,128)S(1)}, u32[]{:S(2)}, u32[]{:S(2)}) collective-permute-start(f32[16,1024]{1,0:T(8,128)S(1)} %get-tuple-element.35.own_second_ref), channel_id=1, source_target_pairs={{0,4},{1,2},{2,1},{3,7},{4,0},{5,6},{6,5},{7,3},{8,12},{9,10},{10,... | collective-permute-start | bytes 196616 | tf_op jit(solution)/shard_map/ppermute | solution.py:405
  5.7 2.7 %collective-permute-start.3 = (f32[16,1024]{1,0:T(8,128)S(1)}, f32[16,1024]{1,0:T(8,128)S(1)}, u32[]{:S(2)}, u32[]{:S(2)}) collective-permute-start(f32[16,1024]{1,0:T(8,128)S(1)} %get-tuple-element.36.own_first_ref), channel_id=1, source_target_pairs={{0,1},{1,0},{2,3},{3,2},{4,5},{5,4},{6,7},{7,6},{8,9},{9,8},{10,11... | collective-permute-start | bytes 196616 | tf_op jit(solution)/shard_map/ppermute | solution.py:405
  8.4 0.9 %shard_map.69 = (bf16[1024,1024]{1,0:T(8,128)(2,1)S(1)}, bf16[512,1024]{1,0:T(8,128)(2,1)S(1)}, f32[2,128]{1,0:T(2,128)S(1)}) custom-call(f32[4,8,1024]{2,1,0:T(8,128)S(1)} %get-tuple-element.27.b_ref, f32[4,8,1024]{2,1,0:T(8,128)S(1)} %get-tuple-element.31.draw_ref, f32[4,8,1024]{2,1,0:T(8,128)S(1)} %get-tuple-element.32.slot_ref), custom_call_target="tpu_custom_call" | custom-call | flops 25165824 | tf_op jit(solution)/shard_map/pallas_call | solution.py:379
  9.3 0.0 collective-permute-done.got_second_ref.x_second_ref
  9.3 0.0 collective-permute-done.1.got_first_ref.x_first_ref
  9.3 0.6 %shard_map.70 = (f32[6,8,1024]{2,1,0:T(8,128)S(1)}, f32[5,8,1024]{2,1,0:T(8,128)S(1)}, f32[4,8,1024]{2,1,0:T(8,128)S(1)}, f32[16,32]{1,0:T(8,128)S(1)}) custom-call(f32[4,8,1024]{2,1,0:T(8,128)S(1)} %get-tuple-element.27.b_ref, f32[4,8,1024]{2,1,0:T(8,128)S(1)} %get-tuple-element.37.cond_ref, f32[4,8,1024]{2,1,0:T(8,128)S(1)} %get-tuple-element.28.cap_ref, ...), custom_call_target="tpu_custom_call" | custom-call | flops 25165824 | tf_op jit(solution)/shard_map/pallas_call | solution.py:379
  9.9 0.0 collective-permute-done.2.y_second_ref
  9.9 0.9 %collective-permute-done.3.y_first_ref = f32[16,1024]{1,0:T(8,128)S(1)} collective-permute-done((f32[16,1024]{1,0:T(8,128)S(1)}, f32[16,1024]{1,0:T(8,128)S(1)}, u32[]{:S(2)}, u32[]{:S(2)}) %collective-permute-start.3) | collective-permute-done | bytes 65568 | tf_op jit(solution)/shard_map/ppermute | solution.py:405
  10.8 1.0 %shard_map.71 = (f32[4,8,1024]{2,1,0:T(8,128)S(1)}, f32[4,8,1024]{2,1,0:T(8,128)S(1)}, f32[4,128]{1,0:T(4,128)S(1)}, f32[4,1024]{1,0:T(4,128)S(1)}, f32[4,1024]{1,0:T(4,128)S(1)}, /*index=5*/f32[24,1024]{1,0:T(8,128)S(1)}) custom-call(f32[4,8,1024]{2,1,0:T(8,128)S(1)} %get-tuple-element.27.b_ref, f32[4,8,1024]{2,1,0:T(8,128)S(1)} %get-tuple-element.28.cap_ref, ...), custom_call_target="tpu_custom_call" | custom-call | flops 25165824 | tf_op jit(solution)/shard_map/pallas_call | solution.py:379
  11.8 0.6 %broadcast_in_dim.2 = f32[16,4,128]{2,1,0:T(4,128)} broadcast(f32[4,128]{1,0:T(4,128)S(1)} %get-tuple-element.46), dimensions={1,2} | broadcast | bytes 34816 | tf_op jit(solution)/shard_map/broadcast_in_dim | solution.py:414
  12.4 5.3 %all-to-all-start = ((f32[16,4,128]{2,1,0:T(4,128)}), f32[16,4,128]{2,1,0:T(4,128)S(1)}, u32[]{:S(2)}, u32[]{:S(2)}) async-start(f32[16,4,128]{2,1,0:T(4,128)} %broadcast_in_dim.2), calls=%async_computation | async-start | bytes 65536 | tf_op jit(solution)/shard_map/all_to_all | solution.py:415
  17.7 0.6 %collective-permute-start.4 = (f32[4,1024]{1,0:T(4,128)S(1)}, f32[4,1024]{1,0:T(4,128)S(1)}, u32[]{:S(2)}, u32[]{:S(2)}) collective-permute-start(f32[4,1024]{1,0:T(4,128)S(1)} %get-tuple-element.50), channel_id=1, source_target_pairs={{0,1},{1,0},{2,3},{3,2},{4,5},{5,4},{6,7},{7,6},{8,9},{9,8},{10,11... | collective-permute-start | bytes 49160 | tf_op jit(solution)/shard_map/ppermute | solution.py:405
  18.3 0.0 collective-permute-start.5
  18.3 3.2 %collective-permute-done.4.corner_first_ref = f32[4,1024]{1,0:T(4,128)S(1)} collective-permute-done((f32[4,1024]{1,0:T(4,128)S(1)}, f32[4,1024]{1,0:T(4,128)S(1)}, u32[]{:S(2)}, u32[]{:S(2)}) %collective-permute-start.4) | collective-permute-done | bytes 16416 | tf_op jit(solution)/shard_map/ppermute | solution.py:405
  21.4 0.0 collective-permute-done.5.corner_second_ref
  21.4 0.0 all-to-all-done.sketch_ref
  21.4 1.1 %shard_map.72 = (f32[4,8,1024]{2,1,0:T(8,128)}, f32[4,8,1024]{2,1,0:T(8,128)}) custom-call(f32[16,4,128]{2,1,0:T(4,128)S(1)} %all-to-all-done.sketch_ref, f32[4,8,1024]{2,1,0:T(8,128)S(1)} %get-tuple-element.27.b_ref, f32[4,8,1024]{2,1,0:T(8,128)S(1)} %get-tuple-element.47.image_ref, f32[4,8,1024]{2,1,0:T(8,128)S(1)} %get-tuple-element.48.twice_ref, ...), custom_call_target="tpu_custom_call" | custom-call | tf_op jit(solution)/shard_map/pallas_call | solution.py:379
Async XLA Ops:
  2.1 7.2 %collective-permute-start = (f32[28,1024]{1,0:T(8,128)S(1)}, f32[28,1024]{1,0:T(8,128)S(1)}, u32[]{:S(2)}, u32[]{:S(2)}) collective-permute-start(f32[28,1024]{1,0:T(8,128)S(1)} %get-tuple-element.39), channel_id=1, source_target_pairs={{0,1},{1,0},{2,3},{3,2},{4,8},{5,9},{6,10},{7,11},{8,4},{9,5},{10,... | collective-permute-start | bytes 344072 | tf_op jit(solution)/shard_map/ppermute | solution.py:405
  5.2 4.1 %collective-permute-start.1 = (f32[28,1024]{1,0:T(8,128)S(1)}, f32[28,1024]{1,0:T(8,128)S(1)}, u32[]{:S(2)}, u32[]{:S(2)}) collective-permute-start(f32[28,1024]{1,0:T(8,128)S(1)} %get-tuple-element.40), channel_id=1, source_target_pairs={{0,4},{1,5},{2,6},{3,7},{4,0},{5,1},{6,2},{7,3},{8,12},{9,13},{10,... | collective-permute-start | bytes 344072 | tf_op jit(solution)/shard_map/ppermute | solution.py:405
  5.3 4.6 %collective-permute-start.2 = (f32[16,1024]{1,0:T(8,128)S(1)}, f32[16,1024]{1,0:T(8,128)S(1)}, u32[]{:S(2)}, u32[]{:S(2)}) collective-permute-start(f32[16,1024]{1,0:T(8,128)S(1)} %get-tuple-element.35.own_second_ref), channel_id=1, source_target_pairs={{0,4},{1,2},{2,1},{3,7},{4,0},{5,6},{6,5},{7,3},{8,12},{9,10},{10,... | collective-permute-start | bytes 196616 | tf_op jit(solution)/shard_map/ppermute | solution.py:405
  5.7 5.1 %collective-permute-start.3 = (f32[16,1024]{1,0:T(8,128)S(1)}, f32[16,1024]{1,0:T(8,128)S(1)}, u32[]{:S(2)}, u32[]{:S(2)}) collective-permute-start(f32[16,1024]{1,0:T(8,128)S(1)} %get-tuple-element.36.own_first_ref), channel_id=1, source_target_pairs={{0,1},{1,0},{2,3},{3,2},{4,5},{5,4},{6,7},{7,6},{8,9},{9,8},{10,11... | collective-permute-start | bytes 196616 | tf_op jit(solution)/shard_map/ppermute | solution.py:405
  12.4 9.0 %all-to-all-start = ((f32[16,4,128]{2,1,0:T(4,128)}), f32[16,4,128]{2,1,0:T(4,128)S(1)}, u32[]{:S(2)}, u32[]{:S(2)}) async-start(f32[16,4,128]{2,1,0:T(4,128)} %broadcast_in_dim.2), calls=%async_computation | async-start | bytes 65536 | tf_op jit(solution)/shard_map/all_to_all | solution.py:415
  17.7 3.7 %collective-permute-start.4 = (f32[4,1024]{1,0:T(4,128)S(1)}, f32[4,1024]{1,0:T(4,128)S(1)}, u32[]{:S(2)}, u32[]{:S(2)}) collective-permute-start(f32[4,1024]{1,0:T(4,128)S(1)} %get-tuple-element.50), channel_id=1, source_target_pairs={{0,1},{1,0},{2,3},{3,2},{4,5},{5,4},{6,7},{7,6},{8,9},{9,8},{10,11... | collective-permute-start | bytes 49160 | tf_op jit(solution)/shard_map/ppermute | solution.py:405
  18.3 3.2 %collective-permute-start.5 = (f32[4,1024]{1,0:T(4,128)S(1)}, f32[4,1024]{1,0:T(4,128)S(1)}, u32[]{:S(2)}, u32[]{:S(2)}) collective-permute-start(f32[4,1024]{1,0:T(4,128)S(1)} %get-tuple-element.51), channel_id=1, source_target_pairs={{0,4},{1,2},{2,1},{3,7},{4,0},{5,6},{6,5},{7,3},{8,12},{9,10},{10,... | collective-permute-start | bytes 49160 | tf_op jit(solution)/shard_map/ppermute | solution.py:405
